TPU v7x, 32 devices: a whole 2x2x4 slice. The times are simulated.
32 devices in a mesh: head: 16 (over z, y, x), seq: 2 (over core).
Axes of the slice: x: 2, y: 2, z: 4, core: 2. Of those that a mesh axis runs over, the one named last changes fastest.
Arguments:
- tokens: bfloat16 [2, 2048, 2048], P('seq', 'head'), may hold values from -6 to 6
- cotangent: bfloat16 [2, 2048, 2048], P('seq', 'head'), may hold values from -6 to 6
- segment_ids: int32 [2, 2048], P('seq', 'head'), may hold values from 0 to 3, never falling along the last dimension, each value on 1 to 1024 neighbouring positions
- owner_map: int32 [256], replicated, may hold values from 0 to 255, each once
- weights: float32 [256, 512, 512], P(('head', 'seq')), may hold values from -0.125 to 0.125
- norm_gains: float32 [4, 2048], replicated, may hold values from 0.5 to 1.5
- left_stats: float32 [256, 512, 512], P(('head', 'seq')), as said below
- right_stats: float32 [256, 512, 512], P(('head', 'seq')), as said below
- left_root: float32 [256, 512, 512], P(('head', 'seq')), as said below
- right_root: float32 [256, 512, 512], P(('head', 'seq')), as said below
Outputs:
- output: bfloat16 [2, 2048, 2048], P('seq', 'head')
- input_grad: float32 [2, 2048, 2048], P('seq', 'head')
- grad_slots: float32 [256, 512, 512], P(('head', 'seq'))
- left_new: float32 [256, 512, 512], P(('head', 'seq'))
- right_new: float32 [256, 512, 512], P(('head', 'seq'))
- new_weights: float32 [256, 512, 512], P(('head', 'seq'))
- gain_grads: float32 [4, 2048], replicated
- new_gains: float32 [4, 2048], replicated
Inputs may be any that keep to these rules, and one draw needn't show every extreme that they name: `segment_ids`: within each row ids never fall, each sequence spans 1 to 1024 positions, and one spans exactly 1024. `owner_map`: each block number stands in exactly one slot. `left_stats`: each slot's matrix is symmetric. `right_stats`: each slot's matrix is symmetric. `left_root`: each slot's matrix is symmetric. `right_root`: each slot's matrix is symmetric.
All inputs are finite; a program needn't handle non-finite values.
Results may differ from a plain program's by a relative error of at most 0.015.
Values may be sent and summed in bfloat16 or wider, within the bound.
No kernel may reach another device: no remote copies, remote signals or barrier semaphores. Data moves between devices by JAX's collectives and lax.ppermute only.
A program may use at most 512 MiB of HBM per device.

v0:
```python
import jax
import jax.numpy as jnp
import numpy as np
from jax import lax
from jax.sharding import PartitionSpec as P

FF = 8192
HEADS = 16
SEGMAX = 1024
QB = 512


epsilon = 1e-06
rope_base = 500000.0
decay_rate = 0.5
step_rate = 0.5
gain_rate = 0.3
highest = lax.Precision.HIGHEST


def grid_mul(rows, grid):
    row_blocks, col_blocks, block_side, unused_side = grid.shape
    shaped = rows.reshape(rows.shape[0], row_blocks, block_side)
    out = jnp.einsum("trk,rckn->tcn", shaped, grid, preferred_element_type=jnp.float32)
    return out.reshape(rows.shape[0], col_blocks * block_side)


def grid_back(rows, grid):
    row_blocks, col_blocks, block_side, unused_side = grid.shape
    shaped = rows.reshape(rows.shape[0], col_blocks, block_side)
    out = jnp.einsum("tcn,rckn->trk", shaped, grid, preferred_element_type=jnp.float32)
    return out.reshape(rows.shape[0], row_blocks * block_side)


def rms_norm(values, gain_vec):
    return (
        values * lax.rsqrt(jnp.mean(values * values, axis=-1, keepdims=True) + epsilon) * gain_vec
    )


def positions_of(segment_row):
    length = segment_row.shape[0]
    indices = jnp.arange(length, dtype=jnp.int32)
    earlier = jnp.concatenate([jnp.full((1,), -1, jnp.int32), segment_row[:-1]])
    begins = lax.cummax(jnp.where(segment_row != earlier, indices, 0), axis=0)
    return indices - begins


def rotate(vectors, places, head_count):
    token_count = vectors.shape[0]
    head_size = vectors.shape[1] // head_count
    half_size = head_size // 2
    frequency = rope_base ** (-2.0 * jnp.arange(half_size, dtype=jnp.float32) / head_size)
    angles = places.astype(jnp.float32)[:, None] * frequency[None, :]
    cosine = jnp.cos(angles)[:, None, :]
    sine_part = jnp.sin(angles)[:, None, :]
    grouped = vectors.reshape(token_count, head_count, head_size)
    first_half = grouped[..., :half_size]
    second_half = grouped[..., half_size:]
    turned = jnp.concatenate(
        [
            first_half * cosine - second_half * sine_part,
            second_half * cosine + first_half * sine_part,
        ],
        axis=-1,
    )
    return turned.reshape(token_count, head_count * head_size)


def matrix_shapes(model_width, hidden_width):
    return [(model_width, model_width)] * 4 + [
        (model_width, hidden_width),
        (model_width, hidden_width),
        (hidden_width, model_width),
    ]


def assemble(every_block, inverse, model_width, hidden_width, block_side):
    grids = []
    offset = 0
    for row_count, col_count in matrix_shapes(model_width, hidden_width):
        number = row_count // block_side * (col_count // block_side)
        picked = jnp.take(every_block, inverse[offset : offset + number], axis=0)
        grids.append(
            picked.reshape(row_count // block_side, col_count // block_side, block_side, block_side)
        )
        offset = offset + number
    return grids


def block_offsets(model_width, hidden_width, block_side):
    left_base = [0, 0, 0, model_width, 2 * model_width, 2 * model_width, 3 * model_width]
    right_base = [
        0,
        model_width,
        2 * model_width,
        3 * model_width,
        4 * model_width,
        4 * model_width + hidden_width,
        4 * model_width + 2 * hidden_width,
    ]
    left_list = []
    right_list = []
    for matrix_id, sizes_pair in enumerate(matrix_shapes(model_width, hidden_width)):
        for row_block in range(sizes_pair[0] // block_side):
            for col_block in range(sizes_pair[1] // block_side):
                left_list.append(left_base[matrix_id] + row_block * block_side)
                right_list.append(right_base[matrix_id] + col_block * block_side)
    return (jnp.asarray(np.array(left_list, np.int32)), jnp.asarray(np.array(right_list, np.int32)))


def body(
    tokens,
    cotangent,
    segment_ids,
    owner_map,
    weights,
    norm_gains,
    left_stats,
    right_stats,
    left_root,
    right_root,
):
    model_width = tokens.shape[2]
    local_count = tokens.shape[1]
    block_side = weights.shape[1]
    total_blocks = owner_map.shape[0]
    group_size = lax.axis_size("head")
    local_heads = HEADS // group_size
    head_size = model_width // HEADS
    local_width = local_heads * head_size
    score_scale = head_size ** (-0.5)
    inverse = (
        jnp.zeros((total_blocks,), jnp.int32)
        .at[owner_map]
        .set(jnp.arange(total_blocks, dtype=jnp.int32))
    )
    every_block = lax.all_gather(weights.astype(jnp.bfloat16), ("head", "seq"), axis=0, tiled=True)
    w_query, w_key, w_value, w_output, w_gate, w_up, w_down = assemble(
        every_block, inverse, model_width, FF, block_side
    )
    inputs = tokens[0]
    row_ids = lax.all_gather(segment_ids, "head", axis=1, tiled=True)[0]
    row_length = row_ids.shape[0]
    places = lax.dynamic_slice_in_dim(
        positions_of(row_ids), lax.axis_index("head") * local_count, local_count
    )

    def shape_query(raw_vecs, gain_vec):
        return rotate(rms_norm(raw_vecs, gain_vec), places, HEADS)

    query_raw = grid_mul(inputs, w_query)
    key_raw = grid_mul(inputs, w_key)
    value_send = grid_mul(inputs, w_value).astype(jnp.bfloat16)
    query_send = shape_query(query_raw, norm_gains[2]).astype(jnp.bfloat16)
    key_send = shape_query(key_raw, norm_gains[3]).astype(jnp.bfloat16)
    query_rows, key_rows, value_rows = (
        lax.all_to_all(query_send, "head", split_axis=1, concat_axis=0, tiled=True),
        lax.all_to_all(key_send, "head", split_axis=1, concat_axis=0, tiled=True),
        lax.all_to_all(value_send, "head", split_axis=1, concat_axis=0, tiled=True),
    )
    window = min(QB + SEGMAX, row_length)
    block_count = row_length // QB
    starts = jnp.arange(block_count, dtype=jnp.int32) * QB

    def block_scores(query_start):
        key_start = jnp.clip(query_start + QB - window, 0, row_length - window)
        query_blk = lax.dynamic_slice_in_dim(query_rows, query_start, QB).reshape(
            QB, local_heads, head_size
        )
        key_blk = lax.dynamic_slice_in_dim(key_rows, key_start, window).reshape(
            window, local_heads, head_size
        )
        value_blk = lax.dynamic_slice_in_dim(value_rows, key_start, window).reshape(
            window, local_heads, head_size
        )
        raw_scores = (
            jnp.einsum("qhd,khd->hqk", query_blk, key_blk, preferred_element_type=jnp.float32)
            * score_scale
        )
        query_ids = lax.dynamic_slice_in_dim(row_ids, query_start, QB)
        key_ids = lax.dynamic_slice_in_dim(row_ids, key_start, window)
        query_place = query_start + jnp.arange(QB, dtype=jnp.int32)
        key_place = key_start + jnp.arange(window, dtype=jnp.int32)
        allowed = (query_ids[:, None] == key_ids[None, :]) & (
            key_place[None, :] <= query_place[:, None]
        )
        scores = jnp.where(allowed[None], raw_scores, -1e30)
        return (scores, query_blk, key_blk, value_blk, key_start)

    def attend(query_start):
        scores, query_blk, key_blk, value_blk, key_start = block_scores(query_start)
        top_score = jnp.max(scores, axis=-1, keepdims=True)
        expo = jnp.exp(scores - top_score)
        totals = jnp.sum(expo, axis=-1, keepdims=True)
        attention = (expo / totals).astype(jnp.bfloat16)
        mixture = jnp.einsum(
            "hqk,khd->qhd", attention, value_blk, preferred_element_type=jnp.float32
        )
        return (
            mixture.reshape(QB, local_width).astype(jnp.bfloat16),
            (top_score + jnp.log(totals))[..., 0],
        )

    mixed_blocks, log_sums = lax.map(attend, starts)
    mixed_rows = mixed_blocks.reshape(row_length, local_width)
    attended = lax.all_to_all(mixed_rows, "head", split_axis=0, concat_axis=1, tiled=True)
    out_attn_raw = grid_mul(attended, w_output)
    resid = inputs.astype(jnp.float32) + rms_norm(out_attn_raw, norm_gains[0])
    resid_low = resid.astype(jnp.bfloat16)

    def activate(gate_in, upward):
        return jax.nn.silu(gate_in) * upward

    gate_raw = grid_mul(resid_low, w_gate)
    up_raw = grid_mul(resid_low, w_up)
    hidden = activate(gate_raw, up_raw).astype(jnp.bfloat16)
    down_raw = grid_mul(hidden, w_down)
    result = resid + rms_norm(down_raw, norm_gains[1])
    output = result.astype(jnp.bfloat16)[None]
    b_query, b_key, b_value, b_output, b_gate, b_up, b_down = (
        w_query,
        w_key,
        w_value,
        w_output,
        w_gate,
        w_up,
        w_down,
    )
    upstream = cotangent[0].astype(jnp.float32)
    unused_down, down_norm_back = jax.vjp(rms_norm, down_raw, norm_gains[1])
    down_grad, gain_mlp_grad = down_norm_back(upstream)
    down_low = down_grad.astype(jnp.bfloat16)
    hidden_grad = grid_back(down_low, b_down)
    unused_act, act_back = jax.vjp(activate, gate_raw, up_raw)
    gate_grad, up_grad = act_back(hidden_grad)
    gate_low = gate_grad.astype(jnp.bfloat16)
    up_low = up_grad.astype(jnp.bfloat16)
    resid_grad = upstream + grid_back(gate_low, b_gate) + grid_back(up_low, b_up)
    unused_attn, attn_norm_back = jax.vjp(rms_norm, out_attn_raw, norm_gains[0])
    out_attn_grad, gain_attn_grad = attn_norm_back(resid_grad)
    out_attn_low = out_attn_grad.astype(jnp.bfloat16)
    attended_grad = grid_back(out_attn_low, b_output).astype(jnp.bfloat16)
    grad_rows = lax.all_to_all(attended_grad, "head", split_axis=1, concat_axis=0, tiled=True)

    def attend_back(carry, paired):
        key_acc, value_acc = carry
        query_start, log_sum = paired
        scores, query_blk, key_blk, value_blk, key_start = block_scores(query_start)
        attention = jnp.exp(scores - log_sum[..., None])
        grad_blk = lax.dynamic_slice_in_dim(grad_rows, query_start, QB).reshape(
            QB, local_heads, head_size
        )
        prob_grad = jnp.einsum(
            "qhd,khd->hqk", grad_blk, value_blk, preferred_element_type=jnp.float32
        )
        center = jnp.sum(attention * prob_grad, axis=-1, keepdims=True)
        score_grad = (attention * (prob_grad - center)).astype(jnp.bfloat16)
        query_grad = (
            jnp.einsum("hqk,khd->qhd", score_grad, key_blk, preferred_element_type=jnp.float32)
            * score_scale
        )
        key_part = (
            jnp.einsum("hqk,qhd->khd", score_grad, query_blk, preferred_element_type=jnp.float32)
            * score_scale
        )
        value_part = jnp.einsum(
            "hqk,qhd->khd",
            attention.astype(jnp.bfloat16),
            grad_blk,
            preferred_element_type=jnp.float32,
        )
        key_now = lax.dynamic_slice_in_dim(key_acc, key_start, window)
        value_now = lax.dynamic_slice_in_dim(value_acc, key_start, window)
        key_acc = lax.dynamic_update_slice_in_dim(key_acc, key_now + key_part, key_start, 0)
        value_acc = lax.dynamic_update_slice_in_dim(value_acc, value_now + value_part, key_start, 0)
        return ((key_acc, value_acc), query_grad.reshape(QB, local_width))

    zero_rows = jnp.zeros((row_length, local_heads, head_size), jnp.float32)
    (key_total, value_total), query_blocks = lax.scan(
        attend_back, (zero_rows, zero_rows), (starts, log_sums)
    )
    qkv_back = (
        query_blocks.reshape(row_length, local_width).astype(jnp.bfloat16),
        key_total.reshape(row_length, local_width).astype(jnp.bfloat16),
        value_total.reshape(row_length, local_width).astype(jnp.bfloat16),
    )
    query_back, key_back, value_back = (
        lax.all_to_all(qkv_back[0], "head", split_axis=0, concat_axis=1, tiled=True),
        lax.all_to_all(qkv_back[1], "head", split_axis=0, concat_axis=1, tiled=True),
        lax.all_to_all(qkv_back[2], "head", split_axis=0, concat_axis=1, tiled=True),
    )
    unused_query, query_shape_back = jax.vjp(shape_query, query_raw, norm_gains[2])
    query_raw_grad, gain_query_grad = query_shape_back(query_back.astype(jnp.float32))
    unused_key, key_shape_back = jax.vjp(shape_query, key_raw, norm_gains[3])
    key_raw_grad, gain_key_grad = key_shape_back(key_back.astype(jnp.float32))
    query_low = query_raw_grad.astype(jnp.bfloat16)
    key_low = key_raw_grad.astype(jnp.bfloat16)
    input_grad = (
        resid_grad
        + grid_back(query_low, b_query)
        + grid_back(key_low, b_key)
        + grid_back(value_back, b_value)
    )
    left_cat = jnp.concatenate([inputs, attended, resid_low, hidden], axis=1)
    right_cat = jnp.concatenate(
        [query_low, key_low, value_back, out_attn_low, gate_low, up_low, down_low], axis=1
    )
    left_table, right_table = block_offsets(model_width, FF, block_side)

    def column_pair(left_start, right_start):
        left_part = lax.dynamic_slice_in_dim(left_cat, left_start, block_side, 1)
        right_part = lax.dynamic_slice_in_dim(right_cat, right_start, block_side, 1)
        return (left_part, right_part)

    left_every = jnp.take(left_table, owner_map)
    right_every = jnp.take(right_table, owner_map)
    left_send, right_send = jax.vmap(column_pair)(left_every, right_every)
    left_got, right_got = (
        lax.all_to_all(left_send, ("head", "seq"), split_axis=0, concat_axis=1, tiled=True),
        lax.all_to_all(right_send, ("head", "seq"), split_axis=0, concat_axis=1, tiled=True),
    )
    grad_slots = jnp.einsum("stl,str->slr", left_got, right_got, preferred_element_type=jnp.float32)
    gain_local = jnp.stack([gain_attn_grad, gain_mlp_grad, gain_query_grad, gain_key_grad])
    gain_grads = lax.psum(gain_local, ("head", "seq"))

    def batched(left_side, right_side, form):
        return jnp.einsum(
            form, left_side, right_side, precision=highest, preferred_element_type=jnp.float32
        )

    left_new = decay_rate * left_stats + (1.0 - decay_rate) * batched(
        grad_slots, grad_slots, "sij,skj->sik"
    )
    right_new = decay_rate * right_stats + (1.0 - decay_rate) * batched(
        grad_slots, grad_slots, "sji,sjk->sik"
    )
    update = batched(batched(left_root, grad_slots, "sij,sjk->sik"), right_root, "sij,sjk->sik")
    new_weights = weights - step_rate * update
    new_gains = norm_gains - gain_rate * gain_grads * lax.rsqrt(
        jnp.mean(gain_grads * gain_grads, axis=1, keepdims=True) + epsilon
    )
    return (
        output,
        input_grad[None],
        grad_slots,
        left_new,
        right_new,
        new_weights,
        gain_grads,
        new_gains,
    )


def solution(mesh):
    return jax.shard_map(
        body,
        mesh=mesh,
        in_specs=(
            P("seq", "head", None),
            P("seq", "head", None),
            P("seq", "head"),
            P(),
            P(("head", "seq"), None, None),
            P(),
            P(("head", "seq"), None, None),
            P(("head", "seq"), None, None),
            P(("head", "seq"), None, None),
            P(("head", "seq"), None, None),
        ),
        out_specs=(
            P("seq", "head", None),
            P("seq", "head", None),
            P(("head", "seq"), None, None),
            P(("head", "seq"), None, None),
            P(("head", "seq"), None, None),
            P(("head", "seq"), None, None),
            P(),
            P(),
        ),
        check_vma=False,
    )
```

profile of v0, /device:TPU:0, one launch (start us, length us, event | category | flops | bytes accessed | tf_op | source)
XLA Modules:
  0.0 4049.1 jit_solution(4521726762703260720)
XLA Ops:
  13.3 42.6 %all_gather.7 = s32[1,2048]{1,0:T(1,128)S(1)} all-gather(s32[1,128]{1,0:T(1,128)S(1)} %copy-done.57), channel_id=1, replica_groups=mesh['head'=16,'seq'=2] {'head'}, dimensions={1}, use_global_device_ids=true | all-gather | bytes 8704 | tf_op jit(solution)/shard_map/all_gather | solution.py:143
  60.8 634.1 %all-gather.2.cloned.1.call-done = bf16[256,512,512]{2,1,0:T(8,128)(2,1)} async-done(((bf16[8,512,512]{2,1,0:T(8,128)(2,1)}), bf16[256,512,512]{2,1,0:T(8,128)(2,1)}) %all-gather.2.cloned.1.call-update) | async-done | bytes 134217744 | tf_op jit(solution)/shard_map/all_gather | solution.py:138
  762.9 22.9 gather_fusion.6
  794.9 22.8 broadcast_select_fusion
  817.8 22.8 gather_fusion.4
  848.6 22.8 broadcast_select_fusion.2
  871.4 22.8 gather_fusion.5
  896.2 40.3 while.36
  943.5 22.8 broadcast_select_fusion.1
  987.1 22.9 copy.178
  1010.0 42.8 %copy.170 = bf16[16,512,512,4]{2,1,0,3:T(8,128)(2,1)} copy(bf16[16,512,512,4]{1,2,0,3:T(8,128)(2,1)} %bitcast.373) | data formatting | bytes 67108864 | tf_op jit(solution)/shard_map/trk,rckn->tcn/dot_general | solution.py:24
  1052.8 22.9 copy.180
  1075.7 42.8 %copy.172 = bf16[16,512,512,4]{2,1,0,3:T(8,128)(2,1)} copy(bf16[16,512,512,4]{1,2,0,3:T(8,128)(2,1)} %bitcast.375) | data formatting | bytes 67108864 | tf_op jit(solution)/shard_map/trk,rckn->tcn/dot_general | solution.py:24
  1118.5 22.9 copy.176
  1141.4 47.1 %copy.174 = bf16[4,512,512,16]{2,1,0,3:T(8,128)(2,1)} copy(bf16[4,512,512,16]{1,2,0,3:T(8,128)(2,1)} %bitcast.371) | data formatting | bytes 67108864 | tf_op jit(solution)/shard_map/trk,rckn->tcn/dot_general | solution.py:24
  1340.8 94.3 %while.37 = (s32[]{:T(128)}, f32[2048,1,128]{0,2,1:T(8,128)}, f32[2048,1,128]{2,0,1:T(8,128)}, bf16[4,512,128]{2,1,0:T(8,128)(2,1)}, s32[4]{0:T(128)S(1)}, /*ind...) while((s32[]{:T(128)}, f32[2048,1,128]{0,2,1:T(8,128)}, ...), condition=%wide.region_15.18_spmd, body=%wide.region_13.17_spmd.sunk | while | flops 1016792576 | bytes 37013808 | solution.py:280
  1485.3 746.4 %while.38 = (s32[]{:T(128)}, bf16[128,14336]{1,0:T(8,128)(2,1)}, s32[256,2]{0,1:T(2,128)S(1)}, bf16[256,128,512]{2,1,0:T(8,128)(2,1)}, s32[]{:T(128)}) while((s32[]{:T(128)}, bf16[128,14336]{1,0:T(8,128)(2,1)}, s32[256,2]{0,1:T(2,128)S(1)}, bf16[256,128,512]{2,1,0:T(8,128)(2,1)}, s32[]{:T(128)}) %tuple.153), condition=%wide.while_cond, body=%wide.while_body.sunk | while | flops 2 | bytes 262757 | solution.py:312
  2278.3 746.7 %while.39 = (s32[]{:T(128)}, bf16[128,26624]{1,0:T(8,128)(2,1)}, s32[256,2]{0,1:T(2,128)S(1)}, bf16[256,128,512]{2,1,0:T(8,128)(2,1)}, s32[]{:T(128)}) while((s32[]{:T(128)}, bf16[128,26624]{1,0:T(8,128)(2,1)}, s32[256,2]{0,1:T(2,128)S(1)}, bf16[256,128,512]{2,1,0:T(8,128)(2,1)}, s32[]{:T(128)}) %tuple.156), condition=%wide.while_cond.1, body=%wide.while_body.1.sunk | while | flops 2 | bytes 262757 | solution.py:313
  3055.7 743.9 %psum.7 = f32[4,2048]{1,0:T(4,128)S(1)} all-reduce(f32[4,2048]{1,0:T(4,128)S(1)} %pad_maximum_fusion.3), channel_id=1, replica_groups=mesh['head'=16,'seq'=2] {'head','seq'}, use_global_device_ids=true, to_apply=%region_22.26 | all-reduce | flops 8192 | bytes 65536 | tf_op jit(solution)/shard_map/psum | solution.py:325
  3816.1 46.1 %copy.198 = bf16[32,8,128,512]{2,0,3,1:T(8,128)(2,1)} copy(bf16[32,8,128,512]{3,2,1,0:T(8,128)(2,1)} %bitcast.105) | data formatting | bytes 67108864 | tf_op jit(solution)/shard_map/all_to_all | solution.py:320
  3862.2 49.3 %all_to_all.142 = bf16[8,4096,512]{1,2,0:T(8,128)(2,1)} reshape(bf16[8,32,128,512]{2,1,3,0:T(8,128)(2,1)} %bitcast.380) | data formatting | bytes 67108864 | tf_op jit(solution)/shard_map/all_to_all | solution.py:320
  3911.5 23.0 copy.204
  3934.6 32.6 fusion.92
  4022.1 19.7 multiply_subtract_fusion
  (1934 shorter events, 2083.4 us)
Async XLA Ops:
  7.2 49.6 %copy-start.52 = (s32[256]{0:T(256)S(1)}, s32[256]{0:T(256)}, u32[]{:S(2)}) copy-start(s32[256]{0:T(256)} %param.25) | copy-start | bytes 3076
  7.2 52.0 %copy-start.38 = (f32[4,2048]{1,0:T(4,128)S(1)}, f32[4,2048]{1,0:T(4,128)}, u32[]{:S(2)}) copy-start(f32[4,2048]{1,0:T(4,128)} %param.27) | copy-start | bytes 98308
  7.2 687.6 %all-gather.2.cloned.1.call-start = ((), (), s32[]{:S(2)}) async-start(), calls=%async_computation.10 | async-start | bytes 138412032 | tf_op jit(solution)/shard_map/all_gather | solution.py:138
  56.8 644.4 %copy-start.54 = (s32[256]{0:T(256)}, s32[256]{0:T(256)S(1)}, u32[]{:S(2)}) copy-start(s32[256]{0:T(256)S(1)} %compare_select_fusion.2) | copy-start | bytes 3076
  60.4 701.9 %copy-start.41 = (f32[1,2048]{1,0:T(1,128)}, f32[1,2048]{1,0:T(1,128)S(1)}, u32[]{:S(2)}) copy-start(f32[1,2048]{1,0:T(1,128)S(1)} %get-tuple-element.511) | copy-start | bytes 24580
  60.4 725.4 %copy-start.43 = (f32[1,2048]{1,0:T(1,128)}, f32[1,2048]{1,0:T(1,128)S(1)}, u32[]{:S(2)}) copy-start(f32[1,2048]{1,0:T(1,128)S(1)} %get-tuple-element.512) | copy-start | bytes 24580
  60.7 725.3 %copy-start.32 = (f32[128,64]{1,0:T(8,128)}, f32[128,64]{1,0:T(8,128)S(1)}, u32[]{:S(2)}) copy-start(f32[128,64]{1,0:T(8,128)S(1)} %get-tuple-element.526) | copy-start | bytes 98308
  60.8 725.3 %copy-start.34 = (f32[128,64]{1,0:T(8,128)}, f32[128,64]{1,0:T(8,128)S(1)}, u32[]{:S(2)}) copy-start(f32[128,64]{1,0:T(8,128)S(1)} %get-tuple-element.527) | copy-start | bytes 98308
  751.8 36.1 all-to-all-start
  787.9 53.8 %all-to-all-start.2 = ((bf16[128,16,128]{2,0,1:T(8,128)(2,1)}), bf16[128,16,128]{2,0,1:T(8,128)(2,1)}, u32[]{:S(2)}, u32[]{:S(2)}) async-start(bf16[128,16,128]{2,0,1:T(8,128)(2,1)} %pad_maximum_fusion.2), calls=%async_computation.2 | async-start | bytes 1048576 | tf_op jit(solution)/shard_map/all_to_all | solution.py:159
  841.7 54.6 %all-to-all-start.1 = ((bf16[128,16,128]{2,0,1:T(8,128)(2,1)}), bf16[128,16,128]{2,0,1:T(8,128)(2,1)}, u32[]{:S(2)}, u32[]{:S(2)}) async-start(bf16[128,16,128]{2,0,1:T(8,128)(2,1)} %pad_maximum_fusion.1), calls=%async_computation.1 | async-start | bytes 1048576 | tf_op jit(solution)/shard_map/all_to_all | solution.py:158
  936.5 252.0 %all-to-all-start.3 = ((bf16[16,128,128]{2,1,0:T(8,128)(2,1)}), bf16[16,128,128]{2,1,0:T(8,128)(2,1)S(1)}, u32[]{:S(2)}, u32[]{:S(2)}) async-start(bf16[16,128,128]{2,1,0:T(8,128)(2,1)} %bitcast.45), calls=%async_computation.3 | async-start | bytes 1048576 | tf_op jit(solution)/shard_map/all_to_all | solution.py:207
  1317.5 21.2 all-to-all-start.4
  1340.8 98.3 %copy-start.55 = (s32[256]{0:T(256)S(1)}, s32[256]{0:T(256)}, u32[]{:S(2)}) copy-start(s32[256]{0:T(256)} %copy-done.54) | copy-start | bytes 3076
  1340.8 98.3 %copy-start.1 = (s32[256]{0:T(256)S(1)}, s32[256]{0:T(256)}, u32[]{:S(2)}) copy-start(s32[256]{0:T(256)} %constant.265.clone2.1) | copy-start | bytes 3076
  1340.8 100.3 %copy-start = (s32[256]{0:T(256)S(1)}, s32[256]{0:T(256)}, u32[]{:S(2)}) copy-start(s32[256]{0:T(256)} %constant.264.clone2.1) | copy-start | bytes 3076
  1340.8 102.2 %copy-start.53 = (s32[256]{0:T(256)S(1)}, s32[256]{0:T(256)}, u32[]{:S(2)}) copy-start(s32[256]{0:T(256)} %param.25) | copy-start | bytes 3076
  1435.1 17.7 all-to-all-start.5
  1452.8 17.7 all-to-all-start.6
  1470.5 761.2 %all-to-all-start.7 = ((bf16[16,128,128]{2,1,0:T(8,128)(2,1)}), bf16[16,128,128]{2,1,0:T(8,128)(2,1)S(1)}, u32[]{:S(2)}, u32[]{:S(2)}) async-start(bf16[16,128,128]{2,1,0:T(8,128)(2,1)} %bitcast.97), calls=%async_computation.7 | async-start | bytes 1048576 | tf_op jit(solution)/shard_map/all_to_all | solution.py:291
  2232.6 792.4 %all-to-all-start.8 = ((bf16[256,128,512]{2,1,0:T(8,128)(2,1)}), bf16[256,128,512]{2,1,0:T(8,128)(2,1)}, u32[]{:S(2)}, u32[]{:S(2)}) async-start(bf16[256,128,512]{2,1,0:T(8,128)(2,1)} %get-tuple-element.403), calls=%async_computation.8 | async-start | bytes 67108864 | tf_op jit(solution)/shard_map/all_to_all | solution.py:320
  3025.0 886.6 %all-to-all-start.9 = ((bf16[256,128,512]{2,1,0:T(8,128)(2,1)}), bf16[256,128,512]{2,1,0:T(8,128)(2,1)}, u32[]{:S(2)}, u32[]{:S(2)}) async-start(bf16[256,128,512]{2,1,0:T(8,128)(2,1)} %get-tuple-element.411), calls=%async_computation.9 | async-start | bytes 67108864 | tf_op jit(solution)/shard_map/all_to_all | solution.py:321
  3045.9 753.8 %copy-start.13 = (f32[128,16,128]{0,2,1:T(8,128)S(1)}, f32[128,16,128]{0,2,1:T(8,128)}, u32[]{:S(2)}) copy-start(f32[128,16,128]{0,2,1:T(8,128)} %copy.186) | copy-start | bytes 3145732
  3045.9 756.0 %copy-start.39 = (f32[4,2048]{1,0:T(4,128)S(1)}, f32[4,2048]{1,0:T(4,128)}, u32[]{:S(2)}) copy-start(f32[4,2048]{1,0:T(4,128)} %param.27) | copy-start | bytes 98308
  (53 other events, 825.6 us)
Sparse Core Ops, SparseCore 0:
  13.4 681.4 all-gather.1
where the time goes:
time: 4080 us; the launch traced here: 4050 us
  local copies, waits for them, and re-layouts  2060 us (50%)
  blocking collectives  787 us (19%)
  waiting for transfers between devices  661 us (16%)
  matrix products  307 us (8%)
  other arithmetic  137 us (3%)
  starting transfers between devices  57.1 us (1%)
    gather x1536, local copies, waits for them, and re-layouts  1490 us
    psum x1, blocking collectives, body(): gain_grads = lax.psum(gain_local, ('head', 'seq'))  744 us
    all_gather x1, waiting for transfers between devices, body(): lax.all_gather(weights.astype(jnp.bfloat16), ('head', 'seq'), axis=0, til...  634 us
    dot_general x4, local copies, waits for them, and re-layouts, grid_mul(): jnp.einsum('trk,rckn->tcn', shaped, grid, preferred_element_type=jnp.floa...  146 us
    dot_general x7, local copies, waits for them, and re-layouts, grid_back(): jnp.einsum('tcn,rckn->trk', shaped, grid, preferred_element_type=jnp.floa...  98.8 us
    all_to_all x2, local copies, waits for them, and re-layouts, body(): lax.all_to_all(left_send, ('head', 'seq'), split_axis=0, concat_axis=1, t...  95.5 us
    gather x7, local copies, waits for them, and re-layouts, assemble(): picked = jnp.take(every_block, inverse[offset:offset + number], axis=0)  94.1 us
    select_n x5, other arithmetic, assemble(): picked = jnp.take(every_block, inverse[offset:offset + number], axis=0)  87.2 us
  transfers between devices with their start and end apart: 11, of which 4 were waited for; matrix products, arithmetic and copies ran while one was open for 50% of the time, Pallas kernels for 0%

commit v1 on v0

v1 whole, which is shorter than its diff:
```python
import jax
import jax.numpy as jnp
from jax import lax
from jax.sharding import Mesh
from jax.sharding import PartitionSpec as P

FF = 8192
HEADS = 16
SEGMAX = 1024
QB = 512
Z = 4

epsilon = 1e-06
rope_base = 500000.0
decay_rate = 0.5
step_rate = 0.5
gain_rate = 0.3
bf16 = jnp.bfloat16
f32 = jnp.float32
EVERY = ("hz", "hp", "seq")


def mm(left_side, right_side):
    return jnp.dot(left_side, right_side, preferred_element_type=f32)


def mm_nt(left_side, right_side):
    return lax.dot_general(
        left_side, right_side, (((1,), (1,)), ((), ())), preferred_element_type=f32
    )


def mm_tn(left_side, right_side):
    return lax.dot_general(
        left_side, right_side, (((0,), (0,)), ((), ())), preferred_element_type=f32
    )


def rms_norm(values, gain_vec):
    return (
        values * lax.rsqrt(jnp.mean(values * values, axis=-1, keepdims=True) + epsilon) * gain_vec
    )


def positions_of(segment_row):
    length = segment_row.shape[0]
    indices = jnp.arange(length, dtype=jnp.int32)
    earlier = jnp.concatenate([jnp.full((1,), -1, jnp.int32), segment_row[:-1]])
    begins = lax.cummax(jnp.where(segment_row != earlier, indices, 0), axis=0)
    return indices - begins


UP = [(i, (i + 1) % Z) for i in range(Z)]


def ring_gather(block):
    blocks = [block]
    for _ in range(Z - 1):
        blocks.append(lax.ppermute(blocks[-1], "hz", UP))
    return blocks


def ring_scatter(part_of):
    total = part_of(1).astype(bf16)
    for k in (2, 3):
        total = (lax.ppermute(total, "hz", UP).astype(f32) + part_of(k)).astype(bf16)
    return lax.ppermute(total, "hz", UP).astype(f32) + part_of(0)


def sum_z(values):
    values = values + lax.ppermute(values, "hz", [(i, i ^ 1) for i in range(Z)])
    return values + lax.ppermute(values, "hz", [(i, i ^ 2) for i in range(Z)])


def body(
    tokens,
    cotangent,
    segment_ids,
    owner_map,
    weights,
    norm_gains,
    left_stats,
    right_stats,
    left_root,
    right_root,
):
    model_width = tokens.shape[2]
    local_count = tokens.shape[1]
    slots, side = weights.shape[0], weights.shape[1]
    total_blocks = owner_map.shape[0]
    PN, S = lax.axis_size("hp"), lax.axis_size("seq")
    n = Z * PN * S
    rep = PN * S
    rows = side // n
    head_size = model_width // HEADS
    quarter = model_width // Z
    score_scale = head_size ** (-0.5)
    zi, pi = lax.axis_index("hz"), lax.axis_index("hp")
    relative = (zi - jnp.arange(Z, dtype=jnp.int32)) % Z
    inputs = tokens[0]

    d_blocks, f_blocks = model_width // side, FF // side
    number = jnp.arange(total_blocks, dtype=jnp.int32)
    square = d_blocks * d_blocks
    tall = d_blocks * f_blocks
    lists = []
    grid = number[:square].reshape(d_blocks, Z, d_blocks // Z)
    for m in range(3):
        lists.append((grid + m * square).transpose(1, 0, 2).reshape(Z, -1))
    lists.append((number[:square] + 3 * square).reshape(Z, -1))
    grid = number[:tall].reshape(d_blocks, Z, f_blocks // Z).transpose(1, 0, 2).reshape(Z, -1)
    lists.append(grid + 4 * square)
    lists.append(grid + 4 * square + tall)
    lists.append(number[:tall].reshape(Z, -1) + 4 * square + 2 * tall)
    inverse = jnp.zeros((total_blocks,), jnp.int32).at[owner_map].set(number)

    low = weights.astype(bf16).reshape(slots, PN, S, Z, rows, side)
    low = low.transpose(3, 1, 2, 0, 4, 5).reshape(n * slots, rows, side)
    spread = lax.all_to_all(low, EVERY, 0, 0, tiled=True)

    def fetch(block_lists):
        order = jnp.concatenate(block_lists, axis=1)
        picked = jnp.take(spread, inverse[order.reshape(-1)], axis=0)
        got = lax.all_to_all(picked, "hz", 0, 0, tiled=True)
        got = got.reshape(Z, -1, rows, side).transpose(1, 0, 2, 3).reshape(-1, Z * rows, side)
        return lax.all_gather(got, ("hp", "seq"), axis=0, tiled=False)

    qkvo = fetch(lists[:4])
    gateup = fetch(lists[4:6])
    downs = fetch(lists[6:])

    def matrix(gathered, row_blocks):
        shaped = gathered.reshape(rep, row_blocks, -1, Z * rows, side)
        return shaped.transpose(1, 0, 3, 2, 4).reshape(row_blocks * side, -1)

    w_query, w_key, w_value = (
        matrix(qkvo[:, m * d_blocks : (m + 1) * d_blocks], d_blocks) for m in range(3)
    )
    w_output = matrix(qkvo[:, 3 * d_blocks :], d_blocks // Z)
    half = gateup.shape[1] // 2
    w_gate, w_up = matrix(gateup[:, :half], d_blocks), matrix(gateup[:, half:], d_blocks)
    w_down = matrix(downs, f_blocks // Z)

    group = Z * PN
    row_ids = lax.all_to_all(
        jnp.broadcast_to(segment_ids, (group, local_count)), ("hz", "hp"), 0, 0, tiled=True
    ).reshape(-1)
    row_length = row_ids.shape[0]
    tokens_g = lax.all_gather(inputs, "hz", axis=0, tiled=True)
    places = lax.dynamic_slice_in_dim(
        positions_of(row_ids).reshape(Z, PN, local_count), pi, 1, axis=1
    ).reshape(-1)
    group_tokens = Z * local_count
    half_size = head_size // 2
    frequency = rope_base ** (-2.0 * jnp.arange(half_size, dtype=f32) / head_size)
    angles = places.astype(f32)[:, None] * frequency[None, :]
    cosine = jnp.cos(angles)[:, None, :]
    sine = jnp.sin(angles)[:, None, :]

    def rope(values, sign):
        grouped = values.reshape(group_tokens, -1, head_size)
        first, second = grouped[..., :half_size], grouped[..., half_size:]
        turned = jnp.concatenate(
            [first * cosine - second * sine * sign, second * cosine + first * sine * sign], axis=-1
        )
        return turned.reshape(group_tokens, -1)

    gains_z = lax.dynamic_slice_in_dim(norm_gains[2:4], zi * quarter, quarter, axis=1)

    query_raw = mm(tokens_g, w_query)
    key_raw = mm(tokens_g, w_key)
    value_low = mm(tokens_g, w_value).astype(bf16)
    squares = jnp.stack([jnp.sum(query_raw * query_raw, -1), jnp.sum(key_raw * key_raw, -1)])
    invs = lax.rsqrt(sum_z(squares) / model_width + epsilon)
    query_hat, key_hat = query_raw * invs[0][:, None], key_raw * invs[1][:, None]
    query_low = rope(query_hat * gains_z[0], 1.0).astype(bf16)
    key_low = rope(key_hat * gains_z[1], 1.0).astype(bf16)

    def to_heads(stack):
        m = stack.shape[0]
        shaped = stack.reshape(m, Z, local_count, PN, -1).transpose(3, 0, 1, 2, 4)
        got = lax.all_to_all(shaped, "hp", 0, 0, tiled=True)
        return got.transpose(1, 2, 0, 3, 4).reshape(m, row_length, -1)

    def to_groups(stack):
        m = stack.shape[0]
        shaped = stack.reshape(m, Z, PN, local_count, -1).transpose(2, 0, 1, 3, 4)
        got = lax.all_to_all(shaped, "hp", 0, 0, tiled=True)
        return got.transpose(1, 2, 3, 0, 4).reshape(m, group_tokens, -1)

    qkv_rows = to_heads(jnp.stack([query_low, key_low, value_low]))
    query_rows, key_rows, value_rows = qkv_rows[0], qkv_rows[1], qkv_rows[2]
    local_width = query_rows.shape[1]
    local_heads = local_width // head_size
    window = min(QB + SEGMAX, row_length)
    block_count = row_length // QB
    starts = jnp.arange(block_count, dtype=jnp.int32) * QB

    def block_scores(query_start):
        key_start = jnp.clip(query_start + QB - window, 0, row_length - window)
        query_blk = lax.dynamic_slice_in_dim(query_rows, query_start, QB).reshape(
            QB, local_heads, head_size
        )
        key_blk = lax.dynamic_slice_in_dim(key_rows, key_start, window).reshape(
            window, local_heads, head_size
        )
        value_blk = lax.dynamic_slice_in_dim(value_rows, key_start, window).reshape(
            window, local_heads, head_size
        )
        raw_scores = (
            jnp.einsum("qhd,khd->hqk", query_blk, key_blk, preferred_element_type=f32)
            * score_scale
        )
        query_ids = lax.dynamic_slice_in_dim(row_ids, query_start, QB)
        key_ids = lax.dynamic_slice_in_dim(row_ids, key_start, window)
        query_place = query_start + jnp.arange(QB, dtype=jnp.int32)
        key_place = key_start + jnp.arange(window, dtype=jnp.int32)
        allowed = (query_ids[:, None] == key_ids[None, :]) & (
            key_place[None, :] <= query_place[:, None]
        )
        scores = jnp.where(allowed[None], raw_scores, -1e30)
        return (scores, query_blk, key_blk, value_blk, key_start)

    def attend(query_start):
        scores, query_blk, key_blk, value_blk, key_start = block_scores(query_start)
        top_score = jnp.max(scores, axis=-1, keepdims=True)
        expo = jnp.exp(scores - top_score)
        totals = jnp.sum(expo, axis=-1, keepdims=True)
        attention = (expo / totals).astype(bf16)
        mixture = jnp.einsum("hqk,khd->qhd", attention, value_blk, preferred_element_type=f32)
        return (
            mixture.reshape(QB, local_width).astype(bf16),
            (top_score + jnp.log(totals))[..., 0],
        )

    mixed_blocks, log_sums = lax.map(attend, starts)
    attended = to_groups(mixed_blocks.reshape(1, row_length, local_width))[0]
    attended_rel = jnp.take(attended.reshape(Z, local_count, quarter), relative, axis=0)
    attn_raw = ring_scatter(lambda k: mm(attended_rel[k], w_output))
    resid = inputs.astype(f32) + rms_norm(attn_raw, norm_gains[0])
    resid_low = resid.astype(bf16)

    resid_blocks = ring_gather(resid_low)
    gates = [mm(b, w_gate) for b in resid_blocks]
    ups = [mm(b, w_up) for b in resid_blocks]
    hiddens = [(jax.nn.silu(g) * u).astype(bf16) for g, u in zip(gates, ups)]
    down_raw = ring_scatter(lambda k: mm(hiddens[k], w_down))
    output = (resid + rms_norm(down_raw, norm_gains[1])).astype(bf16)[None]

    upstream = cotangent[0].astype(f32)
    _, down_norm_back = jax.vjp(rms_norm, down_raw, norm_gains[1])
    down_grad, gain_mlp_grad = down_norm_back(upstream)
    down_blocks = ring_gather(down_grad.astype(bf16))
    gate_lows, up_lows = [], []
    for block, gate, up in zip(down_blocks, gates, ups):
        hidden_grad = mm_nt(block, w_down)
        sigma = jax.nn.sigmoid(gate)
        gate_lows.append((hidden_grad * up * sigma * (1.0 + gate * (1.0 - sigma))).astype(bf16))
        up_lows.append((hidden_grad * gate * sigma).astype(bf16))
    resid_grad = upstream + ring_scatter(
        lambda k: mm_nt(gate_lows[k], w_gate) + mm_nt(up_lows[k], w_up)
    )

    def send_grads(pieces):
        joined = jnp.concatenate(pieces, axis=1)
        summed = lax.psum_scatter(joined, ("hp", "seq"), scatter_dimension=0, tiled=True)
        summed = summed.reshape(-1, Z, rows, side).transpose(1, 0, 2, 3)
        return lax.all_to_all(summed, "hz", 0, 0, tiled=True)

    def pieces_of(matrix_grad, row_blocks):
        shaped = matrix_grad.astype(bf16).reshape(row_blocks, rep, Z * rows, -1, side)
        return shaped.transpose(1, 0, 3, 2, 4).reshape(rep, -1, Z * rows, side)

    resid_all = jnp.concatenate(resid_blocks)
    gate_all, up_all = jnp.concatenate(gate_lows), jnp.concatenate(up_lows)
    hidden_all, down_all = jnp.concatenate(hiddens), jnp.concatenate(down_blocks)
    down_sent = send_grads([pieces_of(mm_tn(hidden_all, down_all), f_blocks // Z)])
    gateup_sent = send_grads(
        [
            pieces_of(mm_tn(resid_all, gate_all), d_blocks),
            pieces_of(mm_tn(resid_all, up_all), d_blocks),
        ]
    )

    _, attn_norm_back = jax.vjp(rms_norm, attn_raw, norm_gains[0])
    attn_grad, gain_attn_grad = attn_norm_back(resid_grad)
    attn_blocks = ring_gather(attn_grad.astype(bf16))
    attn_all = jnp.concatenate(attn_blocks)
    attended_grad = mm_nt(attn_all, w_output).astype(bf16)
    output_grad_w = mm_tn(attended_rel.reshape(group_tokens, quarter), attn_all)
    grad_abs = jnp.take(attended_grad.reshape(Z, local_count, quarter), relative, axis=0)
    grad_rows = to_heads(grad_abs.reshape(1, group_tokens, quarter))[0]

    def attend_back(carry, paired):
        key_acc, value_acc = carry
        query_start, log_sum = paired
        scores, query_blk, key_blk, value_blk, key_start = block_scores(query_start)
        attention = jnp.exp(scores - log_sum[..., None])
        grad_blk = lax.dynamic_slice_in_dim(grad_rows, query_start, QB).reshape(
            QB, local_heads, head_size
        )
        prob_grad = jnp.einsum("qhd,khd->hqk", grad_blk, value_blk, preferred_element_type=f32)
        center = jnp.sum(attention * prob_grad, axis=-1, keepdims=True)
        score_grad = (attention * (prob_grad - center)).astype(bf16)
        query_grad = (
            jnp.einsum("hqk,khd->qhd", score_grad, key_blk, preferred_element_type=f32)
            * score_scale
        )
        key_part = (
            jnp.einsum("hqk,qhd->khd", score_grad, query_blk, preferred_element_type=f32)
            * score_scale
        )
        value_part = jnp.einsum(
            "hqk,qhd->khd", attention.astype(bf16), grad_blk, preferred_element_type=f32
        )
        key_now = lax.dynamic_slice_in_dim(key_acc, key_start, window)
        value_now = lax.dynamic_slice_in_dim(value_acc, key_start, window)
        key_acc = lax.dynamic_update_slice_in_dim(key_acc, key_now + key_part, key_start, 0)
        value_acc = lax.dynamic_update_slice_in_dim(value_acc, value_now + value_part, key_start, 0)
        return ((key_acc, value_acc), query_grad.reshape(QB, local_width))

    zero_rows = jnp.zeros((row_length, local_heads, head_size), f32)
    (key_total, value_total), query_blocks = lax.scan(
        attend_back, (zero_rows, zero_rows), (starts, log_sums)
    )
    back = to_groups(
        jnp.stack(
            [
                query_blocks.reshape(row_length, local_width).astype(bf16),
                key_total.reshape(row_length, local_width).astype(bf16),
                value_total.reshape(row_length, local_width).astype(bf16),
            ]
        )
    )
    value_back = back[2]
    query_turn, key_turn = rope(back[0].astype(f32), -1.0), rope(back[1].astype(f32), -1.0)
    gain_query = jnp.sum(query_turn * query_hat, axis=0)
    gain_key = jnp.sum(key_turn * key_hat, axis=0)
    query_turn, key_turn = query_turn * gains_z[0], key_turn * gains_z[1]
    dots = sum_z(jnp.stack([jnp.sum(query_turn * query_hat, -1), jnp.sum(key_turn * key_hat, -1)]))
    dots = dots / model_width
    query_back = ((query_turn - query_hat * dots[0][:, None]) * invs[0][:, None]).astype(bf16)
    key_back = ((key_turn - key_hat * dots[1][:, None]) * invs[1][:, None]).astype(bf16)
    attn_sent = send_grads(
        [
            pieces_of(mm_tn(tokens_g, query_back), d_blocks),
            pieces_of(mm_tn(tokens_g, key_back), d_blocks),
            pieces_of(mm_tn(tokens_g, value_back), d_blocks),
            pieces_of(output_grad_w, d_blocks // Z),
        ]
    )
    back_rel = jnp.take(
        jnp.stack([query_back, key_back, value_back]).reshape(3, Z, local_count, quarter),
        relative,
        axis=1,
    )
    input_grad = resid_grad + ring_scatter(
        lambda k: mm_nt(back_rel[0, k], w_query)
        + mm_nt(back_rel[1, k], w_key)
        + mm_nt(back_rel[2, k], w_value)
    )

    spots = jnp.zeros((2, model_width), f32)
    spots = lax.dynamic_update_slice(spots, jnp.stack([gain_query, gain_key]), (0, zi * quarter))
    gain_local = jnp.concatenate([jnp.stack([gain_attn_grad, gain_mlp_grad]), spots])
    shares = lax.all_to_all(gain_local.reshape(n, -1), EVERY, 0, 0, tiled=True)
    share = jnp.sum(shares, axis=0)
    gain_grads = lax.all_to_all(
        jnp.broadcast_to(share, (n, share.shape[0])), EVERY, 0, 0, tiled=True
    ).reshape(gain_local.shape)

    sent = jnp.concatenate([attn_sent, gateup_sent, down_sent], axis=1)
    sent = sent.reshape(total_blocks, rows, side)
    order = jnp.concatenate(lists, axis=1).reshape(-1)
    where_is = jnp.zeros((total_blocks,), jnp.int32).at[order].set(number)
    to_slots = jnp.take(sent, where_is[owner_map], axis=0)
    got = lax.all_to_all(to_slots, EVERY, 0, 0, tiled=True)
    got = got.reshape(Z, PN, S, slots, rows, side).transpose(3, 1, 2, 0, 4, 5)
    grad_low = got.reshape(slots, side, side)
    grad_slots = grad_low.astype(f32)

    def batched(left_side, right_side, form):
        return jnp.einsum(form, left_side, right_side, preferred_element_type=f32)

    left_new = decay_rate * left_stats + (1.0 - decay_rate) * batched(
        grad_low, grad_low, "sij,skj->sik"
    )
    right_new = decay_rate * right_stats + (1.0 - decay_rate) * batched(
        grad_low, grad_low, "sji,sjk->sik"
    )
    middle = batched(left_root.astype(bf16), grad_low, "sij,sjk->sik").astype(bf16)
    update = batched(middle, right_root.astype(bf16), "sij,sjk->sik")
    new_weights = weights - step_rate * update
    new_gains = norm_gains - gain_rate * gain_grads * lax.rsqrt(
        jnp.mean(gain_grads * gain_grads, axis=1, keepdims=True) + epsilon
    )
    return (
        output,
        input_grad[None],
        grad_slots,
        left_new,
        right_new,
        new_weights,
        gain_grads,
        new_gains,
    )


def solution(mesh):
    heads, seqs = mesh.shape["head"], mesh.shape["seq"]
    fine = Mesh(mesh.devices.reshape(Z, heads // Z, seqs), EVERY)
    tok = P("seq", ("hz", "hp"), None)
    slot = P(EVERY, None, None)
    return jax.shard_map(
        body,
        mesh=fine,
        in_specs=(tok, tok, P("seq", ("hz", "hp")), P(), slot, P(), slot, slot, slot, slot),
        out_specs=(tok, tok, slot, slot, slot, slot, P(), P()),
        check_vma=False,
    )
```

time: 4080 us -> 1510 us (0.37)
  local copies, waits for them, and re-layouts: 2060 us -> 320 us
  blocking collectives: 787 us -> 139 us
  matrix products: 307 us -> 231 us
  other arithmetic: 137 us -> 71.9 us
  waiting for transfers between devices: 661 us -> 609 us
    gather x1545 -> x11, local copies, waits for them, and re-layouts: 1590 us -> 22.9 us  [the longest x6 11.3 us: fetch(): picked = jnp.take(spread, inverse[order.reshape(-1)], axis=0)]
    psum x1 -> x0, blocking collectives: 744 us -> none  [body(): gain_grads = lax.psum(gain_local, ('head', 'seq'))]
    all_gather x1 -> x4, waiting for transfers between devices: 634 us -> 0.04 us  [the longest x3 0.02 us: fetch(): return lax.all_gather(got, ('hp', 'seq'), axis=0, tiled=False)]
    dot_general x11 -> x0, local copies, waits for them, and re-layouts: 245 us -> none  [the longest x4 146 us: grid_mul(): jnp.einsum('trk,rckn->tcn', shaped, grid, preferred_element_type=jnp.floa...]
    ppermute x0 -> x25, waiting for transfers between devices: none -> 223 us  [the longest x8 114 us: ring_scatter(): lax.ppermute(total, 'hz', UP).astype(f32) + part_of(k)]
    reduce_scatter x0 -> x2, waiting for transfers between devices: none -> 181 us  [send_grads(): lax.psum_scatter(joined, ('hp', 'seq'), scatter_dimension=0, tiled=True)]
    all_to_all x10 -> x12, waiting for transfers between devices: 26.5 us -> 199 us  [the longest x1 90.4 us: body(): spread = lax.all_to_all(low, EVERY, 0, 0, tiled=True)]
    all_to_all x0 -> x3, blocking collectives: none -> 139 us  [fetch(): got = lax.all_to_all(picked, 'hz', 0, 0, tiled=True)]
  transfers between devices with their start and end apart: 11 -> 44, of which waited for: 4 -> 29; matrix products, arithmetic and copies ran while one was open for 50% -> 27% of each run, Pallas kernels for 0% -> 0%
where the time goes in v1:
time: 1510 us; the launch traced here: 1500 us
  waiting for transfers between devices  609 us (40%)
  local copies, waits for them, and re-layouts  320 us (21%)
  matrix products  231 us (15%)
  blocking collectives  139 us (9%)
  starting transfers between devices  92.4 us (6%)
  other arithmetic  71.9 us (5%)
  loops' own time  21.3 us (1%)
  between operations  16.8 us (1%)
    reduce_scatter x2, waiting for transfers between devices, send_grads(): lax.psum_scatter(joined, ('hp', 'seq'), scatter_dimension=0, tiled=True)  181 us
    all_to_all x3, blocking collectives, fetch(): got = lax.all_to_all(picked, 'hz', 0, 0, tiled=True)  139 us
    ppermute x8, waiting for transfers between devices, ring_scatter(): lax.ppermute(total, 'hz', UP).astype(f32) + part_of(k)  114 us
    all_to_all x1, waiting for transfers between devices, body(): spread = lax.all_to_all(low, EVERY, 0, 0, tiled=True)  90.4 us
    reshape x8, local copies, waits for them, and re-layouts, pieces_of(): matrix_grad.astype(bf16).reshape(row_blocks, rep, Z * rows, -1, side)  81.5 us
    dot_general x25, matrix products, mm_nt(): lax.dot_general(left_side, right_side, (((1,), (1,)), ((), ())), preferre...  67.1 us
    ppermute x9, waiting for transfers between devices, ring_gather(): blocks.append(lax.ppermute(blocks[-1], 'hz', UP))  60.4 us
    unnamed x263, local copies, waits for them, and re-layouts  51 us
  transfers between devices with their start and end apart: 44, of which 29 were waited for; matrix products, arithmetic and copies ran while one was open for 27% of the time, Pallas kernels for 0%

profile of v1, /device:TPU:0, one launch (start us, length us, event | category | flops | bytes accessed | tf_op | source)
XLA Modules:
  0.0 1501.4 jit_solution(11378801178923654345)
XLA Ops:
  24.5 90.4 %all-to-all-done = bf16[256,16,512]{2,1,0:T(8,128)(2,1)} async-done(((bf16[256,16,512]{2,1,0:T(8,128)(2,1)}), bf16[256,16,512]{2,1,0:T(8,128)(2,1)}, u32[]{:S(2)}, u32[]{:S(2)}) %all-to-all-start) | async-done | bytes 4194336 | tf_op jit(solution)/shard_map/all_to_all | solution.py:119
  117.8 29.1 %all_to_all.84 = bf16[64,16,512]{2,1,0:T(8,128)(2,1)S(1)} all-to-all(bf16[64,16,512]{2,1,0:T(8,128)(2,1)S(1)} %broadcast_select_fusion.3), channel_id=1, replica_groups=mesh['hz'=4,'hp'=4,'seq'=2] {'hz'}, dimensions={0} | all-to-all | bytes 2097152 | tf_op jit(solution)/shard_map/all_to_all | solution.py:124
  153.2 27.7 %all_to_all.85 = bf16[64,16,512]{2,1,0:T(8,128)(2,1)S(1)} all-to-all(bf16[64,16,512]{2,1,0:T(8,128)(2,1)S(1)} %broadcast_select_fusion.2), channel_id=1, replica_groups=mesh['hz'=4,'hp'=4,'seq'=2] {'hz'}, dimensions={0} | all-to-all | bytes 2097152 | tf_op jit(solution)/shard_map/all_to_all | solution.py:124
  187.1 82.6 %all_to_all.86 = bf16[128,16,512]{2,1,0:T(8,128)(2,1)S(1)} all-to-all(bf16[128,16,512]{2,1,0:T(8,128)(2,1)S(1)} %broadcast_select_fusion.1), channel_id=1, replica_groups=mesh['hz'=4,'hp'=4,'seq'=2] {'hz'}, dimensions={0} | all-to-all | bytes 4194304 | tf_op jit(solution)/shard_map/all_to_all | solution.py:124
  314.3 27.9 %all-to-all-done.3 = bf16[4,3,4,128,128]{3,2,4,1,0:T(4,128)(2,1)S(1)} async-done(((bf16[4,3,4,128,128]{3,2,4,1,0:T(4,128)(2,1)}), bf16[4,3,4,128,128]{3,2,4,1,0:T(4,128)(2,1)S(1)}, u32[]{:S(2)}, u32[]{:S(2)}) %all-to-all-start.3) | async-done | bytes 1572896 | tf_op jit(solution)/shard_map/all_to_all | solution.py:182
  344.5 40.4 %while.34 = (s32[]{:T(128)}, bf16[4,512,128]{2,1,0:T(8,128)(2,1)}, f32[4,1,512]{2,1,0:T(1,128)}, s32[4]{0:T(128)S(1)}, bf16[2048,128]{1,0:T(8,128)(2,1)}, /*inde...) while((s32[]{:T(128)}, bf16[4,512,128]{2,1,0:T(8,128)(2,1)}, ...), condition=%wide.region_8.10_spmd, body=%wide.region_5.9_spmd.sunk | while | flops 411371008 | bytes 11071739 | solution.py:236
  393.8 11.8 all-to-all-done.4
  409.7 11.8 collective-permute-done.2
  448.0 12.9 collective-permute-done.5
  667.3 12.1 collective-permute-done.16
  680.7 12.7 collective-permute-done.17
  693.5 11.8 collective-permute-done.18
  733.0 112.3 %while.35 = (s32[]{:T(128)}, f32[2048,1,128]{2,0,1:T(8,128)}, f32[2048,1,128]{2,0,1:T(8,128)}, bf16[4,512,128]{2,1,0:T(8,128)(2,1)}, s32[4]{0:T(128)S(1)}, /*ind...) while((s32[]{:T(128)}, f32[2048,1,128]{2,0,1:T(8,128)}, ...), condition=%wide.region_15.18_spmd, body=%wide.region_13.17_spmd.sunk | while | flops 1016792576 | bytes 54315336 | solution.py:323
  926.4 14.7 reshape.944
  961.1 14.7 reshape.941
  993.6 14.5 reshape.939
  1018.0 14.1 pad_maximum_fusion
  1052.0 68.2 %reduce-scatter.8.cloned.1.call-done = bf16[1,16,64,512]{3,2,1,0:T(8,128)(2,1)} async-done(((bf16[8,16,64,512]{3,2,1,0:T(8,128)(2,1)}), bf16[1,16,64,512]{3,2,1,0:T(8,128)(2,1)}) %reduce-scatter.8.cloned.1.call-update) | async-done | bytes 1048592 | tf_op jit(solution)/shard_map/reduce_scatter | solution.py:266
  1127.0 112.7 %reduce-scatter.6.cloned.1.call-done = bf16[1,32,64,512]{3,2,1,0:T(8,128)(2,1)} async-done(((bf16[8,32,64,512]{3,2,1,0:T(8,128)(2,1)}), bf16[1,32,64,512]{3,2,1,0:T(8,128)(2,1)}) %reduce-scatter.6.cloned.1.call-update) | async-done | bytes 2097168 | tf_op jit(solution)/shard_map/reduce_scatter | solution.py:266
  1252.5 44.3 %all-to-all-done.10 = bf16[4,32,16,512]{3,2,1,0:T(8,128)(2,1)S(1)} async-done(((bf16[4,32,16,512]{3,2,1,0:T(8,128)(2,1)}), bf16[4,32,16,512]{3,2,1,0:T(8,128)(2,1)S(1)}, u32[]{:S(2)}, u32[]{:S(2)}) %all-to-all-start.10) | async-done | bytes 2097184 | tf_op jit(solution)/shard_map/all_to_all | solution.py:268
  1334.8 67.5 %collective-permute-done.22 = bf16[128,2048]{1,0:T(8,128)(2,1)S(1)} collective-permute-done((bf16[128,2048]{1,0:T(8,128)(2,1)S(1)}, bf16[128,2048]{1,0:T(8,128)(2,1)S(1)}, u32[]{:S(2)}, u32[]{:S(2)}) %collective-permute-start.22) | collective-permute-done | bytes 524320 | tf_op jit(solution)/shard_map/ppermute | solution.py:66
  1403.9 20.5 %collective-permute-start.23 = (bf16[128,2048]{1,0:T(8,128)(2,1)}, bf16[128,2048]{1,0:T(8,128)(2,1)}, u32[]{:S(2)}, u32[]{:S(2)}) collective-permute-start(bf16[128,2048]{1,0:T(8,128)(2,1)} %add_convert_fusion.1), channel_id=1, source_target_pairs={{0,8},{8,16},{16,24},{24,0},{1,9},{9,17},{17,25},{25,1},{2,10},{10... | collective-permute-start | bytes 1572872 | tf_op jit(solution)/shard_map/ppermute | solution.py:66
  1441.5 12.7 collective-permute-done.24
  1478.6 15.5 %multiply_subtract_fusion = f32[8,512,512]{2,1,0:T(8,128)} fusion(f32[8,512,512]{2,1,0:T(8,128)} %param.22, f32[8,512,512]{2,1,0:T(8,128)} %param.27, bf16[8,512,512]{2,1,0:T(8,128)(2,1)} %bitcast.510, f32[8,512,512]{2,1,0:T(8,128)} %param.26), kind=kOutput, calls=%fused_computation.66 | convolution fusion | flops 4305453056 | bytes 37748736 | tf_op jit(solution)/shard_map/sij,sjk->sik/dot_general | solution.py:383
  (729 shorter events, 733.0 us)
Async XLA Ops:
  13.6 101.3 %all-to-all-start = ((bf16[256,16,512]{2,1,0:T(8,128)(2,1)}), bf16[256,16,512]{2,1,0:T(8,128)(2,1)}, u32[]{:S(2)}, u32[]{:S(2)}) async-start(bf16[256,16,512]{2,1,0:T(8,128)(2,1)} %bitcast.540), calls=%async_computation | async-start | bytes 8388608 | tf_op jit(solution)/shard_map/all_to_all | solution.py:119
  21.0 263.9 %all-gather.6.cloned.1.call-start = ((), (), s32[]{:S(2)}) async-start(), calls=%async_computation.17 | async-start | bytes 9437184 | tf_op jit(solution)/shard_map/all_gather | solution.py:126
  148.0 143.8 %all-gather.12.cloned.1.call-start = ((), (), s32[]{:S(2)}) async-start(), calls=%async_computation.22 | async-start | bytes 2621440 | tf_op jit(solution)/shard_map/all_gather | solution.py:149
  148.8 312.2 %all-gather.10.cloned.1.call-start = ((), (), s32[]{:S(2)}) async-start(), calls=%async_computation.19 | async-start | bytes 9437184 | tf_op jit(solution)/shard_map/all_gather | solution.py:126
  182.0 301.1 %all-gather.8.cloned.1.call-start = ((), (), s32[]{:S(2)}) async-start(), calls=%async_computation.18 | async-start | bytes 18874368 | tf_op jit(solution)/shard_map/all_gather | solution.py:126
  310.7 31.5 %all-to-all-start.3 = ((bf16[4,3,4,128,128]{3,2,4,1,0:T(4,128)(2,1)}), bf16[4,3,4,128,128]{3,2,4,1,0:T(4,128)(2,1)S(1)}, u32[]{:S(2)}, u32[]{:S(2)}) async-start(bf16[4,3,4,128,128]{3,2,4,1,0:T(4,128)(2,1)} %maximum_bitcast_fusion), calls=%async_computation.3 | async-start | bytes 3145728 | tf_op jit(solution)/shard_map/all_to_all | solution.py:182
  387.1 18.5 %all-to-all-start.4 = ((bf16[4,1,4,128,128]{4,3,2,1,0:T(8,128)(2,1)}), bf16[4,1,4,128,128]{4,3,2,1,0:T(8,128)(2,1)}, u32[]{:S(2)}, u32[]{:S(2)}) async-start(bf16[4,1,4,128,128]{4,3,2,1,0:T(8,128)(2,1)} %copy.225), calls=%async_computation.4 | async-start | bytes 1048576 | tf_op jit(solution)/shard_map/all_to_all | solution.py:188
  460.9 21.7 %collective-permute-start.7 = (bf16[128,2048]{1,0:T(8,128)(2,1)S(1)}, bf16[128,2048]{1,0:T(8,128)(2,1)}, u32[]{:S(2)}, u32[]{:S(2)}) collective-permute-start(bf16[128,2048]{1,0:T(8,128)(2,1)S(1)} %collective-permute-done.5), channel_id=1, source_target_pairs={{0,8},{8,16},{16,24},{24,0},{1,9},{9,17},{17,25},{25,1},{2,10},{10... | collective-permute-start | bytes 1572872 | tf_op jit(solution)/shard_map/ppermute | solution.py:59
  482.6 64.9 %collective-permute-start.9 = (bf16[128,2048]{1,0:T(8,128)(2,1)}, bf16[128,2048]{1,0:T(8,128)(2,1)}, u32[]{:S(2)}, u32[]{:S(2)}) collective-permute-start(bf16[128,2048]{1,0:T(8,128)(2,1)} %collective-permute-done.7), channel_id=1, source_target_pairs={{0,8},{8,16},{16,24},{24,0},{1,9},{9,17},{17,25},{25,1},{2,10},{10... | collective-permute-start | bytes 1572872 | tf_op jit(solution)/shard_map/ppermute | solution.py:59
  561.0 16.3 %collective-permute-start.8 = (bf16[128,2048]{1,0:T(8,128)(2,1)S(1)}, bf16[128,2048]{1,0:T(8,128)(2,1)S(1)}, u32[]{:S(2)}, u32[]{:S(2)}) collective-permute-start(bf16[128,2048]{1,0:T(8,128)(2,1)S(1)} %add_convert_fusion.6), channel_id=1, source_target_pairs={{0,8},{8,16},{16,24},{24,0},{1,9},{9,17},{17,25},{25,1},{2,10},{10... | collective-permute-start | bytes 1572872 | tf_op jit(solution)/shard_map/ppermute | solution.py:66
  620.3 21.4 %collective-permute-start.12 = (bf16[128,2048]{1,0:T(8,128)(2,1)}, bf16[128,2048]{1,0:T(8,128)(2,1)}, u32[]{:S(2)}, u32[]{:S(2)}) collective-permute-start(bf16[128,2048]{1,0:T(8,128)(2,1)} %fusion.43), channel_id=1, source_target_pairs={{0,8},{8,16},{16,24},{24,0},{1,9},{9,17},{17,25},{25,1},{2,10},{10... | collective-permute-start | bytes 1572872 | tf_op jit(solution)/shard_map/ppermute | solution.py:66
  631.0 16.9 %collective-permute-start.15 = (bf16[128,2048]{1,0:T(8,128)(2,1)}, bf16[128,2048]{1,0:T(8,128)(2,1)}, u32[]{:S(2)}, u32[]{:S(2)}) collective-permute-start(bf16[128,2048]{1,0:T(8,128)(2,1)} %collective-permute-done.13), channel_id=1, source_target_pairs={{0,8},{8,16},{16,24},{24,0},{1,9},{9,17},{17,25},{25,1},{2,10},{10... | collective-permute-start | bytes 1572872 | tf_op jit(solution)/shard_map/ppermute | solution.py:59
  646.9 16.2 %collective-permute-start.14 = (bf16[128,2048]{1,0:T(8,128)(2,1)}, bf16[128,2048]{1,0:T(8,128)(2,1)}, u32[]{:S(2)}, u32[]{:S(2)}) collective-permute-start(bf16[128,2048]{1,0:T(8,128)(2,1)} %add_convert_fusion.3), channel_id=1, source_target_pairs={{0,8},{8,16},{16,24},{24,0},{1,9},{9,17},{17,25},{25,1},{2,10},{10... | collective-permute-start | bytes 1572872 | tf_op jit(solution)/shard_map/ppermute | solution.py:66
  849.4 15.8 %all-to-all-start.8 = ((bf16[4,3,4,128,128]{4,3,2,1,0:T(8,128)(2,1)}), bf16[4,3,4,128,128]{4,3,2,1,0:T(8,128)(2,1)S(1)}, u32[]{:S(2)}, u32[]{:S(2)}) async-start(bf16[4,3,4,128,128]{4,3,2,1,0:T(8,128)(2,1)} %copy.241), calls=%async_computation.8 | async-start | bytes 3145728 | tf_op jit(solution)/shard_map/all_to_all | solution.py:188
  853.0 191.1 %all-reduce.3.cloned.1.call-start = ((), (), s32[]{:S(2)}) async-start(), calls=%async_computation.23 | async-start | bytes 16777216
  916.6 203.5 %reduce-scatter.8.cloned.1.call-start = ((), (), s32[]{:S(2)}) async-start(), calls=%async_computation.21 | async-start | bytes 9437184 | tf_op jit(solution)/shard_map/reduce_scatter | solution.py:266
  951.2 288.5 %reduce-scatter.6.cloned.1.call-start = ((), (), s32[]{:S(2)}) async-start(), calls=%async_computation.20 | async-start | bytes 18874368 | tf_op jit(solution)/shard_map/reduce_scatter | solution.py:266
  1047.2 75.2 %all-to-all-start.9 = ((bf16[4,16,16,512]{3,2,1,0:T(8,128)(2,1)}), bf16[4,16,16,512]{3,2,1,0:T(8,128)(2,1)S(1)}, u32[]{:S(2)}, u32[]{:S(2)}) async-start(bf16[4,16,16,512]{3,2,1,0:T(8,128)(2,1)} %copy.255), calls=%async_computation.9 | async-start | bytes 2097152 | tf_op jit(solution)/shard_map/all_to_all | solution.py:268
  1122.4 120.5 %all-to-all-start.11 = ((bf16[4,16,16,512]{3,2,1,0:T(8,128)(2,1)}), bf16[4,16,16,512]{3,2,1,0:T(8,128)(2,1)S(1)}, u32[]{:S(2)}, u32[]{:S(2)}) async-start(bf16[4,16,16,512]{3,2,1,0:T(8,128)(2,1)} %bitcast.455), calls=%async_computation.13 | async-start | bytes 2097152 | tf_op jit(solution)/shard_map/all_to_all | solution.py:268
  1243.9 53.0 %all-to-all-start.10 = ((bf16[4,32,16,512]{3,2,1,0:T(8,128)(2,1)}), bf16[4,32,16,512]{3,2,1,0:T(8,128)(2,1)S(1)}, u32[]{:S(2)}, u32[]{:S(2)}) async-start(bf16[4,32,16,512]{3,2,1,0:T(8,128)(2,1)} %bitcast.453), calls=%async_computation.11 | async-start | bytes 4194304 | tf_op jit(solution)/shard_map/all_to_all | solution.py:268
  1312.6 142.8 %all-to-all-start.12 = ((bf16[256,16,512]{2,1,0:T(8,128)(2,1)}), bf16[256,16,512]{2,1,0:T(8,128)(2,1)}, u32[]{:S(2)}, u32[]{:S(2)}) async-start(bf16[256,16,512]{2,1,0:T(8,128)(2,1)} %broadcast_select_fusion), calls=%async_computation.14 | async-start | bytes 8388608 | tf_op jit(solution)/shard_map/all_to_all | solution.py:377
  1328.1 74.2 %collective-permute-start.22 = (bf16[128,2048]{1,0:T(8,128)(2,1)S(1)}, bf16[128,2048]{1,0:T(8,128)(2,1)S(1)}, u32[]{:S(2)}, u32[]{:S(2)}) collective-permute-start(bf16[128,2048]{1,0:T(8,128)(2,1)S(1)} %fusion.44), channel_id=1, source_target_pairs={{0,8},{8,16},{16,24},{24,0},{1,9},{9,17},{17,25},{25,1},{2,10},{10... | collective-permute-start | bytes 1572872 | tf_op jit(solution)/shard_map/ppermute | solution.py:66
  1403.9 32.2 %collective-permute-start.23 = (bf16[128,2048]{1,0:T(8,128)(2,1)}, bf16[128,2048]{1,0:T(8,128)(2,1)}, u32[]{:S(2)}, u32[]{:S(2)}) collective-permute-start(bf16[128,2048]{1,0:T(8,128)(2,1)} %add_convert_fusion.1), channel_id=1, source_target_pairs={{0,8},{8,16},{16,24},{24,0},{1,9},{9,17},{17,25},{25,1},{2,10},{10... | collective-permute-start | bytes 1572872 | tf_op jit(solution)/shard_map/ppermute | solution.py:66
  1438.1 16.2 %collective-permute-start.24 = (bf16[128,2048]{1,0:T(8,128)(2,1)}, bf16[128,2048]{1,0:T(8,128)(2,1)S(1)}, u32[]{:S(2)}, u32[]{:S(2)}) collective-permute-start(bf16[128,2048]{1,0:T(8,128)(2,1)} %add_convert_fusion), channel_id=1, source_target_pairs={{0,8},{8,16},{16,24},{24,0},{1,9},{9,17},{17,25},{25,1},{2,10},{10... | collective-permute-start | bytes 1572872 | tf_op jit(solution)/shard_map/ppermute | solution.py:67
  (149 other events, 1430.1 us)
Sparse Core Ops, SparseCore 0:
  148.1 53.1 all-gather.5
  202.9 68.6 all-gather.11
  274.0 70.1 all-gather.9
  346.5 94.6 all-gather.7
  916.7 127.3 all-reduce.2
  1048.4 71.6 reduce-scatter.7
  1123.7 115.9 reduce-scatter.5

commit v2 on v1

v2 whole, which is shorter than its diff:
```python
import functools

import jax
import jax.numpy as jnp
from jax import lax
from jax.experimental import pallas as pl
from jax.experimental.pallas import tpu as pltpu
from jax.sharding import Mesh
from jax.sharding import PartitionSpec as P

FF = 8192
HEADS = 16
SEGMAX = 1024
QB = 256
Z = 4

epsilon = 1e-06
rope_base = 500000.0
decay_rate = 0.5
step_rate = 0.5
gain_rate = 0.3
bf16 = jnp.bfloat16
f32 = jnp.float32
EVERY = ("hz", "hp", "seq")
GROUP = ("hz", "hp")
VMEM_LIMIT = 48 * 1024 * 1024


def mm(left_side, right_side):
    return jnp.dot(left_side, right_side, preferred_element_type=f32)


def mm_nt(left_side, right_side):
    return lax.dot_general(
        left_side, right_side, (((1,), (1,)), ((), ())), preferred_element_type=f32
    )


def mm_tn(left_side, right_side):
    return lax.dot_general(
        left_side, right_side, (((0,), (0,)), ((), ())), preferred_element_type=f32
    )


def params():
    return pltpu.CompilerParams(vmem_limit_bytes=VMEM_LIMIT)


def cost(flops, nbytes, exps=0):
    return pl.CostEstimate(flops=int(flops), bytes_accessed=int(nbytes), transcendentals=int(exps))


def nbytes(*arrays):
    return sum(a.size * a.dtype.itemsize for a in arrays)


def gate_up_kernel(x_ref, g_ref, u_ref, gate_ref, up_ref, hidden_ref):
    side = g_ref.shape[-1]
    for w_ref, y_ref in ((g_ref, gate_ref), (u_ref, up_ref)):
        total = None
        for r in range(w_ref.shape[1]):
            part = mm(x_ref[:, r * side : (r + 1) * side], w_ref[:, r, 0].reshape(side, side))
            total = part if total is None else total + part
        y_ref[...] = total
    gate = gate_ref[...]
    hidden_ref[...] = (gate * jax.nn.sigmoid(gate) * up_ref[...]).astype(bf16)


def gate_up(x, w):
    rep, R, C, part, side = w.shape
    count, half = x.shape[0], C // 2
    wide = jax.ShapeDtypeStruct((count, half * side), f32)
    outs = [wide, wide, jax.ShapeDtypeStruct((count, half * side), bf16)]
    col = pl.BlockSpec((count, side), lambda c: (0, c))
    return pl.pallas_call(
        gate_up_kernel,
        grid=(half,),
        in_specs=[
            pl.BlockSpec(x.shape, lambda c: (0, 0)),
            pl.BlockSpec((rep, R, 1, part, side), lambda c: (0, 0, c, 0, 0)),
            pl.BlockSpec((rep, R, 1, part, side), lambda c: (0, 0, c + half, 0, 0)),
        ],
        out_specs=[col, col, col],
        out_shape=outs,
        compiler_params=params(),
        cost_estimate=cost(2 * count * R * C * side * side, nbytes(x, w, *outs)),
    )(x, w, w)


def nn_kernel(x_ref, w_ref, y_ref):
    side = w_ref.shape[-1]
    total = None
    for r in range(w_ref.shape[1]):
        part = mm(x_ref[:, r * side : (r + 1) * side], w_ref[:, r, 0].reshape(side, side))
        total = part if total is None else total + part
    y_ref[...] = total


def nn(x, w):
    rep, R, C, part, side = w.shape
    count = x.shape[0]
    out = jax.ShapeDtypeStruct((count, C * side), f32)
    return pl.pallas_call(
        nn_kernel,
        grid=(C,),
        in_specs=[
            pl.BlockSpec(x.shape, lambda c: (0, 0)),
            pl.BlockSpec((rep, R, 1, part, side), lambda c: (0, 0, c, 0, 0)),
        ],
        out_specs=pl.BlockSpec((count, side), lambda c: (0, c)),
        out_shape=out,
        compiler_params=params(),
        cost_estimate=cost(2 * count * R * C * side * side, nbytes(x, w, out)),
    )(x, w)


def hidden_back_kernel(x_ref, w_ref, gate_ref, up_ref, y_ref):
    side = w_ref.shape[-1]
    total = None
    for c in range(w_ref.shape[2]):
        part = mm_nt(x_ref[:, c * side : (c + 1) * side], w_ref[:, 0, c].reshape(side, side))
        total = part if total is None else total + part
    gate = gate_ref[...]
    sigma = jax.nn.sigmoid(gate)
    y_ref[0] = (total * up_ref[...] * sigma * (1.0 + gate * (1.0 - sigma))).astype(bf16)
    y_ref[1] = (total * gate * sigma).astype(bf16)


def hidden_back(x, w, gate, up):
    rep, R, C, part, side = w.shape
    count = x.shape[0]
    out = jax.ShapeDtypeStruct((2, count, R * side), bf16)
    col = pl.BlockSpec((count, side), lambda r: (0, r))
    return pl.pallas_call(
        hidden_back_kernel,
        grid=(R,),
        in_specs=[
            pl.BlockSpec(x.shape, lambda r: (0, 0)),
            pl.BlockSpec((rep, 1, C, part, side), lambda r: (0, r, 0, 0, 0)),
            col,
            col,
        ],
        out_specs=pl.BlockSpec((2, count, side), lambda r: (0, 0, r)),
        out_shape=out,
        compiler_params=params(),
        cost_estimate=cost(2 * count * R * C * side * side, nbytes(x, w, gate, up, out)),
    )(x, w, gate, up)


def nt_kernel(x_ref, w_ref, y_ref):
    side = w_ref.shape[-1]
    per = x_ref.shape[2] // side
    total = None
    for c in range(w_ref.shape[2]):
        x = x_ref[c // per, :, (c % per) * side : (c % per + 1) * side]
        part = mm_nt(x, w_ref[:, 0, c].reshape(side, side))
        total = part if total is None else total + part
    y_ref[...] = total


def nt(x, w):
    rep, R, C, part, side = w.shape
    count = x.shape[1]
    out = jax.ShapeDtypeStruct((count, R * side), f32)
    return pl.pallas_call(
        nt_kernel,
        grid=(R,),
        in_specs=[
            pl.BlockSpec(x.shape, lambda r: (0, 0, 0)),
            pl.BlockSpec((rep, 1, C, part, side), lambda r: (0, r, 0, 0, 0)),
        ],
        out_specs=pl.BlockSpec((count, side), lambda r: (0, r)),
        out_shape=out,
        compiler_params=params(),
        cost_estimate=cost(2 * count * R * C * side * side, nbytes(x, w, out)),
    )(x, w)


def tn_kernel(*refs):
    y_ref, half = refs[-1], (len(refs) - 1) // 2
    rep, _, _, part, side = y_ref.shape
    left = jnp.concatenate([r[...] for r in refs[:half]], axis=0)
    right = jnp.concatenate([r[0] for r in refs[half:-1]], axis=0)
    y_ref[:, 0, 0] = mm_tn(left, right).astype(bf16).reshape(rep, part, side)


def tn(lefts, rights, rep, side):
    count = lefts[0].shape[0]
    R = lefts[0].shape[1] // side
    m, per = rights[0].shape[0], rights[0].shape[2] // side
    C = m * per
    out = jax.ShapeDtypeStruct((rep, R, C, side // rep, side), bf16)
    left_spec = pl.BlockSpec((count, side), lambda r, c: (0, r))
    right_spec = pl.BlockSpec((1, count, side), lambda r, c: (c // per, 0, c % per))
    total = count * len(lefts)
    return pl.pallas_call(
        tn_kernel,
        grid=(R, C),
        in_specs=[left_spec] * len(lefts) + [right_spec] * len(rights),
        out_specs=pl.BlockSpec((rep, 1, 1, side // rep, side), lambda r, c: (0, r, c, 0, 0)),
        out_shape=out,
        compiler_params=params(),
        cost_estimate=cost(2 * total * R * C * side * side, nbytes(*lefts, *rights, out)),
    )(*lefts, *rights)


def scores_of(q, k, begin, q_start, k_start, scale):
    scores = mm_nt(k, q) * scale
    key_place = k_start + lax.broadcasted_iota(jnp.int32, scores.shape, 0)
    query_place = q_start + lax.broadcasted_iota(jnp.int32, scores.shape, 1)
    return jnp.where((key_place >= begin) & (key_place <= query_place), scores, -1e30)


def window_start(i, block, window, length):
    start = jnp.clip(i * block + block - window, 0, length - window)
    return pl.multiple_of(start, 128)


def attend_kernel(scale, window, q_ref, k_ref, v_ref, b_ref, o_ref, lse_ref):
    block, length = q_ref.shape[0], k_ref.shape[0]
    i = pl.program_id(0)
    start = window_start(i, block, window, length)
    scores = scores_of(
        q_ref[...], k_ref[pl.ds(start, window), :], b_ref[...], i * block, start, scale
    )
    top = jnp.max(scores, axis=0, keepdims=True)
    expo = jnp.exp(scores - top)
    total = jnp.sum(expo, axis=0, keepdims=True)
    attention = (expo * (1.0 / total)).astype(bf16)
    o_ref[...] = mm_tn(attention, v_ref[pl.ds(start, window), :]).astype(bf16)
    lse_ref[...] = top + jnp.log(total)


def attend(q, k, v, begins, scale):
    length, width = q.shape
    window = min(QB + SEGMAX, length)
    full = pl.BlockSpec((length, width), lambda i: (0, 0))
    rows = pl.BlockSpec((QB, width), lambda i: (i, 0))
    line = pl.BlockSpec((1, QB), lambda i: (0, i))
    return pl.pallas_call(
        functools.partial(attend_kernel, scale, window),
        grid=(length // QB,),
        in_specs=[rows, full, full, line],
        out_specs=[rows, line],
        out_shape=[
            jax.ShapeDtypeStruct((length, width), bf16),
            jax.ShapeDtypeStruct((1, length), f32),
        ],
        compiler_params=params(),
        cost_estimate=cost(4 * length * window * width, 4 * nbytes(q), length * window),
    )(q, k, v, begins)


def attend_back_kernel(
    scale, window, q_ref, d_ref, k_ref, v_ref, b_ref, lse_ref, dq_ref, dk_ref, dv_ref, ka, va
):
    block, length = q_ref.shape[0], k_ref.shape[0]
    i = pl.program_id(0)
    start = window_start(i, block, window, length)
    span = pl.ds(start, window)

    @pl.when(i == 0)
    def _():
        ka[...] = jnp.zeros_like(ka)
        va[...] = jnp.zeros_like(va)

    q, d, k = q_ref[...], d_ref[...], k_ref[span, :]
    scores = scores_of(q, k, b_ref[...], i * block, start, scale)
    attention = jnp.exp(scores - lse_ref[...])
    prob_grad = mm_nt(v_ref[span, :], d)
    center = jnp.sum(attention * prob_grad, axis=0, keepdims=True)
    score_grad = (attention * (prob_grad - center)).astype(bf16)
    dq_ref[...] = (mm_tn(score_grad, k) * scale).astype(bf16)
    ka[span, :] += mm(score_grad, q) * scale
    va[span, :] += mm(attention.astype(bf16), d)

    @pl.when(i == pl.num_programs(0) - 1)
    def _():
        dk_ref[...] = ka[...].astype(bf16)
        dv_ref[...] = va[...].astype(bf16)


def attend_back(q, d, k, v, begins, lse, scale):
    length, width = q.shape
    window = min(QB + SEGMAX, length)
    full = pl.BlockSpec((length, width), lambda i: (0, 0))
    rows = pl.BlockSpec((QB, width), lambda i: (i, 0))
    line = pl.BlockSpec((1, QB), lambda i: (0, i))
    return pl.pallas_call(
        functools.partial(attend_back_kernel, scale, window),
        grid=(length // QB,),
        in_specs=[rows, rows, full, full, line, line],
        out_specs=[rows, full, full],
        out_shape=[jax.ShapeDtypeStruct((length, width), bf16)] * 3,
        scratch_shapes=[pltpu.VMEM((length, width), f32)] * 2,
        compiler_params=params(),
        cost_estimate=cost(10 * length * window * width, 8 * nbytes(q), length * window),
    )(q, d, k, v, begins, lse)


def shampoo_kernel(g_ref, ls_ref, rs_ref, lr_ref, rr_ref, w_ref, go_ref, lo_ref, ro_ref, wo_ref):
    g = g_ref[0]
    go_ref[0] = g.astype(f32)
    lo_ref[0] = decay_rate * ls_ref[0] + (1.0 - decay_rate) * mm_nt(g, g)
    ro_ref[0] = decay_rate * rs_ref[0] + (1.0 - decay_rate) * mm_tn(g, g)
    middle = mm(lr_ref[0].astype(bf16), g).astype(bf16)
    wo_ref[0] = w_ref[0] - step_rate * mm(middle, rr_ref[0].astype(bf16))


def shampoo(g, *rest):
    slots, side, _ = g.shape
    spec = pl.BlockSpec((1, side, side), lambda s: (s, 0, 0))
    return pl.pallas_call(
        shampoo_kernel,
        grid=(slots,),
        in_specs=[spec] * 6,
        out_specs=[spec] * 4,
        out_shape=[jax.ShapeDtypeStruct(g.shape, f32)] * 4,
        compiler_params=params(),
        cost_estimate=cost(8 * slots * side**3, 38 * g.size),
    )(g, *rest)


def rms_norm(values, gain_vec):
    return (
        values * lax.rsqrt(jnp.mean(values * values, axis=-1, keepdims=True) + epsilon) * gain_vec
    )


def begins_of(segment_row):
    length = segment_row.shape[0]
    indices = jnp.arange(length, dtype=jnp.int32)
    earlier = jnp.concatenate([jnp.full((1,), -1, jnp.int32), segment_row[:-1]])
    return lax.cummax(jnp.where(segment_row != earlier, indices, 0), axis=0)


UP = [(i, (i + 1) % Z) for i in range(Z)]


def ring_gather(block):
    blocks = [block]
    for _ in range(Z - 1):
        blocks.append(lax.ppermute(blocks[-1], "hz", UP))
    return blocks


def ring_scatter(part_of):
    total = part_of(1).astype(bf16)
    for k in (2, 3):
        total = (lax.ppermute(total, "hz", UP).astype(f32) + part_of(k)).astype(bf16)
    return lax.ppermute(total, "hz", UP).astype(f32) + part_of(0)


def sum_group(values):
    size = lax.axis_size(GROUP)
    spread = jnp.broadcast_to(values, (size,) + values.shape)
    return jnp.sum(lax.all_to_all(spread, GROUP, 0, 0, tiled=True), axis=0)


def sum_seq_scatter(values):
    S = lax.axis_size("seq")
    if S != 2:
        return lax.psum_scatter(values, "seq", scatter_dimension=0, tiled=False)
    c = lax.axis_index("seq")
    mine = lax.dynamic_index_in_dim(values, c, 0, keepdims=False)
    other = lax.dynamic_index_in_dim(values, 1 - c, 0, keepdims=False)
    got = lax.ppermute(other, "seq", [(0, 1), (1, 0)])
    return (mine.astype(f32) + got.astype(f32)).astype(bf16)


def body(
    tokens,
    cotangent,
    segment_ids,
    owner_map,
    weights,
    norm_gains,
    left_stats,
    right_stats,
    left_root,
    right_root,
):
    model_width = tokens.shape[2]
    local_count = tokens.shape[1]
    slots, side = weights.shape[0], weights.shape[1]
    total_blocks = owner_map.shape[0]
    PN, S = lax.axis_size("hp"), lax.axis_size("seq")
    n = Z * PN * S
    rep = PN * S
    rows = side // n
    part = Z * rows
    head_size = model_width // HEADS
    quarter = model_width // Z
    score_scale = head_size ** (-0.5)
    zi, pi = lax.axis_index("hz"), lax.axis_index("hp")
    head = zi * PN + pi
    relative = (zi - jnp.arange(Z, dtype=jnp.int32)) % Z
    inputs = tokens[0]

    D, F = model_width // side, FF // side
    number = jnp.arange(total_blocks, dtype=jnp.int32)
    square, tall = D * D, D * F
    qkv_number = number[: 3 * square].reshape(3, D, Z, D // Z)
    qkv_list = qkv_number.transpose(2, 1, 0, 3).reshape(Z, -1)
    out_list = number[3 * square : 4 * square]
    gateup_list = number[4 * square : 4 * square + 2 * tall].reshape(2, D, Z, F // Z)
    gateup_list = gateup_list.transpose(2, 1, 0, 3).reshape(Z, -1)
    down_list = number[4 * square + 2 * tall :].reshape(Z, -1)
    inverse = jnp.zeros((total_blocks,), jnp.int32).at[owner_map].set(number)

    low = weights.astype(bf16).reshape(slots, PN, S, Z, rows, side)
    low = low.transpose(3, 1, 2, 0, 4, 5).reshape(n * slots, rows, side)
    spread = lax.all_to_all(low, EVERY, 0, 0, tiled=True)

    def pick(numbers):
        return jnp.take(spread, inverse[numbers], axis=0)

    heads_send = pick(number[: 3 * square]).reshape(3, D, Z, rows, PN, head_size)
    heads_send = heads_send.transpose(2, 4, 0, 1, 3, 5)[:, :, None]
    heads_send = jnp.broadcast_to(heads_send, (Z, PN, S, 3, D, rows, head_size))
    heads_got = lax.all_to_all(
        heads_send.reshape(n, 3, D, rows, head_size), EVERY, 0, 0, tiled=True
    ).reshape(Z, PN, S, 3, D, rows, head_size)
    w_heads = heads_got.transpose(4, 1, 2, 0, 5, 3, 6).reshape(model_width, 3 * head_size)

    out_all = lax.all_gather(pick(out_list), EVERY, axis=0, tiled=False)
    out_all = out_all.reshape(Z, PN, S, D, D, rows, side)
    w_output = out_all.transpose(3, 1, 2, 0, 5, 4, 6).reshape(model_width, model_width)

    def fetch(numbers, R):
        got = lax.all_to_all(pick(numbers.reshape(-1)), "hz", 0, 0, tiled=True)
        got = got.reshape(Z, R, -1, rows, side).transpose(1, 2, 0, 3, 4)
        return lax.all_gather(
            got.reshape(R, -1, part, side), ("hp", "seq"), axis=0, tiled=False
        )

    w_gateup = fetch(gateup_list, D)
    w_down = fetch(down_list, F // Z)
    w_qkv = fetch(qkv_list, D)

    group = Z * PN
    row_ids = lax.all_to_all(
        jnp.broadcast_to(segment_ids, (group, local_count)), GROUP, 0, 0, tiled=True
    ).reshape(-1)
    length = row_ids.shape[0]
    tokens_row = lax.all_gather(inputs, GROUP, axis=0, tiled=True)
    begins = begins_of(row_ids)
    places = jnp.arange(length, dtype=jnp.int32) - begins
    half_size = head_size // 2
    frequency = rope_base ** (-2.0 * jnp.arange(half_size, dtype=f32) / head_size)
    angles = places.astype(f32)[:, None] * frequency[None, :]
    cosine, sine = jnp.cos(angles), jnp.sin(angles)

    def rope(values, sign):
        first, second = values[:, :half_size], values[:, half_size:]
        return jnp.concatenate(
            [first * cosine - second * sine * sign, second * cosine + first * sine * sign], axis=-1
        )

    gains_head = lax.dynamic_slice_in_dim(norm_gains[2:4], head * head_size, head_size, axis=1)

    raw = mm(tokens_row, w_heads)
    query_raw, key_raw = raw[:, :head_size], raw[:, head_size : 2 * head_size]
    value_row = raw[:, 2 * head_size :].astype(bf16)
    squares = jnp.stack([jnp.sum(query_raw * query_raw, -1), jnp.sum(key_raw * key_raw, -1)])
    invs = lax.rsqrt(sum_group(squares) / model_width + epsilon)
    query_hat, key_hat = query_raw * invs[0][:, None], key_raw * invs[1][:, None]
    query_row = rope(query_hat * gains_head[0], 1.0).astype(bf16)
    key_row = rope(key_hat * gains_head[1], 1.0).astype(bf16)

    begin_line = begins[None, :]
    mixed, log_sums = attend(query_row, key_row, value_row, begin_line, score_scale)
    attended = lax.all_to_all(
        mixed.reshape(group, local_count, head_size), GROUP, 0, 0, tiled=True
    )
    attended = attended.transpose(1, 0, 2).reshape(local_count, model_width)
    attn_raw = mm(attended, w_output)
    resid = inputs.astype(f32) + rms_norm(attn_raw, norm_gains[0])

    resid_blocks = ring_gather(resid.astype(bf16))
    gates, ups, hiddens = zip(*[gate_up(b, w_gateup) for b in resid_blocks])
    down_raw = ring_scatter(lambda k: nn(hiddens[k], w_down))
    output = (resid + rms_norm(down_raw, norm_gains[1])).astype(bf16)[None]

    upstream = cotangent[0].astype(f32)
    _, down_norm_back = jax.vjp(rms_norm, down_raw, norm_gains[1])
    down_grad, gain_mlp_grad = down_norm_back(upstream)
    down_blocks = ring_gather(down_grad.astype(bf16))
    gateup_grads = [
        hidden_back(b, w_down, gate, up) for b, gate, up in zip(down_blocks, gates, ups)
    ]
    resid_grad = upstream + ring_scatter(lambda k: nt(gateup_grads[k], w_gateup))

    def send_grads(pieces):
        pieces = pieces.reshape(rep, -1, part, side)
        summed = lax.psum_scatter(pieces, ("hp", "seq"), scatter_dimension=0, tiled=True)
        summed = summed.reshape(-1, Z, rows, side).transpose(1, 0, 2, 3)
        return lax.all_to_all(summed, "hz", 0, 0, tiled=True)

    down_sent = send_grads(tn(hiddens, [b[None] for b in down_blocks], rep, side))
    gateup_sent = send_grads(tn(resid_blocks, gateup_grads, rep, side))

    _, attn_norm_back = jax.vjp(rms_norm, attn_raw, norm_gains[0])
    attn_grad, gain_attn_grad = attn_norm_back(resid_grad)
    attn_low = attn_grad.astype(bf16)
    attended_grad = mm_nt(attn_low, w_output).astype(bf16)
    grad_row = lax.all_to_all(
        attended_grad.reshape(local_count, group, head_size).transpose(1, 0, 2),
        GROUP,
        0,
        0,
        tiled=True,
    ).reshape(length, head_size)

    def to_groups(stack):
        m = stack.shape[0]
        shaped = stack.reshape(m, Z, PN, local_count, head_size).transpose(2, 0, 1, 3, 4)
        got = lax.all_to_all(shaped, "hp", 0, 0, tiled=True)
        got = jnp.take(got, relative, axis=2)
        return got.transpose(2, 1, 3, 0, 4).reshape(Z, m, local_count, quarter)

    attended_rel = to_groups(mixed[None])
    attn_blocks = ring_gather(attn_low)
    out_sent = send_grads(
        tn([attended_rel[k, 0] for k in range(Z)], [b[None] for b in attn_blocks], rep, side)
    )

    query_grad, key_grad, value_grad = attend_back(
        query_row, grad_row, key_row, value_row, begin_line, log_sums, score_scale
    )
    query_turn, key_turn = rope(query_grad.astype(f32), -1.0), rope(key_grad.astype(f32), -1.0)
    gain_query = jnp.sum(query_turn * query_hat, axis=0)
    gain_key = jnp.sum(key_turn * key_hat, axis=0)
    query_turn, key_turn = query_turn * gains_head[0], key_turn * gains_head[1]
    dots = sum_group(
        jnp.stack([jnp.sum(query_turn * query_hat, -1), jnp.sum(key_turn * key_hat, -1)])
    )
    dots = dots / model_width
    query_back = ((query_turn - query_hat * dots[0][:, None]) * invs[0][:, None]).astype(bf16)
    key_back = ((key_turn - key_hat * dots[1][:, None]) * invs[1][:, None]).astype(bf16)

    back_rel = to_groups(jnp.stack([query_back, key_back, value_grad]))
    input_grad = resid_grad + ring_scatter(lambda k: nt(back_rel[k], w_qkv))

    back_row = jnp.concatenate([query_back, key_back, value_grad], axis=1)
    heads_grad = mm_tn(tokens_row, back_row).astype(bf16)
    heads_grad = heads_grad.reshape(D, PN, S, Z, rows, 3, head_size).transpose(2, 3, 1, 5, 0, 4, 6)
    heads_sum = sum_seq_scatter(heads_grad)
    heads_sent = lax.all_to_all(
        heads_sum.reshape(group, 3, D, rows, head_size), GROUP, 0, 0, tiled=True
    ).reshape(Z, PN, 3, D, rows, head_size)
    heads_sent = heads_sent.transpose(2, 3, 0, 4, 1, 5).reshape(3 * square, rows, side)

    spots = jnp.zeros((2, model_width), f32)
    spots = lax.dynamic_update_slice(spots, jnp.stack([gain_query, gain_key]), (0, head * head_size))
    gain_local = jnp.concatenate([jnp.stack([gain_attn_grad, gain_mlp_grad]), spots])
    shares = lax.all_to_all(gain_local.reshape(n, -1), EVERY, 0, 0, tiled=True)
    share = jnp.sum(shares, axis=0)
    gain_grads = lax.all_to_all(
        jnp.broadcast_to(share, (n, share.shape[0])), EVERY, 0, 0, tiled=True
    ).reshape(gain_local.shape)

    flat = [a.reshape(-1, rows, side) for a in (heads_sent, out_sent, gateup_sent, down_sent)]
    sent = jnp.concatenate(flat, axis=0)
    order = [number[: 3 * square], out_list, gateup_list.reshape(-1), down_list.reshape(-1)]
    where_is = jnp.zeros((total_blocks,), jnp.int32).at[jnp.concatenate(order)].set(number)
    to_slots = jnp.take(sent, where_is[owner_map], axis=0)
    got = lax.all_to_all(to_slots, EVERY, 0, 0, tiled=True)
    got = got.reshape(Z, PN, S, slots, rows, side).transpose(3, 1, 2, 0, 4, 5)
    grad_slots, left_new, right_new, new_weights = shampoo(
        got.reshape(slots, side, side), left_stats, right_stats, left_root, right_root, weights
    )
    new_gains = norm_gains - gain_rate * gain_grads * lax.rsqrt(
        jnp.mean(gain_grads * gain_grads, axis=1, keepdims=True) + epsilon
    )
    return (
        output,
        input_grad[None],
        grad_slots,
        left_new,
        right_new,
        new_weights,
        gain_grads,
        new_gains,
    )


def solution(mesh):
    heads, seqs = mesh.shape["head"], mesh.shape["seq"]
    fine = Mesh(mesh.devices.reshape(Z, heads // Z, seqs), EVERY)
    tok = P("seq", GROUP, None)
    slot = P(EVERY, None, None)
    return jax.shard_map(
        body,
        mesh=fine,
        in_specs=(tok, tok, P("seq", GROUP), P(), slot, P(), slot, slot, slot, slot),
        out_specs=(tok, tok, slot, slot, slot, slot, P(), P()),
        check_vma=False,
    )
```

time: 1510 us -> 1180 us (0.78)
  Pallas kernels: 0 us -> 223 us
  local copies, waits for them, and re-layouts: 320 us -> 115 us
  matrix products: 231 us -> 27.7 us
  waiting for transfers between devices: 609 us -> 522 us
  blocking collectives: 139 us -> 106 us
  other arithmetic: 71.9 us -> 49.2 us
  loops' own time: 21.3 us -> 0 us
  starting transfers between devices: 92.4 us -> 109 us
    pallas_call x0 -> x26, Pallas kernels: none -> 223 us  [the longest x8 57 us: nt(): pl.pallas_call(nt_kernel, grid=(R,), in_specs=[pl.BlockSpec(x.shape, lamb...]
    reduce_scatter x2 -> x3, waiting for transfers between devices: 181 us -> 52.8 us  [send_grads(): lax.psum_scatter(pieces, ('hp', 'seq'), scatter_dimension=0, tiled=True)]
    reshape x18 -> x9, local copies, waits for them, and re-layouts: 115 us -> 20.6 us  [the longest x1 11.1 us: body(): out_all = out_all.reshape(Z, PN, S, D, D, rows, side)]
    dot_general x31 -> x0, matrix products: 85.3 us -> none  [the longest x3 30.6 us: batched(): return jnp.einsum(form, left_side, right_side, preferred_element_type=f32)]
    all_to_all x1, waiting for transfers between devices: 90.4 us -> 162 us  [body(): spread = lax.all_to_all(low, EVERY, 0, 0, tiled=True)]
    dot_general x25 -> x1, matrix products: 67.1 us -> 7.85 us  [mm_nt(): lax.dot_general(left_side, right_side, (((1,), (1,)), ((), ())), preferre...]
    all_to_all x3 -> x8, waiting for transfers between devices: 41.5 us -> 83.3 us  [the longest x1 37.8 us: body(): lax.all_to_all(heads_send.reshape(n, 3, D, rows, head_size), EVERY, 0, 0,...]
    ppermute x8 -> x6, waiting for transfers between devices: 114 us -> 74.2 us  [ring_scatter(): lax.ppermute(total, 'hz', UP).astype(f32) + part_of(k)]
  transfers between devices with their start and end apart: 44 -> 44, of which waited for: 29 -> 26; matrix products, arithmetic and copies ran while one was open for 27% -> 14% of each run, Pallas kernels for 0% -> 16%
where the time goes in v2:
time: 1180 us; the launch traced here: 1170 us
  waiting for transfers between devices  522 us (44%)
  Pallas kernels  223 us (19%)
  local copies, waits for them, and re-layouts  115 us (10%)
  starting transfers between devices  109 us (9%)
  blocking collectives  106 us (9%)
  other arithmetic  49.2 us (4%)
  matrix products  27.7 us (2%)
  between operations  16.3 us (1%)
    all_to_all x1, waiting for transfers between devices, body(): spread = lax.all_to_all(low, EVERY, 0, 0, tiled=True)  162 us
    all_to_all x2, blocking collectives, fetch(): got = lax.all_to_all(pick(numbers.reshape(-1)), 'hz', 0, 0, tiled=True)  106 us
    ppermute x9, waiting for transfers between devices, ring_gather(): blocks.append(lax.ppermute(blocks[-1], 'hz', UP))  78.2 us
    ppermute x6, waiting for transfers between devices, ring_scatter(): lax.ppermute(total, 'hz', UP).astype(f32) + part_of(k)  74.2 us
    pallas_call x8, Pallas kernels, nt(): pl.pallas_call(nt_kernel, grid=(R,), in_specs=[pl.BlockSpec(x.shape, lamb...  57 us
    reduce_scatter x3, waiting for transfers between devices, send_grads(): lax.psum_scatter(pieces, ('hp', 'seq'), scatter_dimension=0, tiled=True)  52.8 us
    all_to_all x3, waiting for transfers between devices, send_grads(): return lax.all_to_all(summed, 'hz', 0, 0, tiled=True)  47.7 us
    pallas_call x3, Pallas kernels, tn(): pl.pallas_call(tn_kernel, grid=(R, C), in_specs=[left_spec] * len(lefts)...  42.6 us
  transfers between devices with their start and end apart: 44, of which 26 were waited for; matrix products, arithmetic and copies ran while one was open for 14% of the time, Pallas kernels for 16%

profile of v2, /device:TPU:0, one launch (start us, length us, event | category | flops | bytes accessed | tf_op | source)
XLA Modules:
  0.0 1169.9 jit_solution(2146141889803751955)
XLA Ops:
  24.0 161.6 %all-to-all-done = bf16[256,16,512]{2,1,0:T(8,128)(2,1)} async-done(((bf16[256,16,512]{2,1,0:T(8,128)(2,1)}), bf16[256,16,512]{2,1,0:T(8,128)(2,1)}, u32[]{:S(2)}, u32[]{:S(2)}) %all-to-all-start) | async-done | bytes 4194336 | tf_op jit(solution)/shard_map/all_to_all | solution.py:413
  194.7 68.0 %all_to_all.104 = bf16[128,16,512]{2,1,0:T(8,128)(2,1)S(1)} all-to-all(bf16[128,16,512]{2,1,0:T(8,128)(2,1)S(1)} %broadcast_select_fusion.1), channel_id=1, replica_groups=mesh['hz'=4,'hp'=4,'seq'=2] {'hz'}, dimensions={0} | all-to-all | bytes 4194304 | tf_op jit(solution)/shard_map/all_to_all | solution.py:431
  268.8 38.5 %all_to_all.105 = bf16[64,16,512]{2,1,0:T(8,128)(2,1)S(1)} all-to-all(bf16[64,16,512]{2,1,0:T(8,128)(2,1)S(1)} %broadcast_select_fusion.2), channel_id=1, replica_groups=mesh['hz'=4,'hp'=4,'seq'=2] {'hz'}, dimensions={0} | all-to-all | bytes 2097152 | tf_op jit(solution)/shard_map/all_to_all | solution.py:431
  318.0 37.8 %all-to-all-done.1 = bf16[32,3,4,16,128]{4,3,2,1,0:T(8,128)(2,1)S(1)} async-done(((bf16[32,3,4,16,128]{4,3,2,1,0:T(8,128)(2,1)}), bf16[32,3,4,16,128]{4,3,2,1,0:T(8,128)(2,1)S(1)}, u32[]{:S(2)}, u32[]{:S(2)}) %all-to-all-start.1) | async-done | bytes 1572896 | tf_op jit(solution)/shard_map/all_to_all | solution.py:421
  400.8 10.2 shard_map.164
  415.7 11.1 copy.221
  426.9 10.4 copy.256
  444.3 13.1 %collective-permute-done.x_ref.refs_1_ = bf16[128,2048]{1,0:T(8,128)(2,1)S(1)} collective-permute-done((bf16[128,2048]{1,0:T(8,128)(2,1)S(1)}, bf16[128,2048]{1,0:T(8,128)(2,1)S(1)}, u32[]{:S(2)}, u32[]{:S(2)}) %collective-permute-start) | collective-permute-done | bytes 524320 | tf_op jit(solution)/shard_map/ppermute | solution.py:343
  494.7 10.1 collective-permute-done.4.x_ref.refs_3_
  534.4 13.4 %collective-permute-done.6.x_ref = bf16[128,2048]{1,0:T(8,128)(2,1)S(1)} collective-permute-done((bf16[128,2048]{1,0:T(8,128)(2,1)S(1)}, bf16[128,2048]{1,0:T(8,128)(2,1)S(1)}, u32[]{:S(2)}, u32[]{:S(2)}) %collective-permute-start.6) | collective-permute-done | bytes 524320 | tf_op jit(solution)/shard_map/ppermute | solution.py:343
  571.9 9.1 shard_map.176
  597.5 9.5 shard_map.178
  613.2 9.5 shard_map.180
  624.1 15.0 %collective-permute-done.16 = bf16[128,2048]{1,0:T(8,128)(2,1)} collective-permute-done((bf16[128,2048]{1,0:T(8,128)(2,1)S(1)}, bf16[128,2048]{1,0:T(8,128)(2,1)}, u32[]{:S(2)}, u32[]{:S(2)}) %collective-permute-start.16) | collective-permute-done | bytes 524320 | tf_op jit(solution)/shard_map/ppermute | solution.py:343
  644.2 11.8 %collective-permute-done.17 = bf16[128,2048]{1,0:T(8,128)(2,1)} collective-permute-done((bf16[128,2048]{1,0:T(8,128)(2,1)}, bf16[128,2048]{1,0:T(8,128)(2,1)}, u32[]{:S(2)}, u32[]{:S(2)}) %collective-permute-start.17) | collective-permute-done | bytes 524320 | tf_op jit(solution)/shard_map/ppermute | solution.py:343
  680.6 11.3 shard_map.188
  696.3 26.7 %shard_map.187 = bf16[8,4,8,64,512]{4,3,2,1,0:T(8,128)(2,1)} custom-call(bf16[128,2048]{1,0:T(8,128)(2,1)S(1)} %fusion.62.x_ref.refs_0_, bf16[128,2048]{1,0:T(8,128)(2,1)S(1)} %copy-done.10, bf16[128,2048]{1,0:T(8,128)(2,1)S(1)} %copy-done.12, bf16[128,2048]{1,0:T(8,128)(2,1)S(1)} %copy-done.14, bf16[2,128,2048]{2,1,0:T(8,128)(2,1)S(1)} %copy-done.2, ...), custom_call_target="tpu_custom_call" | custom-call | flops 8589934592 | bytes 23068672 | tf_op jit(solution)/shard_map/pallas_call | solution.py:196
  746.2 11.7 %shard_map.181 = (bf16[2048,128]{1,0:T(8,128)(2,1)S(1)}, bf16[2048,128]{1,0:T(8,128)(2,1)S(1)}, bf16[2048,128]{1,0:T(8,128)(2,1)S(1)}) custom-call(bf16[2048,128]{1,0:T(8,128)(2,1)S(1)} %copy-done.32, bf16[2048,128]{1,0:T(8,128)(2,1)S(1)} %bitcast.237, bf16[2048,128]{1,0:T(8,128)(2,1)S(1)} %copy-done.34, bf16[2048,128]{1,0:T(8,128)(2,1)S(1)} %copy-done.30, ...), custom_call_target="tpu_custom_call" | custom-call | flops 3355443200 | bytes 4194304 | tf_op jit(solution)/shard_map/pallas_call | solution.py:289
  829.5 18.2 %all-to-all-done.11 = bf16[16,3,4,16,128]{4,3,2,1,0:T(8,128)(2,1)S(1)} async-done(((bf16[16,3,4,16,128]{4,3,2,1,0:T(8,128)(2,1)}), bf16[16,3,4,16,128]{4,3,2,1,0:T(8,128)(2,1)S(1)}, u32[]{:S(2)}, u32[]{:S(2)}) %all-to-all-start.11) | async-done | bytes 786464 | tf_op jit(solution)/shard_map/all_to_all | solution.py:549
  864.0 52.7 %reduce-scatter.6.cloned.1.call-done = bf16[1,32,64,512]{3,2,1,0:T(8,128)(2,1)} async-done(((bf16[8,32,64,512]{3,2,1,0:T(8,128)(2,1)}), bf16[1,32,64,512]{3,2,1,0:T(8,128)(2,1)}) %reduce-scatter.6.cloned.1.call-update) | async-done | bytes 2097168 | tf_op jit(solution)/shard_map/reduce_scatter | solution.py:496
  931.5 42.2 %all-to-all-done.14 = bf16[4,32,16,512]{3,2,1,0:T(8,128)(2,1)S(1)} async-done(((bf16[4,32,16,512]{3,2,1,0:T(8,128)(2,1)}), bf16[4,32,16,512]{3,2,1,0:T(8,128)(2,1)S(1)}, u32[]{:S(2)}, u32[]{:S(2)}) %all-to-all-start.14) | async-done | bytes 2097184 | tf_op jit(solution)/shard_map/all_to_all | solution.py:498
  1016.1 68.3 %collective-permute-done.12 = bf16[128,2048]{1,0:T(8,128)(2,1)S(1)} collective-permute-done((bf16[128,2048]{1,0:T(8,128)(2,1)S(1)}, bf16[128,2048]{1,0:T(8,128)(2,1)S(1)}, u32[]{:S(2)}, u32[]{:S(2)}) %collective-permute-start.12) | collective-permute-done | bytes 524320 | tf_op jit(solution)/shard_map/ppermute | solution.py:350
  1084.5 20.6 %collective-permute-start.13 = (bf16[128,2048]{1,0:T(8,128)(2,1)S(1)}, bf16[128,2048]{1,0:T(8,128)(2,1)S(1)}, u32[]{:S(2)}, u32[]{:S(2)}) collective-permute-start(bf16[128,2048]{1,0:T(8,128)(2,1)S(1)} %add_convert_fusion.1), channel_id=1, source_target_pairs={{0,8},{8,16},{16,24},{24,0},{1,9},{9,17},{17,25},{25,1},{2,10},{10... | collective-permute-start | bytes 1572872 | tf_op jit(solution)/shard_map/ppermute | solution.py:350
  1136.4 26.2 %shard_map.189 = (f32[8,512,512]{2,1,0:T(8,128)}, f32[8,512,512]{2,1,0:T(8,128)}, f32[8,512,512]{2,1,0:T(8,128)}, f32[8,512,512]{2,1,0:T(8,128)}) custom-call(bf16[8,512,512]{2,1,0:T(8,128)(2,1)S(1)} %bitcast.225, f32[8,512,512]{2,1,0:T(8,128)} %ls_ref.1, f32[8,512,512]{2,1,0:T(8,128)} %rs_ref.1, f32[8,512,512]{2,1,0:T(8,128)} %lr_ref.1, ...), custom_call_target="tpu_custom_call" | custom-call | flops 8589934592 | bytes 79691776 | tf_op jit(solution)/shard_map/pallas_call | solution.py:313
  (414 shorter events, 446.6 us)
Async XLA Ops:
  7.2 357.5 %all-gather.15.cloned.1.call-start = ((), (), s32[]{:S(2)}) async-start(), calls=%async_computation.29 | async-start | bytes 8912896 | tf_op jit(solution)/shard_map/all_gather | solution.py:446
  14.3 171.4 %all-to-all-start = ((bf16[256,16,512]{2,1,0:T(8,128)(2,1)}), bf16[256,16,512]{2,1,0:T(8,128)(2,1)}, u32[]{:S(2)}, u32[]{:S(2)}) async-start(bf16[256,16,512]{2,1,0:T(8,128)(2,1)} %bitcast.246), calls=%async_computation | async-start | bytes 8388608 | tf_op jit(solution)/shard_map/all_to_all | solution.py:413
  21.7 394.0 %all-gather.7.cloned.1.call-start = ((), (), s32[]{:S(2)}) async-start(), calls=%async_computation.22 | async-start | bytes 8650752 | tf_op jit(solution)/shard_map/all_gather | solution.py:426
  189.3 268.1 %all-gather.9.cloned.1.call-start = ((), (), s32[]{:S(2)}) async-start(), calls=%async_computation.23 | async-start | bytes 18874368 | tf_op jit(solution)/shard_map/all_gather | solution.py:433
  264.2 207.7 %all-gather.11.cloned.1.call-start = ((), (), s32[]{:S(2)}) async-start(), calls=%async_computation.24 | async-start | bytes 9437184 | tf_op jit(solution)/shard_map/all_gather | solution.py:433
  314.8 41.0 %all-to-all-start.1 = ((bf16[32,3,4,16,128]{4,3,2,1,0:T(8,128)(2,1)}), bf16[32,3,4,16,128]{4,3,2,1,0:T(8,128)(2,1)S(1)}, u32[]{:S(2)}, u32[]{:S(2)}) async-start(bf16[32,3,4,16,128]{4,3,2,1,0:T(8,128)(2,1)} %bitcast.5), calls=%async_computation.1 | async-start | bytes 3145728 | tf_op jit(solution)/shard_map/all_to_all | solution.py:421
  412.0 25.2 %all-to-all-start.4 = ((bf16[16,128,128]{1,2,0:T(8,128)(2,1)}), bf16[16,128,128]{1,2,0:T(8,128)(2,1)S(1)}, u32[]{:S(2)}, u32[]{:S(2)}) async-start(bf16[16,128,128]{1,2,0:T(8,128)(2,1)} %copy.220), calls=%async_computation.4 | async-start | bytes 1048576 | tf_op jit(solution)/shard_map/all_to_all | solution.py:473
  457.4 21.1 %collective-permute-start.2 = (bf16[128,2048]{1,0:T(8,128)(2,1)S(1)}, bf16[128,2048]{1,0:T(8,128)(2,1)S(1)}, u32[]{:S(2)}, u32[]{:S(2)}) collective-permute-start(bf16[128,2048]{1,0:T(8,128)(2,1)S(1)} %collective-permute-done.x_ref.refs_1_), channel_id=1, source_target_pairs={{0,8},{8,16},{16,24},{24,0},{1,9},{9,17},{17,25},{25,1},{2,10},{10... | collective-permute-start | bytes 1572872 | tf_op jit(solution)/shard_map/ppermute | solution.py:343
  478.5 26.3 %collective-permute-start.4 = (bf16[128,2048]{1,0:T(8,128)(2,1)S(1)}, bf16[128,2048]{1,0:T(8,128)(2,1)S(1)}, u32[]{:S(2)}, u32[]{:S(2)}) collective-permute-start(bf16[128,2048]{1,0:T(8,128)(2,1)S(1)} %collective-permute-done.2.x_ref.refs_2_), channel_id=1, source_target_pairs={{0,8},{8,16},{16,24},{24,0},{1,9},{9,17},{17,25},{25,1},{2,10},{10... | collective-permute-start | bytes 1572872 | tf_op jit(solution)/shard_map/ppermute | solution.py:343
  493.6 24.0 %collective-permute-start.3 = (bf16[128,2048]{1,0:T(8,128)(2,1)S(1)}, bf16[128,2048]{1,0:T(8,128)(2,1)S(1)}, u32[]{:S(2)}, u32[]{:S(2)}) collective-permute-start(bf16[128,2048]{1,0:T(8,128)(2,1)S(1)} %add_convert_fusion.6), channel_id=1, source_target_pairs={{0,8},{8,16},{16,24},{24,0},{1,9},{9,17},{17,25},{25,1},{2,10},{10... | collective-permute-start | bytes 1572872 | tf_op jit(solution)/shard_map/ppermute | solution.py:350
  563.5 27.7 %collective-permute-start.10 = (bf16[128,2048]{1,0:T(8,128)(2,1)S(1)}, bf16[128,2048]{1,0:T(8,128)(2,1)S(1)}, u32[]{:S(2)}, u32[]{:S(2)}) collective-permute-start(bf16[128,2048]{1,0:T(8,128)(2,1)S(1)} %collective-permute-done.8.x_ref), channel_id=1, source_target_pairs={{0,8},{8,16},{16,24},{24,0},{1,9},{9,17},{17,25},{25,1},{2,10},{10... | collective-permute-start | bytes 1572872 | tf_op jit(solution)/shard_map/ppermute | solution.py:343
  581.1 25.9 %collective-permute-start.9 = (bf16[128,2048]{1,0:T(8,128)(2,1)S(1)}, bf16[128,2048]{1,0:T(8,128)(2,1)S(1)}, u32[]{:S(2)}, u32[]{:S(2)}) collective-permute-start(bf16[128,2048]{1,0:T(8,128)(2,1)S(1)} %add_convert_fusion.3), channel_id=1, source_target_pairs={{0,8},{8,16},{16,24},{24,0},{1,9},{9,17},{17,25},{25,1},{2,10},{10... | collective-permute-start | bytes 1572872 | tf_op jit(solution)/shard_map/ppermute | solution.py:350
  644.1 183.6 %reduce-scatter.4.cloned.1.call-start = ((), (), s32[]{:S(2)}) async-start(), calls=%async_computation.26 | async-start | bytes 2359296 | tf_op jit(solution)/shard_map/reduce_scatter | solution.py:496
  672.1 179.5 %reduce-scatter.8.cloned.1.call-start = ((), (), s32[]{:S(2)}) async-start(), calls=%async_computation.28 | async-start | bytes 9437184 | tf_op jit(solution)/shard_map/reduce_scatter | solution.py:496
  691.9 224.8 %reduce-scatter.6.cloned.1.call-start = ((), (), s32[]{:S(2)}) async-start(), calls=%async_computation.27 | async-start | bytes 18874368 | tf_op jit(solution)/shard_map/reduce_scatter | solution.py:496
  788.3 24.3 %all-to-all-start.10 = ((bf16[48,16,512]{2,1,0:T(8,128)(2,1)}), bf16[48,16,512]{2,1,0:T(8,128)(2,1)S(1)}, u32[]{:S(2)}, u32[]{:S(2)}) async-start(bf16[48,16,512]{2,1,0:T(8,128)(2,1)} %broadcast_select_fusion.3), calls=%async_computation.10 | async-start | bytes 1572864 | tf_op jit(solution)/shard_map/all_to_all | solution.py:431
  824.1 23.6 %all-to-all-start.11 = ((bf16[16,3,4,16,128]{4,3,2,1,0:T(8,128)(2,1)}), bf16[16,3,4,16,128]{4,3,2,1,0:T(8,128)(2,1)S(1)}, u32[]{:S(2)}, u32[]{:S(2)}) async-start(bf16[16,3,4,16,128]{4,3,2,1,0:T(8,128)(2,1)} %bitcast.73), calls=%async_computation.11 | async-start | bytes 1572864 | tf_op jit(solution)/shard_map/all_to_all | solution.py:549
  859.4 60.4 %all-to-all-start.15 = ((bf16[4,16,16,512]{3,2,1,0:T(8,128)(2,1)}), bf16[4,16,16,512]{3,2,1,0:T(8,128)(2,1)S(1)}, u32[]{:S(2)}, u32[]{:S(2)}) async-start(bf16[4,16,16,512]{3,2,1,0:T(8,128)(2,1)} %copy.247), calls=%async_computation.18 | async-start | bytes 2097152 | tf_op jit(solution)/shard_map/all_to_all | solution.py:498
  863.0 140.8 %all-gather.13.cloned.1.call-start = ((), (), s32[]{:S(2)}) async-start(), calls=%async_computation.25 | async-start | bytes 7077888 | tf_op jit(solution)/shard_map/all_gather | solution.py:433
  920.9 52.8 %all-to-all-start.14 = ((bf16[4,32,16,512]{3,2,1,0:T(8,128)(2,1)}), bf16[4,32,16,512]{3,2,1,0:T(8,128)(2,1)S(1)}, u32[]{:S(2)}, u32[]{:S(2)}) async-start(bf16[4,32,16,512]{3,2,1,0:T(8,128)(2,1)} %copy.246), calls=%async_computation.16 | async-start | bytes 4194304 | tf_op jit(solution)/shard_map/all_to_all | solution.py:498
  973.6 23.2 %all-to-all-start.9 = ((bf16[4,3,4,128,128]{4,3,2,1,0:T(8,128)(2,1)}), bf16[4,3,4,128,128]{4,3,2,1,0:T(8,128)(2,1)}, u32[]{:S(2)}, u32[]{:S(2)}) async-start(bf16[4,3,4,128,128]{4,3,2,1,0:T(8,128)(2,1)} %copy_bitcast_fusion), calls=%async_computation.9 | async-start | bytes 3145728 | tf_op jit(solution)/shard_map/all_to_all | solution.py:518
  996.8 136.7 %all-to-all-start.16 = ((bf16[256,16,512]{2,1,0:T(8,128)(2,1)}), bf16[256,16,512]{2,1,0:T(8,128)(2,1)}, u32[]{:S(2)}, u32[]{:S(2)}) async-start(bf16[256,16,512]{2,1,0:T(8,128)(2,1)} %broadcast_select_fusion), calls=%async_computation.19 | async-start | bytes 8388608 | tf_op jit(solution)/shard_map/all_to_all | solution.py:568
  1008.8 75.6 %collective-permute-start.12 = (bf16[128,2048]{1,0:T(8,128)(2,1)S(1)}, bf16[128,2048]{1,0:T(8,128)(2,1)S(1)}, u32[]{:S(2)}, u32[]{:S(2)}) collective-permute-start(bf16[128,2048]{1,0:T(8,128)(2,1)S(1)} %convert_element_type.150), channel_id=1, source_target_pairs={{0,8},{8,16},{16,24},{24,0},{1,9},{9,17},{17,25},{25,1},{2,10},{10... | collective-permute-start | bytes 1572872 | tf_op jit(solution)/shard_map/ppermute | solution.py:350
  1084.5 32.0 %collective-permute-start.13 = (bf16[128,2048]{1,0:T(8,128)(2,1)S(1)}, bf16[128,2048]{1,0:T(8,128)(2,1)S(1)}, u32[]{:S(2)}, u32[]{:S(2)}) collective-permute-start(bf16[128,2048]{1,0:T(8,128)(2,1)S(1)} %add_convert_fusion.1), channel_id=1, source_target_pairs={{0,8},{8,16},{16,24},{24,0},{1,9},{9,17},{17,25},{25,1},{2,10},{10... | collective-permute-start | bytes 1572872 | tf_op jit(solution)/shard_map/ppermute | solution.py:350
  (84 other events, 1238.8 us)
Sparse Core Ops, SparseCore 0:
  10.8 184.1 all-gather.14
  198.4 103.0 all-gather.6
  304.0 110.7 all-gather.8
  417.2 54.6 all-gather.10
  672.2 38.3 reduce-scatter.3
  714.9 74.8 reduce-scatter.7
  793.3 123.3 reduce-scatter.5
  919.2 45.5 all-gather.12

commit v3 on v2

v3 whole, which is shorter than its diff:
```python
import functools

import jax
import jax.numpy as jnp
from jax import lax
from jax.experimental import pallas as pl
from jax.experimental.pallas import tpu as pltpu
from jax.sharding import Mesh
from jax.sharding import PartitionSpec as P

FF = 8192
HEADS = 16
SEGMAX = 1024
QB = 256
Z = 4

epsilon = 1e-06
rope_base = 500000.0
decay_rate = 0.5
step_rate = 0.5
gain_rate = 0.3
bf16 = jnp.bfloat16
f32 = jnp.float32
EVERY = ("hz", "hp", "seq")
GROUP = ("hz", "hp")
VMEM_LIMIT = 48 * 1024 * 1024


def mm(left_side, right_side):
    return jnp.dot(left_side, right_side, preferred_element_type=f32)


def mm_nt(left_side, right_side):
    return lax.dot_general(
        left_side, right_side, (((1,), (1,)), ((), ())), preferred_element_type=f32
    )


def mm_tn(left_side, right_side):
    return lax.dot_general(
        left_side, right_side, (((0,), (0,)), ((), ())), preferred_element_type=f32
    )


def params():
    return pltpu.CompilerParams(vmem_limit_bytes=VMEM_LIMIT)


def cost(flops, nbytes, exps=0):
    part = 0.1
    return pl.CostEstimate(
        flops=int(part * flops), bytes_accessed=int(part * nbytes), transcendentals=int(part * exps)
    )


def nbytes(*arrays):
    return sum(a.size * a.dtype.itemsize for a in arrays)


def join(refs):
    return refs[0][...] if len(refs) == 1 else jnp.concatenate([r[...] for r in refs], axis=-2)


def whole(array):
    return pl.BlockSpec(array.shape, lambda *_: (0,) * array.ndim)


def gate_up_kernel(*refs):
    *x_refs, g_ref, u_ref, gate_ref, up_ref, hidden_ref = refs
    x, side = join(x_refs), g_ref.shape[-1]
    for w_ref, y_ref in ((g_ref, gate_ref), (u_ref, up_ref)):
        total = None
        for r in range(w_ref.shape[1]):
            part = mm(x[:, r * side : (r + 1) * side], w_ref[:, r, 0].reshape(side, side))
            total = part if total is None else total + part
        y_ref[...] = total
    gate = gate_ref[...]
    hidden_ref[...] = (gate * jax.nn.sigmoid(gate) * up_ref[...]).astype(bf16)


def gate_up(xs, w):
    rep, R, C, part, side = w.shape
    count, half = sum(x.shape[0] for x in xs), C // 2
    wide = jax.ShapeDtypeStruct((count, half * side), f32)
    outs = [wide, wide, jax.ShapeDtypeStruct((count, half * side), bf16)]
    col = pl.BlockSpec((count, side), lambda c: (0, c))
    return pl.pallas_call(
        gate_up_kernel,
        grid=(half,),
        in_specs=[
            *[whole(x) for x in xs],
            pl.BlockSpec((rep, R, 1, part, side), lambda c: (0, 0, c, 0, 0)),
            pl.BlockSpec((rep, R, 1, part, side), lambda c: (0, 0, c + half, 0, 0)),
        ],
        out_specs=[col, col, col],
        out_shape=outs,
        compiler_params=params(),
        cost_estimate=cost(2 * count * R * C * side * side, nbytes(*xs, w, *outs)),
    )(*xs, w, w)


def nn_kernel(x_ref, w_ref, *refs):
    y_ref = refs[-1]
    side = w_ref.shape[-1]
    total = None
    for r in range(w_ref.shape[1]):
        part = mm(x_ref[:, r * side : (r + 1) * side], w_ref[:, r, 0].reshape(side, side))
        total = part if total is None else total + part
    y_ref[...] = total


def nn(x, w, *others, columns=None, row=None):
    rep, R, C, part, side = w.shape
    count = x.shape[0]
    if row is None:
        block, index = (rep, R, 1, part, side), lambda c: (0, 0, c, 0, 0)
        steps = columns or C
    else:
        block, index = (rep, 1, 1, part, side), lambda c: (0, c, row, 0, 0)
        steps = R
    out = jax.ShapeDtypeStruct((count, steps * side), f32)
    return pl.pallas_call(
        nn_kernel,
        grid=(steps,),
        in_specs=[pl.BlockSpec(x.shape, lambda c: (0, 0)), pl.BlockSpec(block, index)]
        + [pl.BlockSpec(memory_space=pl.ANY)] * len(others),
        out_specs=pl.BlockSpec((count, side), lambda c: (0, c)),
        out_shape=out,
        compiler_params=params(),
        cost_estimate=cost(
            2 * count * x.shape[1] * steps * side, nbytes(x, out) + 2 * x.shape[1] * steps * side
        ),
    )(x, w, *others)


def hidden_back_kernel(half, *refs):
    w_ref, gate_ref, up_ref = refs[half : half + 3]
    x, y_ref, side = join(refs[:half]), refs[-1], w_ref.shape[-1]
    total = None
    for c in range(w_ref.shape[2]):
        part = mm_nt(x[:, c * side : (c + 1) * side], w_ref[:, 0, c].reshape(side, side))
        total = part if total is None else total + part
    gate = gate_ref[...]
    sigma = jax.nn.sigmoid(gate)
    y_ref[0] = (total * up_ref[...] * sigma * (1.0 + gate * (1.0 - sigma))).astype(bf16)
    y_ref[1] = (total * gate * sigma).astype(bf16)


def hidden_back(xs, w, gate, up, *others):
    rep, R, C, part, side = w.shape
    count = gate.shape[0]
    out = jax.ShapeDtypeStruct((2, count, R * side), bf16)
    col = pl.BlockSpec((count, side), lambda r: (0, r))
    return pl.pallas_call(
        functools.partial(hidden_back_kernel, len(xs)),
        grid=(R,),
        in_specs=[
            *[whole(x) for x in xs],
            pl.BlockSpec((rep, 1, C, part, side), lambda r: (0, r, 0, 0, 0)),
            col,
            col,
            *[pl.BlockSpec(memory_space=pl.ANY)] * len(others),
        ],
        out_specs=pl.BlockSpec((2, count, side), lambda r: (0, 0, r)),
        out_shape=out,
        compiler_params=params(),
        cost_estimate=cost(2 * count * R * C * side * side, nbytes(*xs, w, gate, up, out)),
    )(*xs, w, gate, up, *others)


def nt_kernel(half, *refs):
    x, w_ref, y_ref = join(refs[:half]), refs[half], refs[-1]
    side = w_ref.shape[-1]
    per = x.shape[2] // side
    total = None
    for c in range(w_ref.shape[1] * w_ref.shape[2]):
        left = x[c // per, :, (c % per) * side : (c % per + 1) * side]
        w = w_ref[:, c // w_ref.shape[2], c % w_ref.shape[2]].reshape(side, side)
        part = mm_nt(left, w)
        total = part if total is None else total + part
    y_ref[...] = total


def nt(xs, w, *others, row=None):
    rep, R, C, part, side = w.shape
    count, depth = sum(x.shape[1] for x in xs), xs[0].shape[0] * xs[0].shape[2]
    if row is None:
        block, index = (rep, 1, depth // side, part, side), lambda r: (0, r, 0, 0, 0)
        steps = R
    else:
        block, index = (rep, R, 1, part, side), lambda r: (0, 0, row, 0, 0)
        steps = 1
    out = jax.ShapeDtypeStruct((count, steps * side), f32)
    return pl.pallas_call(
        functools.partial(nt_kernel, len(xs)),
        grid=(steps,),
        in_specs=[
            *[whole(x) for x in xs],
            pl.BlockSpec(block, index),
            *[pl.BlockSpec(memory_space=pl.ANY)] * len(others),
        ],
        out_specs=pl.BlockSpec((count, side), lambda r: (0, r)),
        out_shape=out,
        compiler_params=params(),
        cost_estimate=cost(
            2 * count * depth * steps * side, nbytes(*xs, out) + 2 * depth * steps * side
        ),
    )(*xs, w, *others)


def tn_kernel(lefts, rights, *refs):
    y_ref = refs[-1]
    rep, _, _, part, side = y_ref.shape
    left, right = join(refs[:lefts]), join(refs[lefts : lefts + rights])
    y_ref[:, 0, 0] = mm_tn(left, right[0]).astype(bf16).reshape(rep, part, side)


def tn(lefts, rights, rep, side, *others, only=None):
    R = lefts[0].shape[1] // side
    m, per = rights[0].shape[0], rights[0].shape[2] // side
    first, C = (0, m * per) if only is None else (only, per)
    out = jax.ShapeDtypeStruct((rep, R, C, side // rep, side), bf16)
    total = sum(x.shape[0] for x in lefts)
    return pl.pallas_call(
        functools.partial(tn_kernel, len(lefts), len(rights)),
        grid=(R, C),
        in_specs=[pl.BlockSpec((x.shape[0], side), lambda r, c: (0, r)) for x in lefts]
        + [
            pl.BlockSpec((1, x.shape[1], side), lambda r, c: (first + c // per, 0, c % per))
            for x in rights
        ]
        + [pl.BlockSpec(memory_space=pl.ANY)] * len(others),
        out_specs=pl.BlockSpec((rep, 1, 1, side // rep, side), lambda r, c: (0, r, c, 0, 0)),
        out_shape=out,
        compiler_params=params(),
        cost_estimate=cost(2 * total * R * C * side * side, nbytes(*lefts, *rights, out)),
    )(*lefts, *rights, *others)


def heads_kernel(half, *refs):
    y_ref = refs[-1]
    rep, _, part, width = y_ref.shape
    left = jnp.concatenate([r[...] for r in refs[:half]], axis=0)
    right = jnp.concatenate([r[...] for r in refs[half : 2 * half]], axis=0)
    y_ref[:, 0] = mm_tn(left, right).astype(bf16).reshape(rep, part, width)


def heads_tn(lefts, rights, rep, side, *others):
    count, R = lefts[0].shape[0], lefts[0].shape[1] // side
    width = rights[0].shape[1]
    out = jax.ShapeDtypeStruct((rep, R, side // rep, width), bf16)
    return pl.pallas_call(
        functools.partial(heads_kernel, len(lefts)),
        grid=(R,),
        in_specs=[pl.BlockSpec((count, side), lambda r: (0, r))] * len(lefts)
        + [pl.BlockSpec((count, width), lambda r: (0, 0))] * len(rights)
        + [pl.BlockSpec(memory_space=pl.ANY)] * len(others),
        out_specs=pl.BlockSpec((rep, 1, side // rep, width), lambda r: (0, r, 0, 0)),
        out_shape=out,
        compiler_params=params(),
        cost_estimate=cost(
            2 * count * len(lefts) * R * side * width, nbytes(*lefts, *rights, out)
        ),
    )(*lefts, *rights, *others)


def scores_of(q, k, begin, q_start, k_start, scale):
    scores = mm_nt(k, q) * scale
    key_place = k_start + lax.broadcasted_iota(jnp.int32, scores.shape, 0)
    query_place = q_start + lax.broadcasted_iota(jnp.int32, scores.shape, 1)
    return jnp.where((key_place >= begin) & (key_place <= query_place), scores, -1e30)


def window_start(i, block, window, length):
    start = jnp.clip(i * block + block - window, 0, length - window)
    return pl.multiple_of(start, 128)


def attend_kernel(scale, window, q_ref, k_ref, v_ref, b_ref, o_ref, lse_ref):
    block, length = q_ref.shape[0], k_ref.shape[0]
    i = pl.program_id(0)
    start = window_start(i, block, window, length)
    scores = scores_of(
        q_ref[...], k_ref[pl.ds(start, window), :], b_ref[...], i * block, start, scale
    )
    top = jnp.max(scores, axis=0, keepdims=True)
    expo = jnp.exp(scores - top)
    total = jnp.sum(expo, axis=0, keepdims=True)
    attention = (expo * (1.0 / total)).astype(bf16)
    o_ref[...] = mm_tn(attention, v_ref[pl.ds(start, window), :]).astype(bf16)
    lse_ref[...] = top + jnp.log(total)


def attend(q, k, v, begins, scale):
    length, width = q.shape
    window = min(QB + SEGMAX, length)
    full = pl.BlockSpec((length, width), lambda i: (0, 0))
    rows = pl.BlockSpec((QB, width), lambda i: (i, 0))
    line = pl.BlockSpec((1, QB), lambda i: (0, i))
    return pl.pallas_call(
        functools.partial(attend_kernel, scale, window),
        grid=(length // QB,),
        in_specs=[rows, full, full, line],
        out_specs=[rows, line],
        out_shape=[
            jax.ShapeDtypeStruct((length, width), bf16),
            jax.ShapeDtypeStruct((1, length), f32),
        ],
        compiler_params=params(),
        cost_estimate=cost(4 * length * window * width, 4 * nbytes(q), length * window),
    )(q, k, v, begins)


def attend_back_kernel(
    scale, window, q_ref, d_ref, k_ref, v_ref, b_ref, lse_ref, *refs
):
    dq_ref, dk_ref, dv_ref, ka, va = refs[-5:]
    block, length = q_ref.shape[0], k_ref.shape[0]
    i = pl.program_id(0)
    start = window_start(i, block, window, length)
    span = pl.ds(start, window)

    @pl.when(i == 0)
    def _():
        ka[...] = jnp.zeros_like(ka)
        va[...] = jnp.zeros_like(va)

    q, d, k = q_ref[...], d_ref[...], k_ref[span, :]
    scores = scores_of(q, k, b_ref[...], i * block, start, scale)
    attention = jnp.exp(scores - lse_ref[...])
    prob_grad = mm_nt(v_ref[span, :], d)
    center = jnp.sum(attention * prob_grad, axis=0, keepdims=True)
    score_grad = (attention * (prob_grad - center)).astype(bf16)
    dq_ref[...] = (mm_tn(score_grad, k) * scale).astype(bf16)
    ka[span, :] += mm(score_grad, q) * scale
    va[span, :] += mm(attention.astype(bf16), d)

    @pl.when(i == pl.num_programs(0) - 1)
    def _():
        dk_ref[...] = ka[...].astype(bf16)
        dv_ref[...] = va[...].astype(bf16)


def attend_back(q, d, k, v, begins, lse, scale, *others):
    length, width = q.shape
    window = min(QB + SEGMAX, length)
    full = pl.BlockSpec((length, width), lambda i: (0, 0))
    rows = pl.BlockSpec((QB, width), lambda i: (i, 0))
    line = pl.BlockSpec((1, QB), lambda i: (0, i))
    return pl.pallas_call(
        functools.partial(attend_back_kernel, scale, window),
        grid=(length // QB,),
        in_specs=[rows, rows, full, full, line, line]
        + [pl.BlockSpec(memory_space=pl.ANY)] * len(others),
        out_specs=[rows, full, full],
        out_shape=[jax.ShapeDtypeStruct((length, width), bf16)] * 3,
        scratch_shapes=[pltpu.VMEM((length, width), f32)] * 2,
        compiler_params=params(),
        cost_estimate=cost(10 * length * window * width, 8 * nbytes(q), length * window),
    )(q, d, k, v, begins, lse, *others)


def shampoo_kernel(g_ref, ls_ref, rs_ref, lr_ref, rr_ref, w_ref, go_ref, lo_ref, ro_ref, wo_ref):
    g = g_ref[0]
    go_ref[0] = g.astype(f32)
    lo_ref[0] = decay_rate * ls_ref[0] + (1.0 - decay_rate) * mm_nt(g, g)
    ro_ref[0] = decay_rate * rs_ref[0] + (1.0 - decay_rate) * mm_tn(g, g)
    middle = mm(lr_ref[0].astype(bf16), g).astype(bf16)
    wo_ref[0] = w_ref[0] - step_rate * mm(middle, rr_ref[0].astype(bf16))


def shampoo(g, *rest):
    slots, side, _ = g.shape
    spec = pl.BlockSpec((1, side, side), lambda s: (s, 0, 0))
    return pl.pallas_call(
        shampoo_kernel,
        grid=(slots,),
        in_specs=[spec] * 6,
        out_specs=[spec] * 4,
        out_shape=[jax.ShapeDtypeStruct(g.shape, f32)] * 4,
        compiler_params=params(),
        cost_estimate=cost(8 * slots * side**3, 38 * g.size),
    )(g, *rest)


def rms_norm(values, gain_vec):
    return (
        values * lax.rsqrt(jnp.mean(values * values, axis=-1, keepdims=True) + epsilon) * gain_vec
    )


def begins_of(segment_row):
    length = segment_row.shape[0]
    indices = jnp.arange(length, dtype=jnp.int32)
    earlier = jnp.concatenate([jnp.full((1,), -1, jnp.int32), segment_row[:-1]])
    return lax.cummax(jnp.where(segment_row != earlier, indices, 0), axis=0)


UP = [(i, (i + 1) % Z) for i in range(Z)]


def ring_gather(block, *others):
    blocks = [block]
    for k in range(Z - 1):
        got = lax.ppermute(blocks[-1], "hz", UP)
        blocks.append(after(got, others[k]) if k < len(others) else got)
    return blocks


def ring_scatter(part_of):
    total = part_of(1).astype(bf16)
    for k in (2, 3):
        total = (lax.ppermute(total, "hz", UP).astype(f32) + part_of(k)).astype(bf16)
    return lax.ppermute(total, "hz", UP).astype(f32) + part_of(0)


def none_kernel(*refs):
    pass


def after(value, *others):
    anywhere = pl.BlockSpec(memory_space=pl.ANY)
    return pl.pallas_call(
        none_kernel,
        in_specs=[anywhere] * (1 + len(others)),
        out_specs=anywhere,
        out_shape=jax.ShapeDtypeStruct(value.shape, value.dtype),
        input_output_aliases={0: 0},
    )(value, *others)


def exchange_z(part_for):
    got = [part_for(0)]
    for j in range(1, Z):
        got.append(lax.ppermute(part_for(j), "hz", [(i, (i + j) % Z) for i in range(Z)]))
    return jnp.stack(got)


def swap(value, bit):
    size = lax.axis_size("hp")
    return lax.ppermute(value, "hp", [(i, i ^ bit) for i in range(size)])


def plane_scatter(pieces):
    PN, S = lax.axis_size("hp"), lax.axis_size("seq")
    if S != 2 or PN != 4:
        return lax.psum_scatter(pieces, ("hp", "seq"), scatter_dimension=0, tiled=False)
    p = lax.axis_index("hp")
    chip = sum_seq_scatter(pieces.reshape((PN, S) + pieces.shape[1:]), 1)
    half = chip.shape[1] // 2

    def add(mine, got):
        return (mine.astype(f32) + got.astype(f32)).astype(bf16)

    def pair(values, first, second):
        return jnp.take(values, jnp.stack([p ^ first, p ^ second]), axis=0, mode="clip")

    one, two = chip[:, :half], chip[:, half:]
    one_got, two_got = swap(pair(one, 1, 3), 1), swap(pair(two, 2, 3), 2)
    one, two = add(pair(one, 0, 2), one_got), add(pair(two, 0, 1), two_got)
    one_got, two_got = swap(one[1], 2), swap(two[1], 1)
    return jnp.concatenate([add(one[0], one_got), add(two[0], two_got)])


def from_group(values):
    size = lax.axis_size(GROUP)
    spread = jnp.broadcast_to(values, (size,) + values.shape)
    return lax.all_to_all(spread, GROUP, 0, 0, tiled=True)


def sum_seq_scatter(values, axis):
    S = lax.axis_size("seq")
    if S != 2:
        return lax.psum_scatter(values, "seq", scatter_dimension=axis, tiled=False)
    c = lax.axis_index("seq")
    mine = lax.dynamic_index_in_dim(values, c, axis, keepdims=False)
    other = lax.dynamic_index_in_dim(values, 1 - c, axis, keepdims=False)
    got = lax.ppermute(other, "seq", [(0, 1), (1, 0)])
    return (mine.astype(f32) + got.astype(f32)).astype(bf16)


def body(
    tokens,
    cotangent,
    segment_ids,
    owner_map,
    weights,
    norm_gains,
    left_stats,
    right_stats,
    left_root,
    right_root,
):
    model_width = tokens.shape[2]
    local_count = tokens.shape[1]
    slots, side = weights.shape[0], weights.shape[1]
    total_blocks = owner_map.shape[0]
    PN, S = lax.axis_size("hp"), lax.axis_size("seq")
    n = Z * PN * S
    rep = PN * S
    rows = side // n
    part = Z * rows
    head_size = model_width // HEADS
    quarter = model_width // Z
    score_scale = head_size ** (-0.5)
    zi, pi = lax.axis_index("hz"), lax.axis_index("hp")
    relative = (zi - jnp.arange(Z, dtype=jnp.int32)) % Z
    inputs = tokens[0]

    def zero_of(value):
        entry = value[(0,) * value.ndim]
        if value.dtype == jnp.int32:
            return (entry < 0).astype(jnp.int32)
        return (entry != entry).astype(jnp.int32)

    D, F = model_width // side, FF // side
    number = jnp.arange(total_blocks, dtype=jnp.int32)
    square, tall = D * D, D * F
    qkv_list = number[: 3 * square].reshape(3, D, Z).transpose(2, 1, 0)
    out_list = number[3 * square : 4 * square].reshape(Z, D, 1)
    attn_list = jnp.concatenate([qkv_list, out_list], axis=2).reshape(Z, -1)
    gateup_list = number[4 * square : 4 * square + 2 * tall].reshape(2, D, Z, F // Z)
    gateup_list = gateup_list.transpose(2, 1, 0, 3).reshape(Z, -1)
    down_list = number[4 * square + 2 * tall :].reshape(Z, -1)
    inverse = jnp.zeros((total_blocks,), jnp.int32).at[owner_map].set(number)

    low = weights.astype(bf16).reshape(slots, PN, S, Z, rows, side)
    low = low.transpose(3, 1, 2, 0, 4, 5).reshape(n * slots, rows, side)
    spread = lax.all_to_all(low, EVERY, 0, 0, tiled=True)
    tokens_g = lax.all_gather(inputs, "hz", axis=0, tiled=True)

    group = Z * PN
    own_ids = segment_ids + zero_of(tokens_g)
    row_ids = from_group(own_ids[0]).reshape(-1)
    length = row_ids.shape[0]

    def fetch(numbers, *others):
        places = inverse[numbers.reshape(-1)]
        for other in others:
            places = places + zero_of(other)
        picked = jnp.take(spread, places, axis=0, mode="clip")
        got = lax.all_to_all(picked, "hz", 0, 0, tiled=True)
        return got.reshape(Z, -1, rows, side).transpose(1, 0, 2, 3).reshape(-1, part, side)

    def all_plane(got, R):
        got = lax.all_gather(got, ("hp", "seq"), axis=0, tiled=False)
        return got.reshape(rep, R, -1, part, side)

    got_attn = fetch(attn_list, tokens_g)
    w_attn = all_plane(got_attn, D)
    def fetch_beside(numbers, other):
        def part_for(j):
            wanted = lax.dynamic_index_in_dim(numbers, (zi + j) % Z, 0, keepdims=False)
            return jnp.take(spread, inverse[wanted] + zero_of(other), axis=0, mode="clip")

        got = jnp.take(exchange_z(part_for), relative, axis=0, mode="clip")
        return got.transpose(1, 0, 2, 3).reshape(-1, part, side)

    w_gateup = all_plane(fetch_beside(gateup_list, got_attn), D)

    begins = begins_of(row_ids)
    places = jnp.arange(length, dtype=jnp.int32) - begins
    half_size = head_size // 2
    frequency = rope_base ** (-2.0 * jnp.arange(half_size, dtype=f32) / head_size)
    angles = places.astype(f32)[:, None] * frequency[None, :]
    cosine, sine = jnp.cos(angles), jnp.sin(angles)
    group_tokens = Z * local_count

    def rope(values, sign):
        first, second = values[:, :half_size], values[:, half_size:]
        return jnp.concatenate(
            [first * cosine - second * sine * sign, second * cosine + first * sine * sign], axis=-1
        )

    head = zi * PN + pi
    gains_head = lax.dynamic_slice_in_dim(norm_gains[2:4], head * head_size, head_size, axis=1)

    def to_heads(stack):
        m = stack.shape[0]
        shaped = stack.reshape(m, Z, local_count, PN, head_size).transpose(3, 0, 1, 2, 4)
        got = lax.all_to_all(shaped, "hp", 0, 0, tiled=True)
        return got.transpose(1, 2, 0, 3, 4).reshape(m, length, head_size)

    def to_groups(stack):
        m = stack.shape[0]
        shaped = stack.reshape(m, Z, PN, local_count, head_size).transpose(2, 0, 1, 3, 4)
        got = lax.all_to_all(shaped, "hp", 0, 0, tiled=True)
        return got.transpose(1, 2, 3, 0, 4).reshape(m, group_tokens, quarter)

    raw = nn(tokens_g, w_attn, columns=3)
    raw_three = raw.reshape(group_tokens, 3, quarter).transpose(1, 0, 2)
    squares = jnp.sum(raw_three[:2] * raw_three[:2], axis=-1)
    squares = from_group(squares).reshape(Z, PN, 2, Z, local_count)
    squares = jnp.sum(squares, axis=0).transpose(1, 2, 0, 3).reshape(2, length, 1)
    raw_row = to_heads(raw_three.astype(bf16))
    invs = lax.rsqrt(squares / model_width + epsilon)
    query_hat, key_hat = (raw_row[i].astype(f32) * invs[i] for i in range(2))
    query_row = rope(query_hat * gains_head[0], 1.0).astype(bf16)
    key_row = rope(key_hat * gains_head[1], 1.0).astype(bf16)
    value_row = raw_row[2]

    got_down = fetch_beside(down_list, raw_row)
    w_down = all_plane(after(got_down, w_gateup), F // Z)

    begin_line = begins[None, :]
    mixed, log_sums = attend(query_row, key_row, value_row, begin_line, score_scale)
    attended = to_groups(mixed[None]).reshape(Z, local_count, quarter)
    attended_rel = jnp.take(attended, relative, axis=0, mode="clip")
    attn_raw = ring_scatter(
        lambda k: nn(attended_rel[k], w_attn, *([got_down] if k == 2 else []), row=3)
    )
    resid = inputs.astype(f32) + rms_norm(attn_raw, norm_gains[0])

    resid_blocks = ring_gather(resid.astype(bf16))

    tokens_z = tokens_g.reshape(Z, local_count, model_width)
    middle = local_count // 2
    tok_one, tok_two = after(tokens_z[:, :middle], resid), after(tokens_z[:, middle:], resid)
    tok_one = jnp.stack([tok_one, swap(tok_one, 1)])
    tok_two = jnp.stack([tok_two, swap(tok_two, 2)])
    tok_parts = [tok_one, swap(tok_one, 2), tok_two, swap(tok_two, 1)]
    tok_parts = [t.reshape(-1, model_width) for t in tok_parts]
    tok_near, tok_far = tok_parts[::2], tok_parts[1::2]
    pairs = [resid_blocks[:2], resid_blocks[2:]]
    gates, ups, hiddens = zip(*[gate_up(pair, w_gateup) for pair in pairs])

    def entry(halves, k):
        return halves[k // 2][k % 2 * local_count : (k % 2 + 1) * local_count]

    downs = [nn(hiddens[0], w_down), nn(hiddens[1], w_down, *tok_near)]
    down_raw = ring_scatter(lambda k: entry(downs, k))
    output = (resid + rms_norm(down_raw, norm_gains[1])).astype(bf16)[None]

    upstream = cotangent[0].astype(f32)
    _, down_norm_back = jax.vjp(rms_norm, down_raw, norm_gains[1])
    down_grad, gain_mlp_grad = down_norm_back(upstream)
    down_blocks = ring_gather(down_grad.astype(bf16))
    gateup_grads = [
        hidden_back(down_blocks[2 * i : 2 * i + 2], w_down, gates[i], ups[i], *[[], tok_far][i])
        for i in range(2)
    ]
    def spread_z(summed):
        summed = summed.reshape(-1, Z, rows, side)
        return exchange_z(
            lambda j: lax.dynamic_index_in_dim(summed, (zi + j) % Z, 1, keepdims=False)
        )

    def blocks_of(pieces):
        return pieces.reshape(rep, -1, part, side)

    def sum_plane(pieces):
        return lax.psum_scatter(
            blocks_of(pieces), ("hp", "seq"), scatter_dimension=0, tiled=False
        )

    down_pieces = tn(hiddens, [b[None] for b in down_blocks], rep, side)
    gate_pieces = tn(resid_blocks, gateup_grads, rep, side, only=0)
    up_pieces = tn(resid_blocks, gateup_grads, rep, side, only=1)
    gate_sum = sum_plane(gate_pieces)
    up_sum = sum_plane(up_pieces)
    down_sum = sum_plane(down_pieces)
    resid_parts = [nt([grads], w_gateup) for grads in gateup_grads]
    resid_grad = upstream + ring_scatter(lambda k: entry(resid_parts, k))

    _, attn_norm_back = jax.vjp(rms_norm, attn_raw, norm_gains[0])
    attn_grad, gain_attn_grad = attn_norm_back(resid_grad)
    attn_low = attn_grad.astype(bf16)
    attn_blocks = ring_gather(attn_low)
    grad_rel = nt([b[None] for b in attn_blocks], w_attn, row=3).astype(bf16)
    grad_rel = grad_rel.reshape(Z, local_count, quarter)
    grad_abs = jnp.take(grad_rel, relative, axis=0, mode="clip")
    grad_row = to_heads(grad_abs.reshape(1, group_tokens, quarter))[0]
    out_pieces = tn(
        [attended_rel[k] for k in range(Z)], [b[None] for b in attn_blocks], rep, side
    )
    out_sum = plane_scatter(blocks_of(out_pieces))
    query_grad, key_grad, value_grad = attend_back(
        query_row,
        grad_row,
        key_row,
        value_row,
        begin_line,
        log_sums,
        score_scale,
    )
    gate_sent = spread_z(gate_sum)
    up_sent, down_sent = spread_z(up_sum), spread_z(down_sum)
    query_turn, key_turn = rope(query_grad.astype(f32), -1.0), rope(key_grad.astype(f32), -1.0)
    gain_query = jnp.sum(query_turn * query_hat, axis=0)
    gain_key = jnp.sum(key_turn * key_hat, axis=0)
    query_turn, key_turn = query_turn * gains_head[0], key_turn * gains_head[1]
    dots = jnp.stack([jnp.sum(query_turn * query_hat, -1), jnp.sum(key_turn * key_hat, -1)])
    dots = jnp.sum(from_group(dots).reshape(group, 2, length), axis=0) / model_width
    dots = dots[..., None]
    query_back = ((query_turn - query_hat * dots[0]) * invs[0]).astype(bf16)
    key_back = ((key_turn - key_hat * dots[1]) * invs[1]).astype(bf16)

    back_row = jnp.concatenate([query_back, key_back, value_grad], axis=1)
    by_half = back_row.reshape(Z, PN, 2, middle, 3 * head_size).transpose(1, 2, 0, 3, 4)

    def rows_of(half, *bits):
        picked = jnp.take(by_half[:, half], jnp.stack([pi ^ bit for bit in bits]), axis=0, mode="clip")
        return picked.reshape(-1, 3 * head_size)

    back_parts = [rows_of(0, 0, 1), rows_of(0, 2, 3), rows_of(1, 0, 2), rows_of(1, 1, 3)]
    heads_grad = heads_tn(tok_parts, back_parts, rep, side)
    heads_sum = sum_seq_scatter(heads_grad.reshape(PN, S, D, part, 3 * head_size), 1)
    heads_sum = heads_sum.reshape(PN, D, Z, rows, 3 * head_size).transpose(2, 0, 1, 3, 4)
    heads_sent = lax.all_to_all(
        heads_sum.reshape(group, D, rows, 3 * head_size), GROUP, 0, 0, tiled=True
    ).reshape(Z, PN, D, rows, 3, head_size)
    heads_sent = heads_sent.transpose(4, 2, 0, 3, 1, 5).reshape(3 * square, rows, side)

    back_abs = to_groups(jnp.stack([query_back, key_back, value_grad]))
    back_rel = jnp.take(
        back_abs.reshape(3, Z, local_count, quarter), relative, axis=1, mode="clip"
    )
    input_grad = resid_grad + ring_scatter(lambda k: nt([back_rel[:, k]], w_attn))

    out_sent = spread_z(out_sum)

    spots = jnp.zeros((2, model_width), f32)
    spots = lax.dynamic_update_slice(spots, jnp.stack([gain_query, gain_key]), (0, head * head_size))
    gain_local = jnp.concatenate([jnp.stack([gain_attn_grad, gain_mlp_grad]), spots])
    shares = lax.all_to_all(gain_local.reshape(n, -1), EVERY, 0, 0, tiled=True)
    share = jnp.sum(shares, axis=0)
    gain_grads = lax.all_to_all(
        jnp.broadcast_to(share, (n, share.shape[0])), EVERY, 0, 0, tiled=True
    ).reshape(gain_local.shape)

    flat = [heads_sent, out_sent, gate_sent, up_sent, down_sent]
    sent = jnp.concatenate([a.reshape(-1, rows, side) for a in flat])
    split = gateup_list.reshape(Z, D, 2, -1)
    order = [out_list, split[:, :, 0], split[:, :, 1], down_list]
    order = [jnp.take(o.reshape(Z, -1), relative, axis=0, mode="clip").reshape(-1) for o in order]
    order = jnp.concatenate([number[: 3 * square]] + order)
    where_is = jnp.zeros((total_blocks,), jnp.int32).at[order].set(number)
    to_slots = jnp.take(sent, where_is[owner_map] + zero_of(input_grad), axis=0, mode="clip")
    got = lax.all_to_all(to_slots, EVERY, 0, 0, tiled=True)
    got = got.reshape(Z, PN, S, slots, rows, side).transpose(3, 1, 2, 0, 4, 5)
    grad_slots, left_new, right_new, new_weights = shampoo(
        got.reshape(slots, side, side), left_stats, right_stats, left_root, right_root, weights
    )
    new_gains = norm_gains - gain_rate * gain_grads * lax.rsqrt(
        jnp.mean(gain_grads * gain_grads, axis=1, keepdims=True) + epsilon
    )
    return (
        output,
        input_grad[None],
        grad_slots,
        left_new,
        right_new,
        new_weights,
        gain_grads,
        new_gains,
    )


def solution(mesh):
    heads, seqs = mesh.shape["head"], mesh.shape["seq"]
    fine = Mesh(mesh.devices.reshape(Z, heads // Z, seqs), EVERY)
    tok = P("seq", GROUP, None)
    slot = P(EVERY, None, None)
    return jax.shard_map(
        body,
        mesh=fine,
        in_specs=(tok, tok, P("seq", GROUP), P(), slot, P(), slot, slot, slot, slot),
        out_specs=(tok, tok, slot, slot, slot, slot, P(), P()),
        check_vma=False,
    )
```

time: 1180 us -> 1120 us (0.949)
  blocking collectives: 106 us -> 28.3 us
  local copies, waits for them, and re-layouts: 115 us -> 143 us
  matrix products: 27.7 us -> 0 us
  Pallas kernels: 223 us -> 202 us
  other arithmetic: 49.2 us -> 63.6 us
  waiting for transfers between devices: 522 us -> 535 us
    all_to_all x1, waiting for transfers between devices: 162 us -> 18.5 us  [body(): spread = lax.all_to_all(low, EVERY, 0, 0, tiled=True)]
    ppermute x9 -> x35, waiting for transfers between devices: 78.2 us -> 185 us  [the longest x18 96.4 us: exchange_z(): lax.ppermute(part_for(j), 'hz', [(i, (i + j) % Z) for i in range(Z)])]
    all_gather x5 -> x4, waiting for transfers between devices: 5.75 us -> 102 us  [the longest x1 102 us: body(): tokens_g = lax.all_gather(inputs, 'hz', axis=0, tiled=True)]
    all_to_all x11 -> x6, waiting for transfers between devices: 131 us -> 36.9 us  [the longest x2 36.9 us: to_heads(): got = lax.all_to_all(shaped, 'hp', 0, 0, tiled=True)]
    all_to_all x1, waiting for transfers between devices: 0.01 us -> 91.8 us  [body(): got = lax.all_to_all(to_slots, EVERY, 0, 0, tiled=True)]
    all_to_all x2 -> x1, blocking collectives: 106 us -> 28.3 us  [fetch(): got = lax.all_to_all(picked, 'hz', 0, 0, tiled=True)]
    reduce_scatter x3, waiting for transfers between devices: 52.8 us -> 0.02 us  [sum_plane(): lax.psum_scatter(blocks_of(pieces), ('hp', 'seq'), scatter_dimension=0, t...]
    ppermute x9 -> x35, starting transfers between devices: 7.04 us -> 45.1 us  [the longest x18 35.1 us: exchange_z(): lax.ppermute(part_for(j), 'hz', [(i, (i + j) % Z) for i in range(Z)])]
  transfers between devices with their start and end apart: 44 -> 68, of which waited for: 26 -> 32; matrix products, arithmetic and copies ran while one was open for 14% -> 15% of each run, Pallas kernels for 16% -> 14%
where the time goes in v3:
time: 1120 us; the launch traced here: 1110 us
  waiting for transfers between devices  535 us (48%)
  Pallas kernels  202 us (18%)
  local copies, waits for them, and re-layouts  143 us (13%)
  starting transfers between devices  116 us (10%)
  other arithmetic  63.6 us (6%)
  blocking collectives  28.3 us (3%)
  between operations  22.4 us (2%)
    all_gather x1, waiting for transfers between devices, body(): tokens_g = lax.all_gather(inputs, 'hz', axis=0, tiled=True)  102 us
    ppermute x18, waiting for transfers between devices, exchange_z(): lax.ppermute(part_for(j), 'hz', [(i, (i + j) % Z) for i in range(Z)])  96.4 us
    all_to_all x1, waiting for transfers between devices, body(): got = lax.all_to_all(to_slots, EVERY, 0, 0, tiled=True)  91.8 us
    ppermute x9, waiting for transfers between devices, ring_gather(): got = lax.ppermute(blocks[-1], 'hz', UP)  84.5 us
    ppermute x8, waiting for transfers between devices, ring_scatter(): lax.ppermute(total, 'hz', UP).astype(f32) + part_of(k)  73.7 us
    pallas_call x4, Pallas kernels, tn(): pl.pallas_call(functools.partial(tn_kernel, len(lefts), len(rights)), gri...  42.6 us
    pallas_call x7, Pallas kernels, nt(): pl.pallas_call(functools.partial(nt_kernel, len(xs)), grid=(steps,), in_s...  41.6 us
    all_to_all x2, waiting for transfers between devices, to_heads(): got = lax.all_to_all(shaped, 'hp', 0, 0, tiled=True)  36.9 us
  transfers between devices with their start and end apart: 68, of which 32 were waited for; matrix products, arithmetic and copies ran while one was open for 15% of the time, Pallas kernels for 14%

profile of v3, /device:TPU:0, one launch (start us, length us, event | category | flops | bytes accessed | tf_op | source)
XLA Modules:
  0.0 1109.6 jit_solution(2121227962180129456)
XLA Ops:
  25.1 102.1 %all-gather.11.cloned.1.call-done = bf16[1,512,2048]{2,1,0:T(8,128)(2,1)} async-done(((bf16[1,128,2048]{2,1,0:T(8,128)(2,1)}), bf16[1,512,2048]{2,1,0:T(8,128)(2,1)}) %all-gather.11.cloned.1.call-update) | async-done | bytes 2097168 | tf_op jit(solution)/shard_map/all_gather | solution.py:530
  129.8 18.5 %all-to-all-done = bf16[256,16,512]{2,1,0:T(8,128)(2,1)} async-done(((bf16[256,16,512]{2,1,0:T(8,128)(2,1)}), bf16[256,16,512]{2,1,0:T(8,128)(2,1)}, u32[]{:S(2)}, u32[]{:S(2)}) %all-to-all-start) | async-done | bytes 4194336 | tf_op jit(solution)/shard_map/all_to_all | solution.py:529
  151.1 28.3 %all_to_all.74 = bf16[64,16,512]{2,1,0:T(8,128)(2,1)S(1)} all-to-all(bf16[64,16,512]{2,1,0:T(8,128)(2,1)S(1)} %gather_fusion.1), channel_id=1, replica_groups=mesh['hz'=4,'hp'=4,'seq'=2] {'hz'}, dimensions={0} | all-to-all | bytes 2097152 | tf_op jit(solution)/shard_map/all_to_all | solution.py:542
  204.1 31.0 %collective-permute-done.8 = bf16[32,16,512]{2,1,0:T(8,128)(2,1)S(1)} collective-permute-done((bf16[32,16,512]{2,1,0:T(8,128)(2,1)S(1)}, bf16[32,16,512]{2,1,0:T(8,128)(2,1)S(1)}, u32[]{:S(2)}, u32[]{:S(2)}) %collective-permute-start.8) | collective-permute-done | bytes 524320 | tf_op jit(solution)/shard_map/ppermute | solution.py:435
  284.0 33.9 %all-to-all-done.2 = bf16[4,3,4,128,128]{4,3,2,1,0:T(8,128)(2,1)S(1)} async-done(((bf16[4,3,4,128,128]{4,3,2,1,0:T(8,128)(2,1)}), bf16[4,3,4,128,128]{4,3,2,1,0:T(8,128)(2,1)S(1)}, u32[]{:S(2)}, u32[]{:S(2)}) %all-to-all-start.2) | async-done | bytes 1572896 | tf_op jit(solution)/shard_map/all_to_all | solution.py:581
  324.5 10.2 shard_map.162
  376.8 12.1 %collective-permute-done = bf16[128,2048]{1,0:T(8,128)(2,1)S(1)} collective-permute-done((bf16[128,2048]{1,0:T(8,128)(2,1)S(1)}, bf16[128,2048]{1,0:T(8,128)(2,1)S(1)}, u32[]{:S(2)}, u32[]{:S(2)}) %collective-permute-start) | collective-permute-done | bytes 524320 | tf_op jit(solution)/shard_map/ppermute | solution.py:413
  427.5 14.7 %collective-permute-done.11.refs_0_.refs_2_ = bf16[128,2048]{1,0:T(8,128)(2,1)S(1)} collective-permute-done((bf16[128,2048]{1,0:T(8,128)(2,1)S(1)}, bf16[128,2048]{1,0:T(8,128)(2,1)S(1)}, u32[]{:S(2)}, u32[]{:S(2)}) %collective-permute-start.11) | collective-permute-done | bytes 524320 | tf_op jit(solution)/shard_map/ppermute | solution.py:405
  466.5 9.9 shard_map.170
  483.0 16.0 %collective-permute-done.15 = bf16[128,2048]{1,0:T(8,128)(2,1)S(1)} collective-permute-done((bf16[128,2048]{1,0:T(8,128)(2,1)S(1)}, bf16[128,2048]{1,0:T(8,128)(2,1)S(1)}, u32[]{:S(2)}, u32[]{:S(2)}) %collective-permute-start.15) | collective-permute-done | bytes 524320 | tf_op jit(solution)/shard_map/ppermute | solution.py:413
  500.9 13.5 %collective-permute-done.16 = bf16[128,2048]{1,0:T(8,128)(2,1)S(1)} collective-permute-done((bf16[128,2048]{1,0:T(8,128)(2,1)S(1)}, bf16[128,2048]{1,0:T(8,128)(2,1)S(1)}, u32[]{:S(2)}, u32[]{:S(2)}) %collective-permute-start.16) | collective-permute-done | bytes 524320 | tf_op jit(solution)/shard_map/ppermute | solution.py:414
  516.9 14.3 %collective-permute-done.17.refs_1_ = bf16[128,2048]{1,0:T(8,128)(2,1)S(1)} collective-permute-done((bf16[128,2048]{1,0:T(8,128)(2,1)S(1)}, bf16[128,2048]{1,0:T(8,128)(2,1)S(1)}, u32[]{:S(2)}, u32[]{:S(2)}) %collective-permute-start.17) | collective-permute-done | bytes 524320 | tf_op jit(solution)/shard_map/ppermute | solution.py:405
  531.2 13.3 %collective-permute-done.19.refs_0_ = bf16[128,2048]{1,0:T(8,128)(2,1)S(1)} collective-permute-done((bf16[128,2048]{1,0:T(8,128)(2,1)S(1)}, bf16[128,2048]{1,0:T(8,128)(2,1)S(1)}, u32[]{:S(2)}, u32[]{:S(2)}) %collective-permute-start.19) | collective-permute-done | bytes 524320 | tf_op jit(solution)/shard_map/ppermute | solution.py:405
  563.4 14.3 %shard_map.186 = bf16[8,4,4,64,512]{4,3,2,1,0:T(8,128)(2,1)} custom-call(bf16[128,2048]{1,0:T(8,128)(2,1)S(1)} %copy-done.6, bf16[128,2048]{1,0:T(8,128)(2,1)S(1)} %copy-done.15, bf16[128,2048]{1,0:T(8,128)(2,1)S(1)} %copy-done.18, bf16[128,2048]{1,0:T(8,128)(2,1)S(1)} %copy-done.21, bf16[2,256,2048]{2,1,0:T(8,128)(2,1)S(1)} %shard_map.174.refs_0_.refs_4_, ...), custom_call_target="tpu_custom_call" | custom-call | flops 429496736 | bytes 1468006 | tf_op jit(solution)/shard_map/pallas_call | solution.py:224
  582.0 14.7 %shard_map.187 = bf16[8,4,4,64,512]{4,3,2,1,0:T(8,128)(2,1)} custom-call(bf16[128,2048]{1,0:T(8,128)(2,1)S(1)} %copy-done.7, bf16[128,2048]{1,0:T(8,128)(2,1)S(1)} %copy-done.16, bf16[128,2048]{1,0:T(8,128)(2,1)S(1)} %copy-done.19, bf16[128,2048]{1,0:T(8,128)(2,1)S(1)} %copy-done.22, bf16[2,256,2048]{2,1,0:T(8,128)(2,1)S(1)} %shard_map.174.refs_0_.refs_4_, ...), custom_call_target="tpu_custom_call" | custom-call | flops 429496736 | bytes 1468006 | tf_op jit(solution)/shard_map/pallas_call | solution.py:224
  620.5 14.2 %collective-permute-done.23 = bf16[128,2048]{1,0:T(8,128)(2,1)S(1)} collective-permute-done((bf16[128,2048]{1,0:T(8,128)(2,1)S(1)}, bf16[128,2048]{1,0:T(8,128)(2,1)S(1)}, u32[]{:S(2)}, u32[]{:S(2)}) %collective-permute-start.23) | collective-permute-done | bytes 524320 | tf_op jit(solution)/shard_map/ppermute | solution.py:413
  635.7 11.3 %shard_map.188 = bf16[8,4,4,64,512]{4,3,2,1,0:T(8,128)(2,1)} custom-call(bf16[256,2048]{1,0:T(8,128)(2,1)S(1)} %copy-done.35, bf16[256,2048]{1,0:T(8,128)(2,1)S(1)} %copy-done.37, bf16[1,128,2048]{2,1,0:T(8,128)(2,1)S(1)} %bitcast.344, bf16[1,128,2048]{2,1,0:T(8,128)(2,1)S(1)} %bitcast.355, bf16[1,128,2048]{2,1,0:T(8,128)(2,1)S(1)} %bitcast.356, ...), custom_call_target="tpu_custom_call" | custom-call | flops 429496736 | bytes 1258291 | tf_op jit(solution)/shard_map/pallas_call | solution.py:224
  654.6 12.1 %collective-permute-done.25 = bf16[128,2048]{1,0:T(8,128)(2,1)S(1)} collective-permute-done((bf16[128,2048]{1,0:T(8,128)(2,1)S(1)}, bf16[128,2048]{1,0:T(8,128)(2,1)S(1)}, u32[]{:S(2)}, u32[]{:S(2)}) %collective-permute-start.25) | collective-permute-done | bytes 524320 | tf_op jit(solution)/shard_map/ppermute | solution.py:405
  705.7 11.7 %shard_map.179 = (bf16[2048,128]{1,0:T(8,128)(2,1)S(1)}, bf16[2048,128]{1,0:T(8,128)(2,1)S(1)}, bf16[2048,128]{1,0:T(8,128)(2,1)S(1)}) custom-call(bf16[2048,128]{1,0:T(8,128)(2,1)S(1)} %copy-done.30, bf16[2048,128]{1,0:T(8,128)(2,1)S(1)} %bitcast.358, bf16[2048,128]{1,0:T(8,128)(2,1)S(1)} %copy-done.32, bf16[2048,128]{1,0:T(8,128)(2,1)S(1)} %bitcast.348, ...), custom_call_target="tpu_custom_call" | custom-call | flops 335544320 | bytes 419430 | tf_op jit(solution)/shard_map/pallas_call | solution.py:350
  836.1 18.7 %collective-permute-done.29 = bf16[128,2048]{1,0:T(8,128)(2,1)S(1)} collective-permute-done((bf16[128,2048]{1,0:T(8,128)(2,1)S(1)}, bf16[128,2048]{1,0:T(8,128)(2,1)S(1)}, u32[]{:S(2)}, u32[]{:S(2)}) %collective-permute-start.29) | collective-permute-done | bytes 524320 | tf_op jit(solution)/shard_map/ppermute | solution.py:413
  908.4 16.2 %collective-permute-done.41 = bf16[16,16,512]{2,1,0:T(8,128)(2,1)} collective-permute-done((bf16[16,16,512]{2,1,0:T(8,128)(2,1)S(1)}, bf16[16,16,512]{2,1,0:T(8,128)(2,1)}, u32[]{:S(2)}, u32[]{:S(2)}) %collective-permute-start.41) | collective-permute-done | bytes 262176 | tf_op jit(solution)/shard_map/ppermute | solution.py:435
  941.8 15.8 %collective-permute-done.44 = bf16[16,16,512]{2,1,0:T(8,128)(2,1)S(1)} collective-permute-done((bf16[16,16,512]{2,1,0:T(8,128)(2,1)S(1)}, bf16[16,16,512]{2,1,0:T(8,128)(2,1)S(1)}, u32[]{:S(2)}, u32[]{:S(2)}) %collective-permute-start.44) | collective-permute-done | bytes 262176 | tf_op jit(solution)/shard_map/ppermute | solution.py:435
  981.4 91.8 %all-to-all-done.10 = bf16[256,16,512]{2,1,0:T(8,128)(2,1)} async-done(((bf16[256,16,512]{2,1,0:T(8,128)(2,1)}), bf16[256,16,512]{2,1,0:T(8,128)(2,1)}, u32[]{:S(2)}, u32[]{:S(2)}) %all-to-all-start.10) | async-done | bytes 4194336 | tf_op jit(solution)/shard_map/all_to_all | solution.py:739
  1076.1 26.2 %shard_map.189 = (f32[8,512,512]{2,1,0:T(8,128)}, f32[8,512,512]{2,1,0:T(8,128)}, f32[8,512,512]{2,1,0:T(8,128)}, f32[8,512,512]{2,1,0:T(8,128)}) custom-call(bf16[8,512,512]{2,1,0:T(8,128)(2,1)S(1)} %bitcast.336, f32[8,512,512]{2,1,0:T(8,128)} %ls_ref.1, f32[8,512,512]{2,1,0:T(8,128)} %rs_ref.1, f32[8,512,512]{2,1,0:T(8,128)} %lr_ref.1, ...), custom_call_target="tpu_custom_call" | custom-call | flops 858993472 | bytes 7969177 | tf_op jit(solution)/shard_map/pallas_call | solution.py:375
  (646 shorter events, 522.3 us)
Async XLA Ops:
  13.6 134.8 %all-to-all-start = ((bf16[256,16,512]{2,1,0:T(8,128)(2,1)}), bf16[256,16,512]{2,1,0:T(8,128)(2,1)}, u32[]{:S(2)}, u32[]{:S(2)}) async-start(bf16[256,16,512]{2,1,0:T(8,128)(2,1)} %bitcast.402), calls=%async_computation | async-start | bytes 8388608 | tf_op jit(solution)/shard_map/all_to_all | solution.py:529
  21.0 106.3 %all-gather.11.cloned.1.call-start = ((), (), s32[]{:S(2)}) async-start(), calls=%async_computation.21 | async-start | bytes 2621440 | tf_op jit(solution)/shard_map/all_gather | solution.py:530
  21.7 228.1 %all-gather.7.cloned.1.call-start = ((), (), s32[]{:S(2)}) async-start(), calls=%async_computation.16 | async-start | bytes 9437184 | tf_op jit(solution)/shard_map/all_gather | solution.py:546
  180.5 192.4 %all-gather.9.cloned.1.call-start = ((), (), s32[]{:S(2)}) async-start(), calls=%async_computation.17 | async-start | bytes 18874368 | tf_op jit(solution)/shard_map/all_gather | solution.py:546
  193.4 41.6 %collective-permute-start.8 = (bf16[32,16,512]{2,1,0:T(8,128)(2,1)S(1)}, bf16[32,16,512]{2,1,0:T(8,128)(2,1)S(1)}, u32[]{:S(2)}, u32[]{:S(2)}) collective-permute-start(bf16[32,16,512]{2,1,0:T(8,128)(2,1)S(1)} %gather_fusion.17), channel_id=1, source_target_pairs={{0,16},{8,24},{16,0},{24,8},{1,17},{9,25},{17,1},{25,9},{2,18},{10... | collective-permute-start | bytes 1572872 | tf_op jit(solution)/shard_map/ppermute | solution.py:435
  197.0 38.1 %collective-permute-start.7 = (bf16[32,16,512]{2,1,0:T(8,128)(2,1)S(1)}, bf16[32,16,512]{2,1,0:T(8,128)(2,1)}, u32[]{:S(2)}, u32[]{:S(2)}) collective-permute-start(bf16[32,16,512]{2,1,0:T(8,128)(2,1)S(1)} %gather_fusion.15), channel_id=1, source_target_pairs={{0,8},{8,16},{16,24},{24,0},{1,9},{9,17},{17,25},{25,1},{2,10},{10... | collective-permute-start | bytes 1572872 | tf_op jit(solution)/shard_map/ppermute | solution.py:435
  278.4 39.4 %all-to-all-start.2 = ((bf16[4,3,4,128,128]{4,3,2,1,0:T(8,128)(2,1)}), bf16[4,3,4,128,128]{4,3,2,1,0:T(8,128)(2,1)S(1)}, u32[]{:S(2)}, u32[]{:S(2)}) async-start(bf16[4,3,4,128,128]{4,3,2,1,0:T(8,128)(2,1)} %copy.182), calls=%async_computation.2 | async-start | bytes 3145728 | tf_op jit(solution)/shard_map/all_to_all | solution.py:581
  372.8 81.6 %all-gather.13.cloned.1.call-start = ((), (), s32[]{:S(2)}) async-start(), calls=%async_computation.22 | async-start | bytes 9437184 | tf_op jit(solution)/shard_map/all_gather | solution.py:546
  373.4 521.8 %reduce-scatter.4.cloned.1.call-start = ((), (), s32[]{:S(2)}) async-start(), calls=%async_computation.18 | async-start | bytes 9437184 | tf_op jit(solution)/shard_map/reduce_scatter | solution.py:652
  415.9 45.5 %collective-permute-start.13 = (bf16[4,64,2048]{2,1,0:T(8,128)(2,1)}, bf16[4,64,2048]{2,1,0:T(8,128)(2,1)}, u32[]{:S(2)}, u32[]{:S(2)}) collective-permute-start(bf16[4,64,2048]{2,1,0:T(8,128)(2,1)} %shard_map.171), channel_id=1, source_target_pairs={{0,2},{2,0},{4,6},{6,4},{1,3},{3,1},{5,7},{7,5},{8,10},{10,8},{12,... | collective-permute-start | bytes 3145736 | tf_op jit(solution)/shard_map/ppermute | solution.py:441
  417.6 45.3 %collective-permute-start.14 = (bf16[4,64,2048]{2,1,0:T(8,128)(2,1)}, bf16[4,64,2048]{2,1,0:T(8,128)(2,1)}, u32[]{:S(2)}, u32[]{:S(2)}) collective-permute-start(bf16[4,64,2048]{2,1,0:T(8,128)(2,1)} %shard_map.172), channel_id=1, source_target_pairs={{0,4},{2,6},{4,0},{6,2},{1,5},{3,7},{5,1},{7,3},{8,12},{10,14},{12... | collective-permute-start | bytes 3145736 | tf_op jit(solution)/shard_map/ppermute | solution.py:441
  499.2 51.9 %collective-permute-start.21 = (bf16[2,4,64,2048]{3,2,1,0:T(8,128)(2,1)S(1)}, bf16[2,4,64,2048]{3,2,1,0:T(8,128)(2,1)}, u32[]{:S(2)}, u32[]{:S(2)}) collective-permute-start(bf16[2,4,64,2048]{3,2,1,0:T(8,128)(2,1)S(1)} %pad_maximum_fusion.1), channel_id=1, source_target_pairs={{0,4},{2,6},{4,0},{6,2},{1,5},{3,7},{5,1},{7,3},{8,12},{10,14},{12... | collective-permute-start | bytes 6291464 | tf_op jit(solution)/shard_map/ppermute | solution.py:441
  500.9 50.1 %collective-permute-start.22 = (bf16[2,4,64,2048]{3,2,1,0:T(8,128)(2,1)S(1)}, bf16[2,4,64,2048]{3,2,1,0:T(8,128)(2,1)}, u32[]{:S(2)}, u32[]{:S(2)}) collective-permute-start(bf16[2,4,64,2048]{3,2,1,0:T(8,128)(2,1)S(1)} %copy-done.58), channel_id=1, source_target_pairs={{0,2},{2,0},{4,6},{6,4},{1,3},{3,1},{5,7},{7,5},{8,10},{10,8},{12,... | collective-permute-start | bytes 6291464 | tf_op jit(solution)/shard_map/ppermute | solution.py:441
  577.7 323.6 %reduce-scatter.6.cloned.1.call-start = ((), (), s32[]{:S(2)}) async-start(), calls=%async_computation.19 | async-start | bytes 9437184 | tf_op jit(solution)/shard_map/reduce_scatter | solution.py:652
  596.8 309.8 %reduce-scatter.8.cloned.1.call-start = ((), (), s32[]{:S(2)}) async-start(), calls=%async_computation.20 | async-start | bytes 9437184 | tf_op jit(solution)/shard_map/reduce_scatter | solution.py:652
  748.0 45.5 %all-to-all-start.8 = ((bf16[4,3,4,128,128]{4,3,2,1,0:T(8,128)(2,1)}), bf16[4,3,4,128,128]{4,3,2,1,0:T(8,128)(2,1)}, u32[]{:S(2)}, u32[]{:S(2)}) async-start(bf16[4,3,4,128,128]{4,3,2,1,0:T(8,128)(2,1)} %copy.203), calls=%async_computation.8 | async-start | bytes 3145728 | tf_op jit(solution)/shard_map/all_to_all | solution.py:587
  793.4 36.7 %collective-permute-start.36 = (bf16[2,64,512]{2,1,0:T(8,128)(2,1)}, bf16[2,64,512]{2,1,0:T(8,128)(2,1)}, u32[]{:S(2)}, u32[]{:S(2)}) collective-permute-start(bf16[2,64,512]{2,1,0:T(8,128)(2,1)} %slice_bitcast_fusion.6), channel_id=1, source_target_pairs={{0,2},{2,0},{4,6},{6,4},{1,3},{3,1},{5,7},{7,5},{8,10},{10,8},{12,... | collective-permute-start | bytes 393224 | tf_op jit(solution)/shard_map/ppermute | solution.py:441
  822.3 58.6 %all-to-all-start.9 = ((bf16[16,4,16,384]{3,2,1,0:T(8,128)(2,1)}), bf16[16,4,16,384]{3,2,1,0:T(8,128)(2,1)S(1)}, u32[]{:S(2)}, u32[]{:S(2)}) async-start(bf16[16,4,16,384]{3,2,1,0:T(8,128)(2,1)} %bitcast.428), calls=%async_computation.9 | async-start | bytes 1572864 | tf_op jit(solution)/shard_map/all_to_all | solution.py:709
  855.8 36.3 %collective-permute-start.30 = (bf16[128,2048]{1,0:T(8,128)(2,1)}, bf16[128,2048]{1,0:T(8,128)(2,1)}, u32[]{:S(2)}, u32[]{:S(2)}) collective-permute-start(bf16[128,2048]{1,0:T(8,128)(2,1)} %add_convert_fusion), channel_id=1, source_target_pairs={{0,8},{8,16},{16,24},{24,0},{1,9},{9,17},{17,25},{25,1},{2,10},{10... | collective-permute-start | bytes 1572872 | tf_op jit(solution)/shard_map/ppermute | solution.py:414
  881.5 92.8 %all-to-all-start.12 = ((f32[32,1,256]{2,1,0:T(1,128)}), f32[32,1,256]{2,1,0:T(1,128)}, u32[]{:S(2)}, u32[]{:S(2)}) async-start(f32[32,1,256]{2,1,0:T(1,128)} %broadcast_in_dim.151), calls=%async_computation.15 | async-start | bytes 65536 | tf_op jit(solution)/shard_map/all_to_all | solution.py:727
  902.7 38.4 %collective-permute-start.45 = (bf16[16,16,512]{2,1,0:T(8,128)(2,1)S(1)}, bf16[16,16,512]{2,1,0:T(8,128)(2,1)S(1)}, u32[]{:S(2)}, u32[]{:S(2)}) collective-permute-start(bf16[16,16,512]{2,1,0:T(8,128)(2,1)S(1)} %get-tuple-element.86), channel_id=1, source_target_pairs={{0,24},{8,0},{16,8},{24,16},{1,25},{9,1},{17,9},{25,17},{2,26},{10... | collective-permute-start | bytes 786440 | tf_op jit(solution)/shard_map/ppermute | solution.py:435
  905.5 52.1 %collective-permute-start.44 = (bf16[16,16,512]{2,1,0:T(8,128)(2,1)S(1)}, bf16[16,16,512]{2,1,0:T(8,128)(2,1)S(1)}, u32[]{:S(2)}, u32[]{:S(2)}) collective-permute-start(bf16[16,16,512]{2,1,0:T(8,128)(2,1)S(1)} %get-tuple-element.87), channel_id=1, source_target_pairs={{0,16},{8,24},{16,0},{24,8},{1,17},{9,25},{17,1},{25,9},{2,18},{10... | collective-permute-start | bytes 786440 | tf_op jit(solution)/shard_map/ppermute | solution.py:435
  907.9 49.7 %collective-permute-start.43 = (bf16[16,16,512]{2,1,0:T(8,128)(2,1)S(1)}, bf16[16,16,512]{2,1,0:T(8,128)(2,1)S(1)}, u32[]{:S(2)}, u32[]{:S(2)}) collective-permute-start(bf16[16,16,512]{2,1,0:T(8,128)(2,1)S(1)} %get-tuple-element.88), channel_id=1, source_target_pairs={{0,8},{8,16},{16,24},{24,0},{1,9},{9,17},{17,25},{25,1},{2,10},{10... | collective-permute-start | bytes 786440 | tf_op jit(solution)/shard_map/ppermute | solution.py:435
  974.2 99.0 %all-to-all-start.10 = ((bf16[256,16,512]{2,1,0:T(8,128)(2,1)}), bf16[256,16,512]{2,1,0:T(8,128)(2,1)}, u32[]{:S(2)}, u32[]{:S(2)}) async-start(bf16[256,16,512]{2,1,0:T(8,128)(2,1)} %gather_fusion.36), calls=%async_computation.13 | async-start | bytes 8388608 | tf_op jit(solution)/shard_map/all_to_all | solution.py:739
  (169 other events, 2225.5 us)
Sparse Core Ops, SparseCore 0:
  23.4 103.8 all-gather.10
  180.6 53.6 all-gather.6
  242.6 111.3 all-gather.8
  375.8 67.6 all-gather.12
  577.9 67.9 reduce-scatter.3
  650.2 78.2 reduce-scatter.5
  732.5 92.5 reduce-scatter.7

commit v4 on v3

--- a/solution.py
+++ b/solution.py
@@ -215,11 +215,16 @@
     y_ref[:, 0, 0] = mm_tn(left, right[0]).astype(bf16).reshape(rep, part, side)
 
 
-def tn(lefts, rights, rep, side, *others, only=None):
+def tn(lefts, rights, rep, side, *others, only=None, spare=0, base=None):
     R = lefts[0].shape[1] // side
     m, per = rights[0].shape[0], rights[0].shape[2] // side
     first, C = (0, m * per) if only is None else (only, per)
-    out = jax.ShapeDtypeStruct((rep, R, C, side // rep, side), bf16)
+    out = jax.ShapeDtypeStruct((rep, R + spare, C, side // rep, side), bf16)
+    start, aliases = 0, {}
+    if base is not None:
+        out = jax.ShapeDtypeStruct(base.shape, base.dtype)
+        start, others = base.shape[1] - R, (*others, base)
+        aliases = {len(lefts) + len(rights) + len(others) - 1: 0}
     total = sum(x.shape[0] for x in lefts)
     return pl.pallas_call(
         functools.partial(tn_kernel, len(lefts), len(rights)),
@@ -230,8 +235,9 @@
             for x in rights
         ]
         + [pl.BlockSpec(memory_space=pl.ANY)] * len(others),
-        out_specs=pl.BlockSpec((rep, 1, 1, side // rep, side), lambda r, c: (0, r, c, 0, 0)),
+        out_specs=pl.BlockSpec((rep, 1, 1, side // rep, side), lambda r, c: (0, start + r, c, 0, 0)),
         out_shape=out,
+        input_output_aliases=aliases,
         compiler_params=params(),
         cost_estimate=cost(2 * total * R * C * side * side, nbytes(*lefts, *rights, out)),
     )(*lefts, *rights, *others)
@@ -399,12 +405,15 @@
 UP = [(i, (i + 1) % Z) for i in range(Z)]
 
 
-def ring_gather(block, *others):
+def ring_gather(block, first_use=None):
     blocks = [block]
     for k in range(Z - 1):
-        got = lax.ppermute(blocks[-1], "hz", UP)
-        blocks.append(after(got, others[k]) if k < len(others) else got)
-    return blocks
+        blocks.append(lax.ppermute(blocks[-1], "hz", UP))
+        if k == 0 and first_use:
+            used = first_use(blocks[:2])
+        if k == 1 and first_use:
+            blocks[2] = after(blocks[2], used[0])
+    return (blocks, used) if first_use else blocks
 
 
 def ring_scatter(part_of):
@@ -611,7 +620,7 @@
     )
     resid = inputs.astype(f32) + rms_norm(attn_raw, norm_gains[0])
 
-    resid_blocks = ring_gather(resid.astype(bf16))
+    resid_blocks, near = ring_gather(resid.astype(bf16), lambda pair: gate_up(pair, w_gateup))
 
     tokens_z = tokens_g.reshape(Z, local_count, model_width)
     middle = local_count // 2
@@ -621,8 +630,7 @@
     tok_parts = [tok_one, swap(tok_one, 2), tok_two, swap(tok_two, 1)]
     tok_parts = [t.reshape(-1, model_width) for t in tok_parts]
     tok_near, tok_far = tok_parts[::2], tok_parts[1::2]
-    pairs = [resid_blocks[:2], resid_blocks[2:]]
-    gates, ups, hiddens = zip(*[gate_up(pair, w_gateup) for pair in pairs])
+    gates, ups, hiddens = zip(near, gate_up(resid_blocks[2:], w_gateup))
 
     def entry(halves, k):
         return halves[k // 2][k % 2 * local_count : (k % 2 + 1) * local_count]
@@ -634,11 +642,12 @@
     upstream = cotangent[0].astype(f32)
     _, down_norm_back = jax.vjp(rms_norm, down_raw, norm_gains[1])
     down_grad, gain_mlp_grad = down_norm_back(upstream)
-    down_blocks = ring_gather(down_grad.astype(bf16))
-    gateup_grads = [
-        hidden_back(down_blocks[2 * i : 2 * i + 2], w_down, gates[i], ups[i], *[[], tok_far][i])
-        for i in range(2)
-    ]
+    down_blocks, near = ring_gather(
+        down_grad.astype(bf16),
+        lambda pair: [hidden_back(pair, w_down, gates[0], ups[0])],
+    )
+    gateup_grads = near + [hidden_back(down_blocks[2:], w_down, gates[1], ups[1], *tok_far)]
+
     def spread_z(summed):
         summed = summed.reshape(-1, Z, rows, side)
         return exchange_z(
@@ -653,13 +662,12 @@
             blocks_of(pieces), ("hp", "seq"), scatter_dimension=0, tiled=False
         )
 
-    down_pieces = tn(hiddens, [b[None] for b in down_blocks], rep, side)
+    down_pieces = tn(hiddens, [b[None] for b in down_blocks], rep, side, spare=quarter // side)
     gate_pieces = tn(resid_blocks, gateup_grads, rep, side, only=0)
     up_pieces = tn(resid_blocks, gateup_grads, rep, side, only=1)
     gate_sum = sum_plane(gate_pieces)
     up_sum = sum_plane(up_pieces)
-    down_sum = sum_plane(down_pieces)
-    resid_parts = [nt([grads], w_gateup) for grads in gateup_grads]
+    resid_parts = [nt([gateup_grads[0]], w_gateup), nt([gateup_grads[1]], w_gateup)]
     resid_grad = upstream + ring_scatter(lambda k: entry(resid_parts, k))
 
     _, attn_norm_back = jax.vjp(rms_norm, attn_raw, norm_gains[0])
@@ -670,10 +678,15 @@
     grad_rel = grad_rel.reshape(Z, local_count, quarter)
     grad_abs = jnp.take(grad_rel, relative, axis=0, mode="clip")
     grad_row = to_heads(grad_abs.reshape(1, group_tokens, quarter))[0]
-    out_pieces = tn(
-        [attended_rel[k] for k in range(Z)], [b[None] for b in attn_blocks], rep, side
-    )
-    out_sum = plane_scatter(blocks_of(out_pieces))
+    last_pieces = tn(
+        [attended_rel[k] for k in range(Z)],
+        [b[None] for b in attn_blocks],
+        rep,
+        side,
+        base=down_pieces,
+    )
+    last_sum = sum_plane(last_pieces)
+    gate_sent = spread_z(after(gate_sum, grad_abs))
     query_grad, key_grad, value_grad = attend_back(
         query_row,
         grad_row,
@@ -683,14 +696,13 @@
         log_sums,
         score_scale,
     )
-    gate_sent = spread_z(gate_sum)
-    up_sent, down_sent = spread_z(up_sum), spread_z(down_sum)
     query_turn, key_turn = rope(query_grad.astype(f32), -1.0), rope(key_grad.astype(f32), -1.0)
     gain_query = jnp.sum(query_turn * query_hat, axis=0)
     gain_key = jnp.sum(key_turn * key_hat, axis=0)
     query_turn, key_turn = query_turn * gains_head[0], key_turn * gains_head[1]
     dots = jnp.stack([jnp.sum(query_turn * query_hat, -1), jnp.sum(key_turn * key_hat, -1)])
     dots = jnp.sum(from_group(dots).reshape(group, 2, length), axis=0) / model_width
+    up_sent, down_sent = spread_z(after(up_sum, dots)), spread_z(last_sum)
     dots = dots[..., None]
     query_back = ((query_turn - query_hat * dots[0]) * invs[0]).astype(bf16)
     key_back = ((key_turn - key_hat * dots[1]) * invs[1]).astype(bf16)
@@ -703,7 +715,7 @@
         return picked.reshape(-1, 3 * head_size)
 
     back_parts = [rows_of(0, 0, 1), rows_of(0, 2, 3), rows_of(1, 0, 2), rows_of(1, 1, 3)]
-    heads_grad = heads_tn(tok_parts, back_parts, rep, side)
+    heads_grad = heads_tn(tok_parts, back_parts, rep, side, gate_sent)
     heads_sum = sum_seq_scatter(heads_grad.reshape(PN, S, D, part, 3 * head_size), 1)
     heads_sum = heads_sum.reshape(PN, D, Z, rows, 3 * head_size).transpose(2, 0, 1, 3, 4)
     heads_sent = lax.all_to_all(
@@ -715,9 +727,10 @@
     back_rel = jnp.take(
         back_abs.reshape(3, Z, local_count, quarter), relative, axis=1, mode="clip"
     )
-    input_grad = resid_grad + ring_scatter(lambda k: nt([back_rel[:, k]], w_attn))
-
-    out_sent = spread_z(out_sum)
+    near_back = nt([back_rel[:, 0], back_rel[:, 1]], w_attn, up_sent, heads_grad)
+    back_parts = [near_back, nt([back_rel[:, 2], back_rel[:, 3]], w_attn)]
+    input_grad = resid_grad + ring_scatter(lambda k: entry(back_parts, k))
+
 
     spots = jnp.zeros((2, model_width), f32)
     spots = lax.dynamic_update_slice(spots, jnp.stack([gain_query, gain_key]), (0, head * head_size))
@@ -728,10 +741,11 @@
         jnp.broadcast_to(share, (n, share.shape[0])), EVERY, 0, 0, tiled=True
     ).reshape(gain_local.shape)
 
-    flat = [heads_sent, out_sent, gate_sent, up_sent, down_sent]
+    flat = [heads_sent, gate_sent, up_sent, down_sent]
     sent = jnp.concatenate([a.reshape(-1, rows, side) for a in flat])
     split = gateup_list.reshape(Z, D, 2, -1)
-    order = [out_list, split[:, :, 0], split[:, :, 1], down_list]
+    last = jnp.concatenate([down_list, out_list.reshape(Z, -1)], axis=1)
+    order = [split[:, :, 0], split[:, :, 1], last]
     order = [jnp.take(o.reshape(Z, -1), relative, axis=0, mode="clip").reshape(-1) for o in order]
     order = jnp.concatenate([number[: 3 * square]] + order)
     where_is = jnp.zeros((total_blocks,), jnp.int32).at[order].set(number)

time: 1120 us -> 1060 us (0.946)
  waiting for transfers between devices: 535 us -> 498 us
  local copies, waits for them, and re-layouts: 143 us -> 126 us
    ppermute x18 -> x15, waiting for transfers between devices: 96.4 us -> 40.1 us  [exchange_z(): lax.ppermute(part_for(j), 'hz', [(i, (i + j) % Z) for i in range(Z)])]
    ppermute x9, waiting for transfers between devices: 84.5 us -> 66.1 us  [ring_gather(): blocks.append(lax.ppermute(blocks[-1], 'hz', UP))]
    ppermute x8, waiting for transfers between devices: 73.7 us -> 55.5 us  [ring_scatter(): lax.ppermute(total, 'hz', UP).astype(f32) + part_of(k)]
    ppermute x8, starting transfers between devices: 4.68 us -> 19 us  [ring_scatter(): lax.ppermute(total, 'hz', UP).astype(f32) + part_of(k)]
    all_to_all x1, waiting for transfers between devices: 0.01 us -> 14.3 us  [body(): lax.all_to_all(heads_sum.reshape(group, D, rows, 3 * head_size), GROUP, 0...]
    ppermute x18 -> x15, starting transfers between devices: 35.1 us -> 21 us  [exchange_z(): lax.ppermute(part_for(j), 'hz', [(i, (i + j) % Z) for i in range(Z)])]
    all_to_all x2, waiting for transfers between devices: 0.01 us -> 13.5 us  [to_groups(): got = lax.all_to_all(shaped, 'hp', 0, 0, tiled=True)]
    ppermute x4, waiting for transfers between devices: 25.3 us -> 36.6 us  [ring_scatter(): return lax.ppermute(total, 'hz', UP).astype(f32) + part_of(0)]
  transfers between devices with their start and end apart: 68 -> 60, of which waited for: 32 -> 35; matrix products, arithmetic and copies ran while one was open for 15% -> 14% of each run, Pallas kernels for 14% -> 14%
where the time goes in v4:
time: 1060 us; the launch traced here: 1050 us
  waiting for transfers between devices  498 us (47%)
  Pallas kernels  196 us (18%)
  local copies, waits for them, and re-layouts  126 us (12%)
  starting transfers between devices  125 us (12%)
  other arithmetic  52.5 us (5%)
  blocking collectives  28.3 us (3%)
  between operations  22.1 us (2%)
    all_gather x1, waiting for transfers between devices, body(): tokens_g = lax.all_gather(inputs, 'hz', axis=0, tiled=True)  102 us
    all_to_all x1, waiting for transfers between devices, body(): got = lax.all_to_all(to_slots, EVERY, 0, 0, tiled=True)  91.8 us
    ppermute x9, waiting for transfers between devices, ring_gather(): blocks.append(lax.ppermute(blocks[-1], 'hz', UP))  66.1 us
    ppermute x8, waiting for transfers between devices, ring_scatter(): lax.ppermute(total, 'hz', UP).astype(f32) + part_of(k)  55.5 us
    pallas_call x4, Pallas kernels, tn(): pl.pallas_call(functools.partial(tn_kernel, len(lefts), len(rights)), gri...  47 us
    all_to_all x2, waiting for transfers between devices, to_heads(): got = lax.all_to_all(shaped, 'hp', 0, 0, tiled=True)  40.5 us
    ppermute x15, waiting for transfers between devices, exchange_z(): lax.ppermute(part_for(j), 'hz', [(i, (i + j) % Z) for i in range(Z)])  40.1 us
    ppermute x4, waiting for transfers between devices, ring_scatter(): return lax.ppermute(total, 'hz', UP).astype(f32) + part_of(0)  36.6 us
  transfers between devices with their start and end apart: 60, of which 35 were waited for; matrix products, arithmetic and copies ran while one was open for 14% of the time, Pallas kernels for 14%

profile of v4, /device:TPU:0, one launch (start us, length us, event | category | flops | bytes accessed | tf_op | source)
XLA Modules:
  0.0 1048.4 jit_solution(3836051092560128115)
XLA Ops:
  25.6 101.7 %all-gather.11.cloned.1.call-done = bf16[1,512,2048]{2,1,0:T(8,128)(2,1)} async-done(((bf16[1,128,2048]{2,1,0:T(8,128)(2,1)}), bf16[1,512,2048]{2,1,0:T(8,128)(2,1)}) %all-gather.11.cloned.1.call-update) | async-done | bytes 2097168 | tf_op jit(solution)/shard_map/all_gather | solution.py:539
  129.7 18.6 %all-to-all-done = bf16[256,16,512]{2,1,0:T(8,128)(2,1)} async-done(((bf16[256,16,512]{2,1,0:T(8,128)(2,1)}), bf16[256,16,512]{2,1,0:T(8,128)(2,1)}, u32[]{:S(2)}, u32[]{:S(2)}) %all-to-all-start) | async-done | bytes 4194336 | tf_op jit(solution)/shard_map/all_to_all | solution.py:538
  151.1 28.3 %all_to_all.74 = bf16[64,16,512]{2,1,0:T(8,128)(2,1)S(1)} all-to-all(bf16[64,16,512]{2,1,0:T(8,128)(2,1)S(1)} %gather_fusion.1), channel_id=1, replica_groups=mesh['hz'=4,'hp'=4,'seq'=2] {'hz'}, dimensions={0} | all-to-all | bytes 2097152 | tf_op jit(solution)/shard_map/all_to_all | solution.py:551
  206.4 20.4 %collective-permute-done.8 = bf16[32,16,512]{2,1,0:T(8,128)(2,1)S(1)} collective-permute-done((bf16[32,16,512]{2,1,0:T(8,128)(2,1)S(1)}, bf16[32,16,512]{2,1,0:T(8,128)(2,1)S(1)}, u32[]{:S(2)}, u32[]{:S(2)}) %collective-permute-start.8) | collective-permute-done | bytes 524320 | tf_op jit(solution)/shard_map/ppermute | solution.py:444
  235.5 14.5 %all-to-all-start.4 = ((s32[16,1,128]{2,1,0:T(1,128)}), s32[16,1,128]{2,1,0:T(1,128)S(1)}, u32[]{:S(2)}, u32[]{:S(2)}) async-start(s32[16,1,128]{2,1,0:T(1,128)} %broadcast_in_dim.125), calls=%async_computation.4 | async-start | bytes 16384 | tf_op jit(solution)/shard_map/all_to_all | solution.py:477
  284.2 33.8 %all-to-all-done.2 = bf16[4,3,4,128,128]{4,3,2,1,0:T(8,128)(2,1)S(1)} async-done(((bf16[4,3,4,128,128]{4,3,2,1,0:T(8,128)(2,1)}), bf16[4,3,4,128,128]{4,3,2,1,0:T(8,128)(2,1)S(1)}, u32[]{:S(2)}, u32[]{:S(2)}) %all-to-all-start.2) | async-done | bytes 1572896 | tf_op jit(solution)/shard_map/all_to_all | solution.py:590
  324.7 10.2 shard_map.162
  425.7 9.8 shard_map.167
  457.1 10.5 shard_map.171
  477.2 13.5 %collective-permute-done.15 = bf16[128,2048]{1,0:T(8,128)(2,1)S(1)} collective-permute-done((bf16[128,2048]{1,0:T(8,128)(2,1)S(1)}, bf16[128,2048]{1,0:T(8,128)(2,1)S(1)}, u32[]{:S(2)}, u32[]{:S(2)}) %collective-permute-start.15) | collective-permute-done | bytes 524320 | tf_op jit(solution)/shard_map/ppermute | solution.py:422
  492.7 13.0 %collective-permute-done.16 = bf16[128,2048]{1,0:T(8,128)(2,1)S(1)} collective-permute-done((bf16[128,2048]{1,0:T(8,128)(2,1)S(1)}, bf16[128,2048]{1,0:T(8,128)(2,1)S(1)}, u32[]{:S(2)}, u32[]{:S(2)}) %collective-permute-start.16) | collective-permute-done | bytes 524320 | tf_op jit(solution)/shard_map/ppermute | solution.py:423
  508.2 13.8 %collective-permute-done.17.refs_1_ = bf16[128,2048]{1,0:T(8,128)(2,1)S(1)} collective-permute-done((bf16[128,2048]{1,0:T(8,128)(2,1)S(1)}, bf16[128,2048]{1,0:T(8,128)(2,1)S(1)}, u32[]{:S(2)}, u32[]{:S(2)}) %collective-permute-start.17) | collective-permute-done | bytes 524320 | tf_op jit(solution)/shard_map/ppermute | solution.py:411
  557.0 14.6 %shard_map.184 = bf16[8,4,4,64,512]{4,3,2,1,0:T(8,128)(2,1)} custom-call(bf16[128,2048]{1,0:T(8,128)(2,1)S(1)} %copy-done.9, bf16[128,2048]{1,0:T(8,128)(2,1)S(1)} %copy-done.24, bf16[128,2048]{1,0:T(8,128)(2,1)S(1)} %copy-done.13, bf16[128,2048]{1,0:T(8,128)(2,1)} %collective-permute-done.12.refs_1_.refs_3_, bf16[2,256,2048]{2,1,0:T(8,128)(2,1)S(1)} %copy-done.1, ...), custom_call_target="tpu_custom_call" | custom-call | flops 429496736 | bytes 1468006 | tf_op jit(solution)/shard_map/pallas_call | solution.py:229
  575.0 15.0 %shard_map.182 = bf16[8,4,4,64,512]{4,3,2,1,0:T(8,128)(2,1)} custom-call(bf16[128,2048]{1,0:T(8,128)(2,1)S(1)} %copy-done.10, bf16[128,2048]{1,0:T(8,128)(2,1)S(1)} %copy-done.25, bf16[128,2048]{1,0:T(8,128)(2,1)S(1)} %copy-done.14, bf16[128,2048]{1,0:T(8,128)(2,1)} %collective-permute-done.12.refs_1_.refs_3_, bf16[2,256,2048]{2,1,0:T(8,128)(2,1)S(1)} %copy-done.1, ...), custom_call_target="tpu_custom_call" | custom-call | flops 429496736 | bytes 1468006 | tf_op jit(solution)/shard_map/pallas_call | solution.py:229
  611.6 13.3 %collective-permute-done.23 = bf16[128,2048]{1,0:T(8,128)(2,1)S(1)} collective-permute-done((bf16[128,2048]{1,0:T(8,128)(2,1)S(1)}, bf16[128,2048]{1,0:T(8,128)(2,1)S(1)}, u32[]{:S(2)}, u32[]{:S(2)}) %collective-permute-start.23) | collective-permute-done | bytes 524320 | tf_op jit(solution)/shard_map/ppermute | solution.py:422
  625.0 13.5 %collective-permute-done.24 = bf16[128,2048]{1,0:T(8,128)(2,1)S(1)} collective-permute-done((bf16[128,2048]{1,0:T(8,128)(2,1)S(1)}, bf16[128,2048]{1,0:T(8,128)(2,1)S(1)}, u32[]{:S(2)}, u32[]{:S(2)}) %collective-permute-start.24) | collective-permute-done | bytes 524320 | tf_op jit(solution)/shard_map/ppermute | solution.py:423
  639.5 15.7 %collective-permute-done.25 = bf16[128,2048]{1,0:T(8,128)(2,1)S(1)} collective-permute-done((bf16[128,2048]{1,0:T(8,128)(2,1)S(1)}, bf16[128,2048]{1,0:T(8,128)(2,1)S(1)}, u32[]{:S(2)}, u32[]{:S(2)}) %collective-permute-start.25) | collective-permute-done | bytes 524320 | tf_op jit(solution)/shard_map/ppermute | solution.py:411
  655.2 16.4 %collective-permute-done.26 = bf16[128,2048]{1,0:T(8,128)(2,1)S(1)} collective-permute-done((bf16[128,2048]{1,0:T(8,128)(2,1)S(1)}, bf16[128,2048]{1,0:T(8,128)(2,1)S(1)}, u32[]{:S(2)}, u32[]{:S(2)}) %collective-permute-start.26) | collective-permute-done | bytes 524320 | tf_op jit(solution)/shard_map/ppermute | solution.py:411
  671.6 14.2 %shard_map.189.refs_8_ = bf16[8,5,4,64,512]{4,3,2,1,0:T(8,128)(2,1)} custom-call(bf16[256,2048]{1,0:T(8,128)(2,1)S(1)} %copy-done.36, bf16[256,2048]{1,0:T(8,128)(2,1)S(1)} %copy-done.38, bf16[1,128,2048]{2,1,0:T(8,128)(2,1)S(1)} %bitcast.329, bf16[1,128,2048]{2,1,0:T(8,128)(2,1)S(1)} %bitcast.334, bf16[1,128,2048]{2,1,0:T(8,128)(2,1)} %bitcast.164.refs_4_, ...), custom_call_target="tpu_custom_call" | custom-call | flops 429496736 | bytes 1468006 | tf_op jit(solution)/shard_map/pallas_call | solution.py:229
  704.4 11.7 %shard_map.181 = (bf16[2048,128]{1,0:T(8,128)(2,1)S(1)}, bf16[2048,128]{1,0:T(8,128)(2,1)S(1)}, bf16[2048,128]{1,0:T(8,128)(2,1)S(1)}) custom-call(bf16[2048,128]{1,0:T(8,128)(2,1)S(1)} %copy-done.31, bf16[2048,128]{1,0:T(8,128)(2,1)S(1)} %bitcast.342, bf16[2048,128]{1,0:T(8,128)(2,1)S(1)} %copy-done.33, bf16[2048,128]{1,0:T(8,128)(2,1)S(1)} %bitcast.333, ...), custom_call_target="tpu_custom_call" | custom-call | flops 335544320 | bytes 419430 | tf_op jit(solution)/shard_map/pallas_call | solution.py:356
  763.8 13.5 %all-to-all-done.8 = bf16[4,3,4,128,128]{4,3,2,1,0:T(8,128)(2,1)} async-done(((bf16[4,3,4,128,128]{4,3,2,1,0:T(8,128)(2,1)}), bf16[4,3,4,128,128]{4,3,2,1,0:T(8,128)(2,1)}, u32[]{:S(2)}, u32[]{:S(2)}) %all-to-all-start.8) | async-done | bytes 1572896 | tf_op jit(solution)/shard_map/all_to_all | solution.py:596
  875.2 14.3 %all-to-all-done.9 = bf16[16,4,16,384]{3,2,1,0:T(8,128)(2,1)} async-done(((bf16[16,4,16,384]{3,2,1,0:T(8,128)(2,1)}), bf16[16,4,16,384]{3,2,1,0:T(8,128)(2,1)}, u32[]{:S(2)}, u32[]{:S(2)}) %all-to-all-start.9) | async-done | bytes 786464 | tf_op jit(solution)/shard_map/all_to_all | solution.py:721
  920.3 91.8 %all-to-all-done.10 = bf16[256,16,512]{2,1,0:T(8,128)(2,1)} async-done(((bf16[256,16,512]{2,1,0:T(8,128)(2,1)}), bf16[256,16,512]{2,1,0:T(8,128)(2,1)}, u32[]{:S(2)}, u32[]{:S(2)}) %all-to-all-start.10) | async-done | bytes 4194336 | tf_op jit(solution)/shard_map/all_to_all | solution.py:753
  1014.9 26.2 %shard_map.191 = (f32[8,512,512]{2,1,0:T(8,128)}, f32[8,512,512]{2,1,0:T(8,128)}, f32[8,512,512]{2,1,0:T(8,128)}, f32[8,512,512]{2,1,0:T(8,128)}) custom-call(bf16[8,512,512]{2,1,0:T(8,128)(2,1)S(1)} %bitcast.321, f32[8,512,512]{2,1,0:T(8,128)} %ls_ref.1, f32[8,512,512]{2,1,0:T(8,128)} %rs_ref.1, f32[8,512,512]{2,1,0:T(8,128)} %lr_ref.1, ...), custom_call_target="tpu_custom_call" | custom-call | flops 858993472 | bytes 7969177 | tf_op jit(solution)/shard_map/pallas_call | solution.py:381
  (580 shorter events, 478.2 us)
Async XLA Ops:
  13.6 134.8 %all-to-all-start = ((bf16[256,16,512]{2,1,0:T(8,128)(2,1)}), bf16[256,16,512]{2,1,0:T(8,128)(2,1)}, u32[]{:S(2)}, u32[]{:S(2)}) async-start(bf16[256,16,512]{2,1,0:T(8,128)(2,1)} %bitcast.382), calls=%async_computation | async-start | bytes 8388608 | tf_op jit(solution)/shard_map/all_to_all | solution.py:538
  21.0 106.3 %all-gather.11.cloned.1.call-start = ((), (), s32[]{:S(2)}) async-start(), calls=%async_computation.21 | async-start | bytes 2621440 | tf_op jit(solution)/shard_map/all_gather | solution.py:539
  21.7 228.3 %all-gather.7.cloned.1.call-start = ((), (), s32[]{:S(2)}) async-start(), calls=%async_computation.16 | async-start | bytes 9437184 | tf_op jit(solution)/shard_map/all_gather | solution.py:555
  180.5 189.9 %all-gather.9.cloned.1.call-start = ((), (), s32[]{:S(2)}) async-start(), calls=%async_computation.17 | async-start | bytes 18874368 | tf_op jit(solution)/shard_map/all_gather | solution.py:555
  192.5 34.4 %collective-permute-start.8 = (bf16[32,16,512]{2,1,0:T(8,128)(2,1)S(1)}, bf16[32,16,512]{2,1,0:T(8,128)(2,1)S(1)}, u32[]{:S(2)}, u32[]{:S(2)}) collective-permute-start(bf16[32,16,512]{2,1,0:T(8,128)(2,1)S(1)} %gather_fusion.17), channel_id=1, source_target_pairs={{0,16},{8,24},{16,0},{24,8},{1,17},{9,25},{17,1},{25,9},{2,18},{10... | collective-permute-start | bytes 1572872 | tf_op jit(solution)/shard_map/ppermute | solution.py:444
  197.1 29.7 %collective-permute-start.9 = (bf16[32,16,512]{2,1,0:T(8,128)(2,1)S(1)}, bf16[32,16,512]{2,1,0:T(8,128)(2,1)}, u32[]{:S(2)}, u32[]{:S(2)}) collective-permute-start(bf16[32,16,512]{2,1,0:T(8,128)(2,1)S(1)} %gather_fusion.19), channel_id=1, source_target_pairs={{0,24},{8,0},{16,8},{24,16},{1,25},{9,1},{17,9},{25,17},{2,26},{10... | collective-permute-start | bytes 1572872 | tf_op jit(solution)/shard_map/ppermute | solution.py:444
  235.5 26.9 %all-to-all-start.4 = ((s32[16,1,128]{2,1,0:T(1,128)}), s32[16,1,128]{2,1,0:T(1,128)S(1)}, u32[]{:S(2)}, u32[]{:S(2)}) async-start(s32[16,1,128]{2,1,0:T(1,128)} %broadcast_in_dim.125), calls=%async_computation.4 | async-start | bytes 16384 | tf_op jit(solution)/shard_map/all_to_all | solution.py:477
  278.6 39.4 %all-to-all-start.2 = ((bf16[4,3,4,128,128]{4,3,2,1,0:T(8,128)(2,1)}), bf16[4,3,4,128,128]{4,3,2,1,0:T(8,128)(2,1)S(1)}, u32[]{:S(2)}, u32[]{:S(2)}) async-start(bf16[4,3,4,128,128]{4,3,2,1,0:T(8,128)(2,1)} %copy.234), calls=%async_computation.2 | async-start | bytes 3145728 | tf_op jit(solution)/shard_map/all_to_all | solution.py:590
  335.9 29.0 %all-to-all-start.5 = ((bf16[4,1,4,128,128]{3,4,2,1,0:T(8,128)(2,1)}), bf16[4,1,4,128,128]{3,4,2,1,0:T(8,128)(2,1)}, u32[]{:S(2)}, u32[]{:S(2)}) async-start(bf16[4,1,4,128,128]{3,4,2,1,0:T(8,128)(2,1)} %bitcast.33), calls=%async_computation.5 | async-start | bytes 1048576 | tf_op jit(solution)/shard_map/all_to_all | solution.py:596
  370.4 74.3 %all-gather.13.cloned.1.call-start = ((), (), s32[]{:S(2)}) async-start(), calls=%async_computation.22 | async-start | bytes 9437184 | tf_op jit(solution)/shard_map/all_gather | solution.py:555
  370.9 381.3 %reduce-scatter.6.cloned.1.call-start = ((), (), s32[]{:S(2)}) async-start(), calls=%async_computation.19 | async-start | bytes 9437184 | tf_op jit(solution)/shard_map/reduce_scatter | solution.py:661
  415.2 37.6 %collective-permute-start.14 = (bf16[4,64,2048]{2,1,0:T(8,128)(2,1)}, bf16[4,64,2048]{2,1,0:T(8,128)(2,1)}, u32[]{:S(2)}, u32[]{:S(2)}) collective-permute-start(bf16[4,64,2048]{2,1,0:T(8,128)(2,1)} %shard_map.173), channel_id=1, source_target_pairs={{0,4},{2,6},{4,0},{6,2},{1,5},{3,7},{5,1},{7,3},{8,12},{10,14},{12... | collective-permute-start | bytes 3145736 | tf_op jit(solution)/shard_map/ppermute | solution.py:450
  416.8 38.7 %collective-permute-start.13 = (bf16[4,64,2048]{2,1,0:T(8,128)(2,1)}, bf16[4,64,2048]{2,1,0:T(8,128)(2,1)}, u32[]{:S(2)}, u32[]{:S(2)}) collective-permute-start(bf16[4,64,2048]{2,1,0:T(8,128)(2,1)} %shard_map.172), channel_id=1, source_target_pairs={{0,2},{2,0},{4,6},{6,4},{1,3},{3,1},{5,7},{7,5},{8,10},{10,8},{12,... | collective-permute-start | bytes 3145736 | tf_op jit(solution)/shard_map/ppermute | solution.py:450
  491.2 46.8 %collective-permute-start.22 = (bf16[2,4,64,2048]{3,2,1,0:T(8,128)(2,1)}, bf16[2,4,64,2048]{3,2,1,0:T(8,128)(2,1)}, u32[]{:S(2)}, u32[]{:S(2)}) collective-permute-start(bf16[2,4,64,2048]{3,2,1,0:T(8,128)(2,1)} %pad_maximum_fusion.3), channel_id=1, source_target_pairs={{0,2},{2,0},{4,6},{6,4},{1,3},{3,1},{5,7},{7,5},{8,10},{10,8},{12,... | collective-permute-start | bytes 6291464 | tf_op jit(solution)/shard_map/ppermute | solution.py:450
  492.7 46.2 %collective-permute-start.21 = (bf16[2,4,64,2048]{3,2,1,0:T(8,128)(2,1)S(1)}, bf16[2,4,64,2048]{3,2,1,0:T(8,128)(2,1)}, u32[]{:S(2)}, u32[]{:S(2)}) collective-permute-start(bf16[2,4,64,2048]{3,2,1,0:T(8,128)(2,1)S(1)} %pad_maximum_fusion.2), channel_id=1, source_target_pairs={{0,4},{2,6},{4,0},{6,2},{1,5},{3,7},{5,1},{7,3},{8,12},{10,14},{12... | collective-permute-start | bytes 6291464 | tf_op jit(solution)/shard_map/ppermute | solution.py:450
  571.6 212.0 %reduce-scatter.4.cloned.1.call-start = ((), (), s32[]{:S(2)}) async-start(), calls=%async_computation.18 | async-start | bytes 9437184 | tf_op jit(solution)/shard_map/reduce_scatter | solution.py:661
  590.0 279.1 %reduce-scatter.8.cloned.1.call-start = ((), (), s32[]{:S(2)}) async-start(), calls=%async_computation.20 | async-start | bytes 11796480 | tf_op jit(solution)/shard_map/reduce_scatter | solution.py:661
  743.8 33.6 %all-to-all-start.8 = ((bf16[4,3,4,128,128]{4,3,2,1,0:T(8,128)(2,1)}), bf16[4,3,4,128,128]{4,3,2,1,0:T(8,128)(2,1)}, u32[]{:S(2)}, u32[]{:S(2)}) async-start(bf16[4,3,4,128,128]{4,3,2,1,0:T(8,128)(2,1)} %copy.254), calls=%async_computation.8 | async-start | bytes 3145728 | tf_op jit(solution)/shard_map/all_to_all | solution.py:596
  754.4 32.6 %collective-permute-start.31 = (bf16[16,16,512]{2,1,0:T(8,128)(2,1)S(1)}, bf16[16,16,512]{2,1,0:T(8,128)(2,1)}, u32[]{:S(2)}, u32[]{:S(2)}) collective-permute-start(bf16[16,16,512]{2,1,0:T(8,128)(2,1)S(1)} %get-tuple-element.87), channel_id=1, source_target_pairs={{0,8},{8,16},{16,24},{24,0},{1,9},{9,17},{17,25},{25,1},{2,10},{10... | collective-permute-start | bytes 786440 | tf_op jit(solution)/shard_map/ppermute | solution.py:444
  847.7 41.8 %all-to-all-start.9 = ((bf16[16,4,16,384]{3,2,1,0:T(8,128)(2,1)}), bf16[16,4,16,384]{3,2,1,0:T(8,128)(2,1)}, u32[]{:S(2)}, u32[]{:S(2)}) async-start(bf16[16,4,16,384]{3,2,1,0:T(8,128)(2,1)} %bitcast.410), calls=%async_computation.11 | async-start | bytes 1572864 | tf_op jit(solution)/shard_map/all_to_all | solution.py:721
  871.3 31.4 %collective-permute-start.38 = (bf16[20,16,512]{2,1,0:T(8,128)(2,1)}, bf16[20,16,512]{2,1,0:T(8,128)(2,1)}, u32[]{:S(2)}, u32[]{:S(2)}) collective-permute-start(bf16[20,16,512]{2,1,0:T(8,128)(2,1)} %get-tuple-element.76), channel_id=1, source_target_pairs={{0,8},{8,16},{16,24},{24,0},{1,9},{9,17},{17,25},{25,1},{2,10},{10... | collective-permute-start | bytes 983048 | tf_op jit(solution)/shard_map/ppermute | solution.py:444
  871.3 31.4 %collective-permute-start.39 = (bf16[20,16,512]{2,1,0:T(8,128)(2,1)}, bf16[20,16,512]{2,1,0:T(8,128)(2,1)}, u32[]{:S(2)}, u32[]{:S(2)}) collective-permute-start(bf16[20,16,512]{2,1,0:T(8,128)(2,1)} %get-tuple-element.75), channel_id=1, source_target_pairs={{0,16},{8,24},{16,0},{24,8},{1,17},{9,25},{17,1},{25,9},{2,18},{10... | collective-permute-start | bytes 983048 | tf_op jit(solution)/shard_map/ppermute | solution.py:444
  873.1 29.7 %collective-permute-start.40 = (bf16[20,16,512]{2,1,0:T(8,128)(2,1)S(1)}, bf16[20,16,512]{2,1,0:T(8,128)(2,1)}, u32[]{:S(2)}, u32[]{:S(2)}) collective-permute-start(bf16[20,16,512]{2,1,0:T(8,128)(2,1)S(1)} %get-tuple-element.74), channel_id=1, source_target_pairs={{0,24},{8,0},{16,8},{24,16},{1,25},{9,1},{17,9},{25,17},{2,26},{10... | collective-permute-start | bytes 983048 | tf_op jit(solution)/shard_map/ppermute | solution.py:444
  911.4 100.6 %all-to-all-start.10 = ((bf16[256,16,512]{2,1,0:T(8,128)(2,1)}), bf16[256,16,512]{2,1,0:T(8,128)(2,1)}, u32[]{:S(2)}, u32[]{:S(2)}) async-start(bf16[256,16,512]{2,1,0:T(8,128)(2,1)} %gather_fusion.31), calls=%async_computation.13 | async-start | bytes 8388608 | tf_op jit(solution)/shard_map/all_to_all | solution.py:753
  (146 other events, 1950.9 us)
Sparse Core Ops, SparseCore 0:
  23.4 103.8 all-gather.10
  180.6 53.6 all-gather.6
  236.8 117.4 all-gather.8
  373.3 71.2 all-gather.12
  571.7 68.4 reduce-scatter.5
  644.5 74.0 reduce-scatter.3
  722.1 89.9 reduce-scatter.7

commit v5 on v4

--- a/solution.py
+++ b/solution.py
@@ -538,10 +538,7 @@
     spread = lax.all_to_all(low, EVERY, 0, 0, tiled=True)
     tokens_g = lax.all_gather(inputs, "hz", axis=0, tiled=True)
 
-    group = Z * PN
-    own_ids = segment_ids + zero_of(tokens_g)
-    row_ids = from_group(own_ids[0]).reshape(-1)
-    length = row_ids.shape[0]
+    group, group_tokens = Z * PN, Z * local_count
 
     def fetch(numbers, *others):
         places = inverse[numbers.reshape(-1)]
@@ -567,39 +564,41 @@
 
     w_gateup = all_plane(fetch_beside(gateup_list, got_attn), D)
 
+    def rope(values, sign):
+        first, second = values[:, :half_size], values[:, half_size:]
+        return jnp.concatenate(
+            [first * cosine - second * sine * sign, second * cosine + first * sine * sign], axis=-1
+        )
+
+    head = zi * PN + pi
+    gains_head = lax.dynamic_slice_in_dim(norm_gains[2:4], head * head_size, head_size, axis=1)
+
+    def to_heads(stack):
+        m = stack.shape[0]
+        shaped = stack.reshape(m, Z, local_count, PN, head_size).transpose(3, 0, 1, 2, 4)
+        got = lax.all_to_all(shaped, "hp", 0, 0, tiled=True)
+        return got.transpose(1, 2, 0, 3, 4).reshape(m, length, head_size)
+
+    def to_groups(stack):
+        m = stack.shape[0]
+        shaped = stack.reshape(m, Z, PN, local_count, head_size).transpose(2, 0, 1, 3, 4)
+        got = lax.all_to_all(shaped, "hp", 0, 0, tiled=True)
+        return got.transpose(1, 2, 3, 0, 4).reshape(m, group_tokens, quarter)
+
+    raw = nn(tokens_g, w_attn, columns=3)
+    raw_three = raw.reshape(group_tokens, 3, quarter).transpose(1, 0, 2)
+    squares = jnp.sum(raw_three[:2] * raw_three[:2], axis=-1)
+    ids = jnp.pad(segment_ids.astype(f32), ((0, 0), (0, group_tokens - local_count)))
+    shared = from_group(jnp.concatenate([squares, ids])).reshape(Z, PN, 3, Z, local_count)
+    squares, row_ids = shared[:, :, :2], shared[:, :, 2, 0].reshape(-1).astype(jnp.int32)
+    length = row_ids.shape[0]
     begins = begins_of(row_ids)
     places = jnp.arange(length, dtype=jnp.int32) - begins
     half_size = head_size // 2
     frequency = rope_base ** (-2.0 * jnp.arange(half_size, dtype=f32) / head_size)
     angles = places.astype(f32)[:, None] * frequency[None, :]
     cosine, sine = jnp.cos(angles), jnp.sin(angles)
-    group_tokens = Z * local_count
-
-    def rope(values, sign):
-        first, second = values[:, :half_size], values[:, half_size:]
-        return jnp.concatenate(
-            [first * cosine - second * sine * sign, second * cosine + first * sine * sign], axis=-1
-        )
-
-    head = zi * PN + pi
-    gains_head = lax.dynamic_slice_in_dim(norm_gains[2:4], head * head_size, head_size, axis=1)
-
-    def to_heads(stack):
-        m = stack.shape[0]
-        shaped = stack.reshape(m, Z, local_count, PN, head_size).transpose(3, 0, 1, 2, 4)
-        got = lax.all_to_all(shaped, "hp", 0, 0, tiled=True)
-        return got.transpose(1, 2, 0, 3, 4).reshape(m, length, head_size)
-
-    def to_groups(stack):
-        m = stack.shape[0]
-        shaped = stack.reshape(m, Z, PN, local_count, head_size).transpose(2, 0, 1, 3, 4)
-        got = lax.all_to_all(shaped, "hp", 0, 0, tiled=True)
-        return got.transpose(1, 2, 3, 0, 4).reshape(m, group_tokens, quarter)
-
-    raw = nn(tokens_g, w_attn, columns=3)
-    raw_three = raw.reshape(group_tokens, 3, quarter).transpose(1, 0, 2)
-    squares = jnp.sum(raw_three[:2] * raw_three[:2], axis=-1)
-    squares = from_group(squares).reshape(Z, PN, 2, Z, local_count)
+
     squares = jnp.sum(squares, axis=0).transpose(1, 2, 0, 3).reshape(2, length, 1)
     raw_row = to_heads(raw_three.astype(bf16))
     invs = lax.rsqrt(squares / model_width + epsilon)
@@ -608,16 +607,15 @@
     key_row = rope(key_hat * gains_head[1], 1.0).astype(bf16)
     value_row = raw_row[2]
 
-    got_down = fetch_beside(down_list, raw_row)
-    w_down = all_plane(after(got_down, w_gateup), F // Z)
+    got_down = fetch_beside(down_list, squares)
 
     begin_line = begins[None, :]
     mixed, log_sums = attend(query_row, key_row, value_row, begin_line, score_scale)
     attended = to_groups(mixed[None]).reshape(Z, local_count, quarter)
     attended_rel = jnp.take(attended, relative, axis=0, mode="clip")
-    attn_raw = ring_scatter(
-        lambda k: nn(attended_rel[k], w_attn, *([got_down] if k == 2 else []), row=3)
-    )
+    attn_parts = [nn(attended_rel[k], w_attn, row=3) for k in range(Z)]
+    attn_raw = ring_scatter(lambda k: attn_parts[k])
+    w_down = all_plane(after(got_down, w_gateup, attn_parts[1]), F // Z)
     resid = inputs.astype(f32) + rms_norm(attn_raw, norm_gains[0])
 
     resid_blocks, near = ring_gather(resid.astype(bf16), lambda pair: gate_up(pair, w_gateup))

time: 1060 us -> 1030 us (0.972)
  waiting for transfers between devices: 498 us -> 476 us
  starting transfers between devices: 125 us -> 112 us
    all_to_all x2, waiting for transfers between devices: 40.5 us -> 16 us  [to_heads(): got = lax.all_to_all(shaped, 'hp', 0, 0, tiled=True)]
    ppermute x8, starting transfers between devices: 19 us -> 5.38 us  [ring_scatter(): lax.ppermute(total, 'hz', UP).astype(f32) + part_of(k)]
    all_to_all x3 -> x2, starting transfers between devices: 27.4 us -> 20.8 us  [from_group(): return lax.all_to_all(spread, GROUP, 0, 0, tiled=True)]
  transfers between devices with their start and end apart: 60 -> 59, of which waited for: 35 -> 33; matrix products, arithmetic and copies ran while one was open for 14% -> 14% of each run, Pallas kernels for 14% -> 15%
where the time goes in v5:
time: 1030 us; the launch traced here: 1020 us
  waiting for transfers between devices  476 us (46%)
  Pallas kernels  195 us (19%)
  local copies, waits for them, and re-layouts  126 us (12%)
  starting transfers between devices  112 us (11%)
  other arithmetic  56.2 us (5%)
  blocking collectives  28.3 us (3%)
  between operations  22.2 us (2%)
    all_gather x1, waiting for transfers between devices, body(): tokens_g = lax.all_gather(inputs, 'hz', axis=0, tiled=True)  102 us
    all_to_all x1, waiting for transfers between devices, body(): got = lax.all_to_all(to_slots, EVERY, 0, 0, tiled=True)  91.8 us
    ppermute x9, waiting for transfers between devices, ring_gather(): blocks.append(lax.ppermute(blocks[-1], 'hz', UP))  69.8 us
    ppermute x8, waiting for transfers between devices, ring_scatter(): lax.ppermute(total, 'hz', UP).astype(f32) + part_of(k)  63.8 us
    pallas_call x4, Pallas kernels, tn(): pl.pallas_call(functools.partial(tn_kernel, len(lefts), len(rights)), gri...  46.8 us
    ppermute x4, waiting for transfers between devices, ring_scatter(): return lax.ppermute(total, 'hz', UP).astype(f32) + part_of(0)  39.3 us
    ppermute x15, waiting for transfers between devices, exchange_z(): lax.ppermute(part_for(j), 'hz', [(i, (i + j) % Z) for i in range(Z)])  33.1 us
    pallas_call x5, Pallas kernels, nt(): pl.pallas_call(functools.partial(nt_kernel, len(xs)), grid=(steps,), in_s...  31.3 us
  transfers between devices with their start and end apart: 59, of which 33 were waited for; matrix products, arithmetic and copies ran while one was open for 14% of the time, Pallas kernels for 15%

profile of v5, /device:TPU:0, one launch (start us, length us, event | category | flops | bytes accessed | tf_op | source)
XLA Modules:
  0.0 1015.8 jit_solution(6895560621453534583)
XLA Ops:
  25.5 101.8 %all-gather.11.cloned.1.call-done = bf16[1,512,2048]{2,1,0:T(8,128)(2,1)} async-done(((bf16[1,128,2048]{2,1,0:T(8,128)(2,1)}), bf16[1,512,2048]{2,1,0:T(8,128)(2,1)}) %all-gather.11.cloned.1.call-update) | async-done | bytes 2097168 | tf_op jit(solution)/shard_map/all_gather | solution.py:539
  129.8 18.5 %all-to-all-done = bf16[256,16,512]{2,1,0:T(8,128)(2,1)} async-done(((bf16[256,16,512]{2,1,0:T(8,128)(2,1)}), bf16[256,16,512]{2,1,0:T(8,128)(2,1)}, u32[]{:S(2)}, u32[]{:S(2)}) %all-to-all-start) | async-done | bytes 4194336 | tf_op jit(solution)/shard_map/all_to_all | solution.py:538
  151.1 28.3 %all_to_all.65 = bf16[64,16,512]{2,1,0:T(8,128)(2,1)S(1)} all-to-all(bf16[64,16,512]{2,1,0:T(8,128)(2,1)S(1)} %gather_fusion.1), channel_id=1, replica_groups=mesh['hz'=4,'hp'=4,'seq'=2] {'hz'}, dimensions={0} | all-to-all | bytes 2097152 | tf_op jit(solution)/shard_map/all_to_all | solution.py:548
  206.5 20.4 %collective-permute-done.5 = bf16[32,16,512]{2,1,0:T(8,128)(2,1)S(1)} collective-permute-done((bf16[32,16,512]{2,1,0:T(8,128)(2,1)S(1)}, bf16[32,16,512]{2,1,0:T(8,128)(2,1)S(1)}, u32[]{:S(2)}, u32[]{:S(2)}) %collective-permute-start.5) | collective-permute-done | bytes 524320 | tf_op jit(solution)/shard_map/ppermute | solution.py:444
  250.3 15.0 %all-to-all-start.3 = ((f32[16,3,512]{2,1,0:T(4,128)}), f32[16,3,512]{2,1,0:T(4,128)S(1)}, u32[]{:S(2)}, u32[]{:S(2)}) async-start(f32[16,3,512]{2,1,0:T(4,128)} %broadcast_in_dim.121), calls=%async_computation.3 | async-start | bytes 262144 | tf_op jit(solution)/shard_map/all_to_all | solution.py:477
  339.1 11.6 %all-gather.9.cloned.1.call-done = bf16[8,32,64,512]{3,2,1,0:T(8,128)(2,1)} async-done(((bf16[1,32,64,512]{3,2,1,0:T(8,128)(2,1)}), bf16[8,32,64,512]{3,2,1,0:T(8,128)(2,1)}) %all-gather.9.cloned.1.call-update) | async-done | bytes 16777232 | tf_op jit(solution)/shard_map/all_gather | solution.py:552
  356.5 11.5 %collective-permute-done = bf16[128,2048]{1,0:T(8,128)(2,1)S(1)} collective-permute-done((bf16[128,2048]{1,0:T(8,128)(2,1)S(1)}, bf16[128,2048]{1,0:T(8,128)(2,1)S(1)}, u32[]{:S(2)}, u32[]{:S(2)}) %collective-permute-start) | collective-permute-done | bytes 524320 | tf_op jit(solution)/shard_map/ppermute | solution.py:422
  371.1 12.1 %collective-permute-done.1 = bf16[128,2048]{1,0:T(8,128)(2,1)S(1)} collective-permute-done((bf16[128,2048]{1,0:T(8,128)(2,1)S(1)}, bf16[128,2048]{1,0:T(8,128)(2,1)S(1)}, u32[]{:S(2)}, u32[]{:S(2)}) %collective-permute-start.1) | collective-permute-done | bytes 524320 | tf_op jit(solution)/shard_map/ppermute | solution.py:422
  459.7 16.2 %collective-permute-done.15 = bf16[128,2048]{1,0:T(8,128)(2,1)S(1)} collective-permute-done((bf16[128,2048]{1,0:T(8,128)(2,1)S(1)}, bf16[128,2048]{1,0:T(8,128)(2,1)S(1)}, u32[]{:S(2)}, u32[]{:S(2)}) %collective-permute-start.15) | collective-permute-done | bytes 524320 | tf_op jit(solution)/shard_map/ppermute | solution.py:422
  478.4 13.0 %collective-permute-done.16 = bf16[128,2048]{1,0:T(8,128)(2,1)S(1)} collective-permute-done((bf16[128,2048]{1,0:T(8,128)(2,1)S(1)}, bf16[128,2048]{1,0:T(8,128)(2,1)S(1)}, u32[]{:S(2)}, u32[]{:S(2)}) %collective-permute-start.16) | collective-permute-done | bytes 524320 | tf_op jit(solution)/shard_map/ppermute | solution.py:423
  494.0 14.3 %collective-permute-done.17.refs_1_ = bf16[128,2048]{1,0:T(8,128)(2,1)S(1)} collective-permute-done((bf16[128,2048]{1,0:T(8,128)(2,1)S(1)}, bf16[128,2048]{1,0:T(8,128)(2,1)S(1)}, u32[]{:S(2)}, u32[]{:S(2)}) %collective-permute-start.17) | collective-permute-done | bytes 524320 | tf_op jit(solution)/shard_map/ppermute | solution.py:411
  522.1 11.2 %collective-permute-done.20.refs_1_ = bf16[128,2048]{1,0:T(8,128)(2,1)S(1)} collective-permute-done((bf16[128,2048]{1,0:T(8,128)(2,1)}, bf16[128,2048]{1,0:T(8,128)(2,1)S(1)}, u32[]{:S(2)}, u32[]{:S(2)}) %collective-permute-start.20) | collective-permute-done | bytes 524320 | tf_op jit(solution)/shard_map/ppermute | solution.py:411
  543.0 14.6 %shard_map.184 = bf16[8,4,4,64,512]{4,3,2,1,0:T(8,128)(2,1)} custom-call(bf16[128,2048]{1,0:T(8,128)(2,1)S(1)} %copy-done.10, bf16[128,2048]{1,0:T(8,128)(2,1)S(1)} %copy-done.25, bf16[128,2048]{1,0:T(8,128)(2,1)S(1)} %copy-done.14, bf16[128,2048]{1,0:T(8,128)(2,1)} %collective-permute-done.12.refs_1_.refs_3_, bf16[2,256,2048]{2,1,0:T(8,128)(2,1)S(1)} %copy-done.1, ...), custom_call_target="tpu_custom_call" | custom-call | flops 429496736 | bytes 1468006 | tf_op jit(solution)/shard_map/pallas_call | solution.py:229
  560.9 14.9 %shard_map.182 = bf16[8,4,4,64,512]{4,3,2,1,0:T(8,128)(2,1)} custom-call(bf16[128,2048]{1,0:T(8,128)(2,1)S(1)} %copy-done.11, bf16[128,2048]{1,0:T(8,128)(2,1)S(1)} %copy-done.26, bf16[128,2048]{1,0:T(8,128)(2,1)S(1)} %copy-done.15, bf16[128,2048]{1,0:T(8,128)(2,1)} %collective-permute-done.12.refs_1_.refs_3_, bf16[2,256,2048]{2,1,0:T(8,128)(2,1)S(1)} %copy-done.1, ...), custom_call_target="tpu_custom_call" | custom-call | flops 429496736 | bytes 1468006 | tf_op jit(solution)/shard_map/pallas_call | solution.py:229
  598.1 12.2 %collective-permute-done.23 = bf16[128,2048]{1,0:T(8,128)(2,1)S(1)} collective-permute-done((bf16[128,2048]{1,0:T(8,128)(2,1)S(1)}, bf16[128,2048]{1,0:T(8,128)(2,1)S(1)}, u32[]{:S(2)}, u32[]{:S(2)}) %collective-permute-start.23) | collective-permute-done | bytes 524320 | tf_op jit(solution)/shard_map/ppermute | solution.py:422
  610.5 13.3 %collective-permute-done.24 = bf16[128,2048]{1,0:T(8,128)(2,1)S(1)} collective-permute-done((bf16[128,2048]{1,0:T(8,128)(2,1)S(1)}, bf16[128,2048]{1,0:T(8,128)(2,1)S(1)}, u32[]{:S(2)}, u32[]{:S(2)}) %collective-permute-start.24) | collective-permute-done | bytes 524320 | tf_op jit(solution)/shard_map/ppermute | solution.py:423
  624.8 12.1 %collective-permute-done.25 = bf16[128,2048]{1,0:T(8,128)(2,1)S(1)} collective-permute-done((bf16[128,2048]{1,0:T(8,128)(2,1)S(1)}, bf16[128,2048]{1,0:T(8,128)(2,1)S(1)}, u32[]{:S(2)}, u32[]{:S(2)}) %collective-permute-start.25) | collective-permute-done | bytes 524320 | tf_op jit(solution)/shard_map/ppermute | solution.py:411
  636.9 11.0 %collective-permute-done.26 = bf16[128,2048]{1,0:T(8,128)(2,1)S(1)} collective-permute-done((bf16[128,2048]{1,0:T(8,128)(2,1)S(1)}, bf16[128,2048]{1,0:T(8,128)(2,1)S(1)}, u32[]{:S(2)}, u32[]{:S(2)}) %collective-permute-start.26) | collective-permute-done | bytes 524320 | tf_op jit(solution)/shard_map/ppermute | solution.py:411
  647.9 14.1 %shard_map.189.refs_8_ = bf16[8,5,4,64,512]{4,3,2,1,0:T(8,128)(2,1)} custom-call(bf16[256,2048]{1,0:T(8,128)(2,1)S(1)} %copy-done.37, bf16[256,2048]{1,0:T(8,128)(2,1)S(1)} %copy-done.39, bf16[1,128,2048]{2,1,0:T(8,128)(2,1)S(1)} %bitcast.324, bf16[1,128,2048]{2,1,0:T(8,128)(2,1)S(1)} %bitcast.329, bf16[1,128,2048]{2,1,0:T(8,128)(2,1)} %bitcast.162.refs_4_, ...), custom_call_target="tpu_custom_call" | custom-call | flops 429496736 | bytes 1468006 | tf_op jit(solution)/shard_map/pallas_call | solution.py:229
  673.7 11.9 %all-to-all-done.5 = bf16[4,1,4,128,128]{4,3,2,1,0:T(8,128)(2,1)S(1)} async-done(((bf16[4,1,4,128,128]{4,3,2,1,0:T(8,128)(2,1)}), bf16[4,1,4,128,128]{4,3,2,1,0:T(8,128)(2,1)S(1)}, u32[]{:S(2)}, u32[]{:S(2)}) %all-to-all-start.5) | async-done | bytes 524320 | tf_op jit(solution)/shard_map/all_to_all | solution.py:579
  685.7 11.7 %shard_map.181 = (bf16[2048,128]{1,0:T(8,128)(2,1)S(1)}, bf16[2048,128]{1,0:T(8,128)(2,1)S(1)}, bf16[2048,128]{1,0:T(8,128)(2,1)S(1)}) custom-call(bf16[2048,128]{1,0:T(8,128)(2,1)S(1)} %copy-done.32, bf16[2048,128]{1,0:T(8,128)(2,1)S(1)} %bitcast.337, bf16[2048,128]{1,0:T(8,128)(2,1)S(1)} %copy-done.30, bf16[2048,128]{1,0:T(8,128)(2,1)S(1)} %bitcast.328, ...), custom_call_target="tpu_custom_call" | custom-call | flops 335544320 | bytes 419430 | tf_op jit(solution)/shard_map/pallas_call | solution.py:356
  854.2 11.0 %all-to-all-start.11 = ((f32[32,1,256]{2,1,0:T(1,128)}), f32[32,1,256]{2,1,0:T(1,128)}, u32[]{:S(2)}, u32[]{:S(2)}) async-start(f32[32,1,256]{2,1,0:T(1,128)} %broadcast_in_dim.141), calls=%async_computation.14 | async-start | bytes 65536 | tf_op jit(solution)/shard_map/all_to_all | solution.py:738
  887.6 91.8 %all-to-all-done.9 = bf16[256,16,512]{2,1,0:T(8,128)(2,1)} async-done(((bf16[256,16,512]{2,1,0:T(8,128)(2,1)}), bf16[256,16,512]{2,1,0:T(8,128)(2,1)}, u32[]{:S(2)}, u32[]{:S(2)}) %all-to-all-start.9) | async-done | bytes 4194336 | tf_op jit(solution)/shard_map/all_to_all | solution.py:751
  982.3 26.2 %shard_map.191 = (f32[8,512,512]{2,1,0:T(8,128)}, f32[8,512,512]{2,1,0:T(8,128)}, f32[8,512,512]{2,1,0:T(8,128)}, f32[8,512,512]{2,1,0:T(8,128)}) custom-call(bf16[8,512,512]{2,1,0:T(8,128)(2,1)S(1)} %bitcast.316, f32[8,512,512]{2,1,0:T(8,128)} %ls_ref.1, f32[8,512,512]{2,1,0:T(8,128)} %rs_ref.1, f32[8,512,512]{2,1,0:T(8,128)} %lr_ref.1, ...), custom_call_target="tpu_custom_call" | custom-call | flops 858993472 | bytes 7969177 | tf_op jit(solution)/shard_map/pallas_call | solution.py:381
  (590 shorter events, 474.6 us)
Async XLA Ops:
  13.6 134.8 %all-to-all-start = ((bf16[256,16,512]{2,1,0:T(8,128)(2,1)}), bf16[256,16,512]{2,1,0:T(8,128)(2,1)}, u32[]{:S(2)}, u32[]{:S(2)}) async-start(bf16[256,16,512]{2,1,0:T(8,128)(2,1)} %bitcast.374), calls=%async_computation | async-start | bytes 8388608 | tf_op jit(solution)/shard_map/all_to_all | solution.py:538
  21.0 106.3 %all-gather.11.cloned.1.call-start = ((), (), s32[]{:S(2)}) async-start(), calls=%async_computation.20 | async-start | bytes 2621440 | tf_op jit(solution)/shard_map/all_gather | solution.py:539
  21.7 216.3 %all-gather.7.cloned.1.call-start = ((), (), s32[]{:S(2)}) async-start(), calls=%async_computation.15 | async-start | bytes 9437184 | tf_op jit(solution)/shard_map/all_gather | solution.py:552
  180.5 170.2 %all-gather.9.cloned.1.call-start = ((), (), s32[]{:S(2)}) async-start(), calls=%async_computation.16 | async-start | bytes 18874368 | tf_op jit(solution)/shard_map/all_gather | solution.py:552
  192.5 34.4 %collective-permute-start.5 = (bf16[32,16,512]{2,1,0:T(8,128)(2,1)S(1)}, bf16[32,16,512]{2,1,0:T(8,128)(2,1)S(1)}, u32[]{:S(2)}, u32[]{:S(2)}) collective-permute-start(bf16[32,16,512]{2,1,0:T(8,128)(2,1)S(1)} %gather_fusion.8), channel_id=1, source_target_pairs={{0,16},{8,24},{16,0},{24,8},{1,17},{9,25},{17,1},{25,9},{2,18},{10... | collective-permute-start | bytes 1572872 | tf_op jit(solution)/shard_map/ppermute | solution.py:444
  197.2 29.7 %collective-permute-start.6 = (bf16[32,16,512]{2,1,0:T(8,128)(2,1)S(1)}, bf16[32,16,512]{2,1,0:T(8,128)(2,1)}, u32[]{:S(2)}, u32[]{:S(2)}) collective-permute-start(bf16[32,16,512]{2,1,0:T(8,128)(2,1)S(1)} %gather_fusion.10), channel_id=1, source_target_pairs={{0,24},{8,0},{16,8},{24,16},{1,25},{9,1},{17,9},{25,17},{2,26},{10... | collective-permute-start | bytes 1572872 | tf_op jit(solution)/shard_map/ppermute | solution.py:444
  281.9 40.9 %collective-permute-start.7 = (bf16[16,16,512]{2,1,0:T(8,128)(2,1)S(1)}, bf16[16,16,512]{2,1,0:T(8,128)(2,1)S(1)}, u32[]{:S(2)}, u32[]{:S(2)}) collective-permute-start(bf16[16,16,512]{2,1,0:T(8,128)(2,1)S(1)} %gather_fusion.15), channel_id=1, source_target_pairs={{0,8},{8,16},{16,24},{24,0},{1,9},{9,17},{17,25},{25,1},{2,10},{10... | collective-permute-start | bytes 786440 | tf_op jit(solution)/shard_map/ppermute | solution.py:444
  285.5 37.3 %collective-permute-start.8 = (bf16[16,16,512]{2,1,0:T(8,128)(2,1)S(1)}, bf16[16,16,512]{2,1,0:T(8,128)(2,1)S(1)}, u32[]{:S(2)}, u32[]{:S(2)}) collective-permute-start(bf16[16,16,512]{2,1,0:T(8,128)(2,1)S(1)} %gather_fusion.17), channel_id=1, source_target_pairs={{0,16},{8,24},{16,0},{24,8},{1,17},{9,25},{17,1},{25,9},{2,18},{10... | collective-permute-start | bytes 786440 | tf_op jit(solution)/shard_map/ppermute | solution.py:444
  289.7 33.1 %collective-permute-start.9 = (bf16[16,16,512]{2,1,0:T(8,128)(2,1)S(1)}, bf16[16,16,512]{2,1,0:T(8,128)(2,1)}, u32[]{:S(2)}, u32[]{:S(2)}) collective-permute-start(bf16[16,16,512]{2,1,0:T(8,128)(2,1)S(1)} %gather_fusion.19), channel_id=1, source_target_pairs={{0,24},{8,0},{16,8},{24,16},{1,25},{9,1},{17,9},{25,17},{2,26},{10... | collective-permute-start | bytes 786440 | tf_op jit(solution)/shard_map/ppermute | solution.py:444
  319.7 105.7 %all-gather.13.cloned.1.call-start = ((), (), s32[]{:S(2)}) async-start(), calls=%async_computation.21 | async-start | bytes 9437184 | tf_op jit(solution)/shard_map/all_gather | solution.py:552
  350.7 383.8 %reduce-scatter.6.cloned.1.call-start = ((), (), s32[]{:S(2)}) async-start(), calls=%async_computation.18 | async-start | bytes 9437184 | tf_op jit(solution)/shard_map/reduce_scatter | solution.py:659
  401.2 30.6 %collective-permute-start.14 = (bf16[4,64,2048]{2,1,0:T(8,128)(2,1)}, bf16[4,64,2048]{2,1,0:T(8,128)(2,1)}, u32[]{:S(2)}, u32[]{:S(2)}) collective-permute-start(bf16[4,64,2048]{2,1,0:T(8,128)(2,1)} %shard_map.173), channel_id=1, source_target_pairs={{0,4},{2,6},{4,0},{6,2},{1,5},{3,7},{5,1},{7,3},{8,12},{10,14},{12... | collective-permute-start | bytes 3145736 | tf_op jit(solution)/shard_map/ppermute | solution.py:450
  402.0 32.8 %collective-permute-start.13 = (bf16[4,64,2048]{2,1,0:T(8,128)(2,1)}, bf16[4,64,2048]{2,1,0:T(8,128)(2,1)}, u32[]{:S(2)}, u32[]{:S(2)}) collective-permute-start(bf16[4,64,2048]{2,1,0:T(8,128)(2,1)} %shard_map.172), channel_id=1, source_target_pairs={{0,2},{2,0},{4,6},{6,4},{1,3},{3,1},{5,7},{7,5},{8,10},{10,8},{12,... | collective-permute-start | bytes 3145736 | tf_op jit(solution)/shard_map/ppermute | solution.py:450
  431.8 27.7 %collective-permute-start.10 = (bf16[128,2048]{1,0:T(8,128)(2,1)S(1)}, bf16[128,2048]{1,0:T(8,128)(2,1)S(1)}, u32[]{:S(2)}, u32[]{:S(2)}) collective-permute-start(bf16[128,2048]{1,0:T(8,128)(2,1)S(1)} %slice.521), channel_id=1, source_target_pairs={{0,8},{8,16},{16,24},{24,0},{1,9},{9,17},{17,25},{25,1},{2,10},{10... | collective-permute-start | bytes 1572872 | tf_op jit(solution)/shard_map/ppermute | solution.py:422
  476.3 45.8 %collective-permute-start.22 = (bf16[2,4,64,2048]{3,2,1,0:T(8,128)(2,1)}, bf16[2,4,64,2048]{3,2,1,0:T(8,128)(2,1)}, u32[]{:S(2)}, u32[]{:S(2)}) collective-permute-start(bf16[2,4,64,2048]{3,2,1,0:T(8,128)(2,1)} %pad_maximum_fusion.3), channel_id=1, source_target_pairs={{0,2},{2,0},{4,6},{6,4},{1,3},{3,1},{5,7},{7,5},{8,10},{10,8},{12,... | collective-permute-start | bytes 6291464 | tf_op jit(solution)/shard_map/ppermute | solution.py:450
  477.8 44.3 %collective-permute-start.21 = (bf16[2,4,64,2048]{3,2,1,0:T(8,128)(2,1)S(1)}, bf16[2,4,64,2048]{3,2,1,0:T(8,128)(2,1)}, u32[]{:S(2)}, u32[]{:S(2)}) collective-permute-start(bf16[2,4,64,2048]{3,2,1,0:T(8,128)(2,1)S(1)} %pad_maximum_fusion.2), channel_id=1, source_target_pairs={{0,4},{2,6},{4,0},{6,2},{1,5},{3,7},{5,1},{7,3},{8,12},{10,14},{12... | collective-permute-start | bytes 6291464 | tf_op jit(solution)/shard_map/ppermute | solution.py:450
  557.6 195.4 %reduce-scatter.4.cloned.1.call-start = ((), (), s32[]{:S(2)}) async-start(), calls=%async_computation.17 | async-start | bytes 9437184 | tf_op jit(solution)/shard_map/reduce_scatter | solution.py:659
  575.9 257.6 %reduce-scatter.8.cloned.1.call-start = ((), (), s32[]{:S(2)}) async-start(), calls=%async_computation.19 | async-start | bytes 11796480 | tf_op jit(solution)/shard_map/reduce_scatter | solution.py:659
  814.0 39.5 %all-to-all-start.8 = ((bf16[16,4,16,384]{3,2,1,0:T(8,128)(2,1)}), bf16[16,4,16,384]{3,2,1,0:T(8,128)(2,1)}, u32[]{:S(2)}, u32[]{:S(2)}) async-start(bf16[16,4,16,384]{3,2,1,0:T(8,128)(2,1)} %bitcast.403), calls=%async_computation.10 | async-start | bytes 1572864 | tf_op jit(solution)/shard_map/all_to_all | solution.py:719
  835.7 35.3 %collective-permute-start.38 = (bf16[20,16,512]{2,1,0:T(8,128)(2,1)}, bf16[20,16,512]{2,1,0:T(8,128)(2,1)}, u32[]{:S(2)}, u32[]{:S(2)}) collective-permute-start(bf16[20,16,512]{2,1,0:T(8,128)(2,1)} %get-tuple-element.73), channel_id=1, source_target_pairs={{0,8},{8,16},{16,24},{24,0},{1,9},{9,17},{17,25},{25,1},{2,10},{10... | collective-permute-start | bytes 983048 | tf_op jit(solution)/shard_map/ppermute | solution.py:444
  836.7 34.2 %collective-permute-start.39 = (bf16[20,16,512]{2,1,0:T(8,128)(2,1)}, bf16[20,16,512]{2,1,0:T(8,128)(2,1)}, u32[]{:S(2)}, u32[]{:S(2)}) collective-permute-start(bf16[20,16,512]{2,1,0:T(8,128)(2,1)} %get-tuple-element.72), channel_id=1, source_target_pairs={{0,16},{8,24},{16,0},{24,8},{1,17},{9,25},{17,1},{25,9},{2,18},{10... | collective-permute-start | bytes 983048 | tf_op jit(solution)/shard_map/ppermute | solution.py:444
  842.7 28.3 %collective-permute-start.40 = (bf16[20,16,512]{2,1,0:T(8,128)(2,1)S(1)}, bf16[20,16,512]{2,1,0:T(8,128)(2,1)}, u32[]{:S(2)}, u32[]{:S(2)}) collective-permute-start(bf16[20,16,512]{2,1,0:T(8,128)(2,1)S(1)} %get-tuple-element.71), channel_id=1, source_target_pairs={{0,24},{8,0},{16,8},{24,16},{1,25},{9,1},{17,9},{25,17},{2,26},{10... | collective-permute-start | bytes 983048 | tf_op jit(solution)/shard_map/ppermute | solution.py:444
  854.2 25.5 %all-to-all-start.11 = ((f32[32,1,256]{2,1,0:T(1,128)}), f32[32,1,256]{2,1,0:T(1,128)}, u32[]{:S(2)}, u32[]{:S(2)}) async-start(f32[32,1,256]{2,1,0:T(1,128)} %broadcast_in_dim.141), calls=%async_computation.14 | async-start | bytes 65536 | tf_op jit(solution)/shard_map/all_to_all | solution.py:738
  879.7 99.8 %all-to-all-start.9 = ((bf16[256,16,512]{2,1,0:T(8,128)(2,1)}), bf16[256,16,512]{2,1,0:T(8,128)(2,1)}, u32[]{:S(2)}, u32[]{:S(2)}) async-start(bf16[256,16,512]{2,1,0:T(8,128)(2,1)} %gather_fusion.31), calls=%async_computation.12 | async-start | bytes 8388608 | tf_op jit(solution)/shard_map/all_to_all | solution.py:751
  (145 other events, 1919.6 us)
Sparse Core Ops, SparseCore 0:
  23.4 103.8 all-gather.10
  180.6 53.6 all-gather.6
  236.8 113.8 all-gather.8
  353.0 57.3 all-gather.12
  557.7 68.5 reduce-scatter.5
  630.6 78.1 reduce-scatter.3
  712.3 81.5 reduce-scatter.7

commit v6 on v5

--- a/solution.py
+++ b/solution.py
@@ -212,13 +212,17 @@
     y_ref = refs[-1]
     rep, _, _, part, side = y_ref.shape
     left, right = join(refs[:lefts]), join(refs[lefts : lefts + rights])
-    y_ref[:, 0, 0] = mm_tn(left, right[0]).astype(bf16).reshape(rep, part, side)
+    whole_row = mm_tn(left, right[0]).astype(bf16)
+    for c in range(y_ref.shape[2]):
+        block = whole_row[:, c * side : (c + 1) * side]
+        y_ref[:, 0, c] = block.reshape(rep, part, side)
 
 
 def tn(lefts, rights, rep, side, *others, only=None, spare=0, base=None):
     R = lefts[0].shape[1] // side
     m, per = rights[0].shape[0], rights[0].shape[2] // side
-    first, C = (0, m * per) if only is None else (only, per)
+    first, steps = (0, m) if only is None else (only, 1)
+    C = steps * per
     out = jax.ShapeDtypeStruct((rep, R + spare, C, side // rep, side), bf16)
     start, aliases = 0, {}
     if base is not None:
@@ -228,14 +232,16 @@
     total = sum(x.shape[0] for x in lefts)
     return pl.pallas_call(
         functools.partial(tn_kernel, len(lefts), len(rights)),
-        grid=(R, C),
-        in_specs=[pl.BlockSpec((x.shape[0], side), lambda r, c: (0, r)) for x in lefts]
+        grid=(steps, R),
+        in_specs=[pl.BlockSpec((x.shape[0], side), lambda j, r: (0, r)) for x in lefts]
         + [
-            pl.BlockSpec((1, x.shape[1], side), lambda r, c: (first + c // per, 0, c % per))
+            pl.BlockSpec((1, x.shape[1], per * side), lambda j, r: (first + j, 0, 0))
             for x in rights
         ]
         + [pl.BlockSpec(memory_space=pl.ANY)] * len(others),
-        out_specs=pl.BlockSpec((rep, 1, 1, side // rep, side), lambda r, c: (0, start + r, c, 0, 0)),
+        out_specs=pl.BlockSpec(
+            (rep, 1, per, side // rep, side), lambda j, r: (0, start + r, j, 0, 0)
+        ),
         out_shape=out,
         input_output_aliases=aliases,
         compiler_params=params(),

time: 1030 us -> 1010 us (0.981)
  Pallas kernels: 195 us -> 175 us
    pallas_call x4, Pallas kernels: 46.8 us -> 26.4 us  [tn(): pl.pallas_call(functools.partial(tn_kernel, len(lefts), len(rights)), gri...]
  transfers between devices with their start and end apart: 59 -> 59, of which waited for: 33 -> 34; matrix products, arithmetic and copies ran while one was open for 14% -> 15% of each run, Pallas kernels for 15% -> 13%
where the time goes in v6:
time: 1010 us; the launch traced here: 996 us
  waiting for transfers between devices  486 us (48%)
  Pallas kernels  175 us (17%)
  local copies, waits for them, and re-layouts  126 us (12%)
  starting transfers between devices  103 us (10%)
  other arithmetic  55.7 us (6%)
  blocking collectives  28.3 us (3%)
  between operations  22.2 us (2%)
    all_gather x1, waiting for transfers between devices, body(): tokens_g = lax.all_gather(inputs, 'hz', axis=0, tiled=True)  102 us
    all_to_all x1, waiting for transfers between devices, body(): got = lax.all_to_all(to_slots, EVERY, 0, 0, tiled=True)  91.8 us
    ppermute x9, waiting for transfers between devices, ring_gather(): blocks.append(lax.ppermute(blocks[-1], 'hz', UP))  73.4 us
    ppermute x8, waiting for transfers between devices, ring_scatter(): lax.ppermute(total, 'hz', UP).astype(f32) + part_of(k)  62.9 us
    ppermute x4, waiting for transfers between devices, ring_scatter(): return lax.ppermute(total, 'hz', UP).astype(f32) + part_of(0)  37.9 us
    ppermute x15, waiting for transfers between devices, exchange_z(): lax.ppermute(part_for(j), 'hz', [(i, (i + j) % Z) for i in range(Z)])  33.1 us
    pallas_call x5, Pallas kernels, nt(): pl.pallas_call(functools.partial(nt_kernel, len(xs)), grid=(steps,), in_s...  31.5 us
    pallas_call x7, Pallas kernels, nn(): pl.pallas_call(nn_kernel, grid=(steps,), in_specs=[pl.BlockSpec(x.shape,...  29.3 us
  transfers between devices with their start and end apart: 59, of which 34 were waited for; matrix products, arithmetic and copies ran while one was open for 15% of the time, Pallas kernels for 13%

profile of v6, /device:TPU:0, one launch (start us, length us, event | category | flops | bytes accessed | tf_op | source)
XLA Modules:
  0.0 995.7 jit_solution(638614166760526371)
XLA Ops:
  25.5 101.8 %all-gather.11.cloned.1.call-done = bf16[1,512,2048]{2,1,0:T(8,128)(2,1)} async-done(((bf16[1,128,2048]{2,1,0:T(8,128)(2,1)}), bf16[1,512,2048]{2,1,0:T(8,128)(2,1)}) %all-gather.11.cloned.1.call-update) | async-done | bytes 2097168 | tf_op jit(solution)/shard_map/all_gather | solution.py:545
  129.8 18.5 %all-to-all-done = bf16[256,16,512]{2,1,0:T(8,128)(2,1)} async-done(((bf16[256,16,512]{2,1,0:T(8,128)(2,1)}), bf16[256,16,512]{2,1,0:T(8,128)(2,1)}, u32[]{:S(2)}, u32[]{:S(2)}) %all-to-all-start) | async-done | bytes 4194336 | tf_op jit(solution)/shard_map/all_to_all | solution.py:544
  151.1 28.3 %all_to_all.65 = bf16[64,16,512]{2,1,0:T(8,128)(2,1)S(1)} all-to-all(bf16[64,16,512]{2,1,0:T(8,128)(2,1)S(1)} %gather_fusion.1), channel_id=1, replica_groups=mesh['hz'=4,'hp'=4,'seq'=2] {'hz'}, dimensions={0} | all-to-all | bytes 2097152 | tf_op jit(solution)/shard_map/all_to_all | solution.py:554
  206.5 20.4 %collective-permute-done.5 = bf16[32,16,512]{2,1,0:T(8,128)(2,1)S(1)} collective-permute-done((bf16[32,16,512]{2,1,0:T(8,128)(2,1)S(1)}, bf16[32,16,512]{2,1,0:T(8,128)(2,1)S(1)}, u32[]{:S(2)}, u32[]{:S(2)}) %collective-permute-start.5) | collective-permute-done | bytes 524320 | tf_op jit(solution)/shard_map/ppermute | solution.py:450
  250.3 15.0 %all-to-all-start.3 = ((f32[16,3,512]{2,1,0:T(4,128)}), f32[16,3,512]{2,1,0:T(4,128)S(1)}, u32[]{:S(2)}, u32[]{:S(2)}) async-start(f32[16,3,512]{2,1,0:T(4,128)} %broadcast_in_dim.121), calls=%async_computation.3 | async-start | bytes 262144 | tf_op jit(solution)/shard_map/all_to_all | solution.py:483
  305.0 10.2 %shard_map.162 = (bf16[2048,128]{1,0:T(8,128)(2,1)S(1)}, f32[1,2048]{1,0:T(1,128)S(1)}) custom-call(bf16[2048,128]{1,0:T(8,128)(2,1)S(1)} %pad_maximum_fusion.11.q_ref, bf16[2048,128]{1,0:T(8,128)(2,1)S(1)} %pad_maximum_fusion.12.k_ref, bf16[2048,128]{1,0:T(8,128)(2,1)S(1)} %bitcast.327, s32[1,2048]{1,0:T(1,128)S(1)} %bitcast.344), custom_call_target="tpu_custom_call" | custom-call | flops 134217728 | bytes 209715 | tf_op jit(solution)/shard_map/pallas_call | solution.py:312
  339.1 11.6 %all-gather.9.cloned.1.call-done = bf16[8,32,64,512]{3,2,1,0:T(8,128)(2,1)} async-done(((bf16[1,32,64,512]{3,2,1,0:T(8,128)(2,1)}), bf16[8,32,64,512]{3,2,1,0:T(8,128)(2,1)}) %all-gather.9.cloned.1.call-update) | async-done | bytes 16777232 | tf_op jit(solution)/shard_map/all_gather | solution.py:558
  356.5 11.5 %collective-permute-done = bf16[128,2048]{1,0:T(8,128)(2,1)S(1)} collective-permute-done((bf16[128,2048]{1,0:T(8,128)(2,1)S(1)}, bf16[128,2048]{1,0:T(8,128)(2,1)S(1)}, u32[]{:S(2)}, u32[]{:S(2)}) %collective-permute-start) | collective-permute-done | bytes 524320 | tf_op jit(solution)/shard_map/ppermute | solution.py:428
  371.1 12.1 %collective-permute-done.1 = bf16[128,2048]{1,0:T(8,128)(2,1)S(1)} collective-permute-done((bf16[128,2048]{1,0:T(8,128)(2,1)S(1)}, bf16[128,2048]{1,0:T(8,128)(2,1)S(1)}, u32[]{:S(2)}, u32[]{:S(2)}) %collective-permute-start.1) | collective-permute-done | bytes 524320 | tf_op jit(solution)/shard_map/ppermute | solution.py:428
  387.0 10.5 %collective-permute-done.2 = bf16[128,2048]{1,0:T(8,128)(2,1)S(1)} collective-permute-done((bf16[128,2048]{1,0:T(8,128)(2,1)S(1)}, bf16[128,2048]{1,0:T(8,128)(2,1)S(1)}, u32[]{:S(2)}, u32[]{:S(2)}) %collective-permute-start.2) | collective-permute-done | bytes 524320 | tf_op jit(solution)/shard_map/ppermute | solution.py:429
  459.7 16.2 %collective-permute-done.15 = bf16[128,2048]{1,0:T(8,128)(2,1)S(1)} collective-permute-done((bf16[128,2048]{1,0:T(8,128)(2,1)S(1)}, bf16[128,2048]{1,0:T(8,128)(2,1)S(1)}, u32[]{:S(2)}, u32[]{:S(2)}) %collective-permute-start.15) | collective-permute-done | bytes 524320 | tf_op jit(solution)/shard_map/ppermute | solution.py:428
  478.4 13.0 %collective-permute-done.16 = bf16[128,2048]{1,0:T(8,128)(2,1)S(1)} collective-permute-done((bf16[128,2048]{1,0:T(8,128)(2,1)S(1)}, bf16[128,2048]{1,0:T(8,128)(2,1)S(1)}, u32[]{:S(2)}, u32[]{:S(2)}) %collective-permute-start.16) | collective-permute-done | bytes 524320 | tf_op jit(solution)/shard_map/ppermute | solution.py:429
  494.0 14.3 %collective-permute-done.17.refs_1_ = bf16[128,2048]{1,0:T(8,128)(2,1)S(1)} collective-permute-done((bf16[128,2048]{1,0:T(8,128)(2,1)S(1)}, bf16[128,2048]{1,0:T(8,128)(2,1)S(1)}, u32[]{:S(2)}, u32[]{:S(2)}) %collective-permute-start.17) | collective-permute-done | bytes 524320 | tf_op jit(solution)/shard_map/ppermute | solution.py:417
  522.1 11.2 %collective-permute-done.20.refs_1_ = bf16[128,2048]{1,0:T(8,128)(2,1)S(1)} collective-permute-done((bf16[128,2048]{1,0:T(8,128)(2,1)}, bf16[128,2048]{1,0:T(8,128)(2,1)S(1)}, u32[]{:S(2)}, u32[]{:S(2)}) %collective-permute-start.20) | collective-permute-done | bytes 524320 | tf_op jit(solution)/shard_map/ppermute | solution.py:417
  584.0 12.4 %collective-permute-done.23 = bf16[128,2048]{1,0:T(8,128)(2,1)S(1)} collective-permute-done((bf16[128,2048]{1,0:T(8,128)(2,1)S(1)}, bf16[128,2048]{1,0:T(8,128)(2,1)S(1)}, u32[]{:S(2)}, u32[]{:S(2)}) %collective-permute-start.23) | collective-permute-done | bytes 524320 | tf_op jit(solution)/shard_map/ppermute | solution.py:428
  596.5 12.4 %collective-permute-done.24 = bf16[128,2048]{1,0:T(8,128)(2,1)S(1)} collective-permute-done((bf16[128,2048]{1,0:T(8,128)(2,1)S(1)}, bf16[128,2048]{1,0:T(8,128)(2,1)S(1)}, u32[]{:S(2)}, u32[]{:S(2)}) %collective-permute-start.24) | collective-permute-done | bytes 524320 | tf_op jit(solution)/shard_map/ppermute | solution.py:429
  609.9 12.6 %collective-permute-done.25 = bf16[128,2048]{1,0:T(8,128)(2,1)S(1)} collective-permute-done((bf16[128,2048]{1,0:T(8,128)(2,1)S(1)}, bf16[128,2048]{1,0:T(8,128)(2,1)S(1)}, u32[]{:S(2)}, u32[]{:S(2)}) %collective-permute-start.25) | collective-permute-done | bytes 524320 | tf_op jit(solution)/shard_map/ppermute | solution.py:417
  622.5 11.0 %collective-permute-done.26 = bf16[128,2048]{1,0:T(8,128)(2,1)S(1)} collective-permute-done((bf16[128,2048]{1,0:T(8,128)(2,1)S(1)}, bf16[128,2048]{1,0:T(8,128)(2,1)S(1)}, u32[]{:S(2)}, u32[]{:S(2)}) %collective-permute-start.26) | collective-permute-done | bytes 524320 | tf_op jit(solution)/shard_map/ppermute | solution.py:417
  655.6 12.0 %all-to-all-done.5 = bf16[4,1,4,128,128]{4,3,2,1,0:T(8,128)(2,1)S(1)} async-done(((bf16[4,1,4,128,128]{4,3,2,1,0:T(8,128)(2,1)}), bf16[4,1,4,128,128]{4,3,2,1,0:T(8,128)(2,1)S(1)}, u32[]{:S(2)}, u32[]{:S(2)}) %all-to-all-start.5) | async-done | bytes 524320 | tf_op jit(solution)/shard_map/all_to_all | solution.py:585
  667.7 11.7 %shard_map.181 = (bf16[2048,128]{1,0:T(8,128)(2,1)S(1)}, bf16[2048,128]{1,0:T(8,128)(2,1)S(1)}, bf16[2048,128]{1,0:T(8,128)(2,1)S(1)}) custom-call(bf16[2048,128]{1,0:T(8,128)(2,1)S(1)} %copy-done.32, bf16[2048,128]{1,0:T(8,128)(2,1)S(1)} %bitcast.337, bf16[2048,128]{1,0:T(8,128)(2,1)S(1)} %copy-done.30, bf16[2048,128]{1,0:T(8,128)(2,1)S(1)} %bitcast.328, ...), custom_call_target="tpu_custom_call" | custom-call | flops 335544320 | bytes 419430 | tf_op jit(solution)/shard_map/pallas_call | solution.py:362
  691.2 10.3 %all-to-all-done.6 = f32[16,2,2048]{2,1,0:T(2,128)S(1)} async-done(((f32[16,2,2048]{2,1,0:T(2,128)}), f32[16,2,2048]{2,1,0:T(2,128)S(1)}, u32[]{:S(2)}, u32[]{:S(2)}) %all-to-all-start.6) | async-done | bytes 262176 | tf_op jit(solution)/shard_map/all_to_all | solution.py:483
  821.2 14.1 %all-to-all-done.8 = bf16[16,4,16,384]{3,2,1,0:T(8,128)(2,1)} async-done(((bf16[16,4,16,384]{3,2,1,0:T(8,128)(2,1)}), bf16[16,4,16,384]{3,2,1,0:T(8,128)(2,1)}, u32[]{:S(2)}, u32[]{:S(2)}) %all-to-all-start.8) | async-done | bytes 786464 | tf_op jit(solution)/shard_map/all_to_all | solution.py:725
  867.5 91.8 %all-to-all-done.9 = bf16[256,16,512]{2,1,0:T(8,128)(2,1)} async-done(((bf16[256,16,512]{2,1,0:T(8,128)(2,1)}), bf16[256,16,512]{2,1,0:T(8,128)(2,1)}, u32[]{:S(2)}, u32[]{:S(2)}) %all-to-all-start.9) | async-done | bytes 4194336 | tf_op jit(solution)/shard_map/all_to_all | solution.py:757
  962.2 26.2 %shard_map.191 = (f32[8,512,512]{2,1,0:T(8,128)}, f32[8,512,512]{2,1,0:T(8,128)}, f32[8,512,512]{2,1,0:T(8,128)}, f32[8,512,512]{2,1,0:T(8,128)}) custom-call(bf16[8,512,512]{2,1,0:T(8,128)(2,1)S(1)} %bitcast.316, f32[8,512,512]{2,1,0:T(8,128)} %ls_ref.1, f32[8,512,512]{2,1,0:T(8,128)} %rs_ref.1, f32[8,512,512]{2,1,0:T(8,128)} %lr_ref.1, ...), custom_call_target="tpu_custom_call" | custom-call | flops 858993472 | bytes 7969177 | tf_op jit(solution)/shard_map/pallas_call | solution.py:387
  (590 shorter events, 464.2 us)
Async XLA Ops:
  13.6 134.8 %all-to-all-start = ((bf16[256,16,512]{2,1,0:T(8,128)(2,1)}), bf16[256,16,512]{2,1,0:T(8,128)(2,1)}, u32[]{:S(2)}, u32[]{:S(2)}) async-start(bf16[256,16,512]{2,1,0:T(8,128)(2,1)} %bitcast.374), calls=%async_computation | async-start | bytes 8388608 | tf_op jit(solution)/shard_map/all_to_all | solution.py:544
  21.0 106.3 %all-gather.11.cloned.1.call-start = ((), (), s32[]{:S(2)}) async-start(), calls=%async_computation.20 | async-start | bytes 2621440 | tf_op jit(solution)/shard_map/all_gather | solution.py:545
  21.7 216.3 %all-gather.7.cloned.1.call-start = ((), (), s32[]{:S(2)}) async-start(), calls=%async_computation.15 | async-start | bytes 9437184 | tf_op jit(solution)/shard_map/all_gather | solution.py:558
  180.5 170.2 %all-gather.9.cloned.1.call-start = ((), (), s32[]{:S(2)}) async-start(), calls=%async_computation.16 | async-start | bytes 18874368 | tf_op jit(solution)/shard_map/all_gather | solution.py:558
  192.5 34.4 %collective-permute-start.5 = (bf16[32,16,512]{2,1,0:T(8,128)(2,1)S(1)}, bf16[32,16,512]{2,1,0:T(8,128)(2,1)S(1)}, u32[]{:S(2)}, u32[]{:S(2)}) collective-permute-start(bf16[32,16,512]{2,1,0:T(8,128)(2,1)S(1)} %gather_fusion.8), channel_id=1, source_target_pairs={{0,16},{8,24},{16,0},{24,8},{1,17},{9,25},{17,1},{25,9},{2,18},{10... | collective-permute-start | bytes 1572872 | tf_op jit(solution)/shard_map/ppermute | solution.py:450
  197.2 29.7 %collective-permute-start.6 = (bf16[32,16,512]{2,1,0:T(8,128)(2,1)S(1)}, bf16[32,16,512]{2,1,0:T(8,128)(2,1)}, u32[]{:S(2)}, u32[]{:S(2)}) collective-permute-start(bf16[32,16,512]{2,1,0:T(8,128)(2,1)S(1)} %gather_fusion.10), channel_id=1, source_target_pairs={{0,24},{8,0},{16,8},{24,16},{1,25},{9,1},{17,9},{25,17},{2,26},{10... | collective-permute-start | bytes 1572872 | tf_op jit(solution)/shard_map/ppermute | solution.py:450
  281.9 40.9 %collective-permute-start.7 = (bf16[16,16,512]{2,1,0:T(8,128)(2,1)S(1)}, bf16[16,16,512]{2,1,0:T(8,128)(2,1)S(1)}, u32[]{:S(2)}, u32[]{:S(2)}) collective-permute-start(bf16[16,16,512]{2,1,0:T(8,128)(2,1)S(1)} %gather_fusion.15), channel_id=1, source_target_pairs={{0,8},{8,16},{16,24},{24,0},{1,9},{9,17},{17,25},{25,1},{2,10},{10... | collective-permute-start | bytes 786440 | tf_op jit(solution)/shard_map/ppermute | solution.py:450
  285.5 37.3 %collective-permute-start.8 = (bf16[16,16,512]{2,1,0:T(8,128)(2,1)S(1)}, bf16[16,16,512]{2,1,0:T(8,128)(2,1)S(1)}, u32[]{:S(2)}, u32[]{:S(2)}) collective-permute-start(bf16[16,16,512]{2,1,0:T(8,128)(2,1)S(1)} %gather_fusion.17), channel_id=1, source_target_pairs={{0,16},{8,24},{16,0},{24,8},{1,17},{9,25},{17,1},{25,9},{2,18},{10... | collective-permute-start | bytes 786440 | tf_op jit(solution)/shard_map/ppermute | solution.py:450
  289.7 33.1 %collective-permute-start.9 = (bf16[16,16,512]{2,1,0:T(8,128)(2,1)S(1)}, bf16[16,16,512]{2,1,0:T(8,128)(2,1)}, u32[]{:S(2)}, u32[]{:S(2)}) collective-permute-start(bf16[16,16,512]{2,1,0:T(8,128)(2,1)S(1)} %gather_fusion.19), channel_id=1, source_target_pairs={{0,24},{8,0},{16,8},{24,16},{1,25},{9,1},{17,9},{25,17},{2,26},{10... | collective-permute-start | bytes 786440 | tf_op jit(solution)/shard_map/ppermute | solution.py:450
  319.7 105.7 %all-gather.13.cloned.1.call-start = ((), (), s32[]{:S(2)}) async-start(), calls=%async_computation.21 | async-start | bytes 9437184 | tf_op jit(solution)/shard_map/all_gather | solution.py:558
  350.7 364.1 %reduce-scatter.6.cloned.1.call-start = ((), (), s32[]{:S(2)}) async-start(), calls=%async_computation.18 | async-start | bytes 9437184 | tf_op jit(solution)/shard_map/reduce_scatter | solution.py:665
  401.2 30.6 %collective-permute-start.14 = (bf16[4,64,2048]{2,1,0:T(8,128)(2,1)}, bf16[4,64,2048]{2,1,0:T(8,128)(2,1)}, u32[]{:S(2)}, u32[]{:S(2)}) collective-permute-start(bf16[4,64,2048]{2,1,0:T(8,128)(2,1)} %shard_map.173), channel_id=1, source_target_pairs={{0,4},{2,6},{4,0},{6,2},{1,5},{3,7},{5,1},{7,3},{8,12},{10,14},{12... | collective-permute-start | bytes 3145736 | tf_op jit(solution)/shard_map/ppermute | solution.py:456
  402.0 32.8 %collective-permute-start.13 = (bf16[4,64,2048]{2,1,0:T(8,128)(2,1)}, bf16[4,64,2048]{2,1,0:T(8,128)(2,1)}, u32[]{:S(2)}, u32[]{:S(2)}) collective-permute-start(bf16[4,64,2048]{2,1,0:T(8,128)(2,1)} %shard_map.172), channel_id=1, source_target_pairs={{0,2},{2,0},{4,6},{6,4},{1,3},{3,1},{5,7},{7,5},{8,10},{10,8},{12,... | collective-permute-start | bytes 3145736 | tf_op jit(solution)/shard_map/ppermute | solution.py:456
  431.8 27.7 %collective-permute-start.10 = (bf16[128,2048]{1,0:T(8,128)(2,1)S(1)}, bf16[128,2048]{1,0:T(8,128)(2,1)S(1)}, u32[]{:S(2)}, u32[]{:S(2)}) collective-permute-start(bf16[128,2048]{1,0:T(8,128)(2,1)S(1)} %slice.521), channel_id=1, source_target_pairs={{0,8},{8,16},{16,24},{24,0},{1,9},{9,17},{17,25},{25,1},{2,10},{10... | collective-permute-start | bytes 1572872 | tf_op jit(solution)/shard_map/ppermute | solution.py:428
  476.3 45.8 %collective-permute-start.22 = (bf16[2,4,64,2048]{3,2,1,0:T(8,128)(2,1)}, bf16[2,4,64,2048]{3,2,1,0:T(8,128)(2,1)}, u32[]{:S(2)}, u32[]{:S(2)}) collective-permute-start(bf16[2,4,64,2048]{3,2,1,0:T(8,128)(2,1)} %pad_maximum_fusion.3), channel_id=1, source_target_pairs={{0,2},{2,0},{4,6},{6,4},{1,3},{3,1},{5,7},{7,5},{8,10},{10,8},{12,... | collective-permute-start | bytes 6291464 | tf_op jit(solution)/shard_map/ppermute | solution.py:456
  477.8 44.3 %collective-permute-start.21 = (bf16[2,4,64,2048]{3,2,1,0:T(8,128)(2,1)S(1)}, bf16[2,4,64,2048]{3,2,1,0:T(8,128)(2,1)}, u32[]{:S(2)}, u32[]{:S(2)}) collective-permute-start(bf16[2,4,64,2048]{3,2,1,0:T(8,128)(2,1)S(1)} %pad_maximum_fusion.2), channel_id=1, source_target_pairs={{0,4},{2,6},{4,0},{6,2},{1,5},{3,7},{5,1},{7,3},{8,12},{10,14},{12... | collective-permute-start | bytes 6291464 | tf_op jit(solution)/shard_map/ppermute | solution.py:456
  551.0 182.6 %reduce-scatter.4.cloned.1.call-start = ((), (), s32[]{:S(2)}) async-start(), calls=%async_computation.17 | async-start | bytes 9437184 | tf_op jit(solution)/shard_map/reduce_scatter | solution.py:665
  562.3 252.3 %reduce-scatter.8.cloned.1.call-start = ((), (), s32[]{:S(2)}) async-start(), calls=%async_computation.19 | async-start | bytes 11796480 | tf_op jit(solution)/shard_map/reduce_scatter | solution.py:665
  795.6 39.7 %all-to-all-start.8 = ((bf16[16,4,16,384]{3,2,1,0:T(8,128)(2,1)}), bf16[16,4,16,384]{3,2,1,0:T(8,128)(2,1)}, u32[]{:S(2)}, u32[]{:S(2)}) async-start(bf16[16,4,16,384]{3,2,1,0:T(8,128)(2,1)} %bitcast.403), calls=%async_computation.10 | async-start | bytes 1572864 | tf_op jit(solution)/shard_map/all_to_all | solution.py:725
  816.8 33.6 %collective-permute-start.38 = (bf16[20,16,512]{2,1,0:T(8,128)(2,1)}, bf16[20,16,512]{2,1,0:T(8,128)(2,1)}, u32[]{:S(2)}, u32[]{:S(2)}) collective-permute-start(bf16[20,16,512]{2,1,0:T(8,128)(2,1)} %get-tuple-element.73), channel_id=1, source_target_pairs={{0,8},{8,16},{16,24},{24,0},{1,9},{9,17},{17,25},{25,1},{2,10},{10... | collective-permute-start | bytes 983048 | tf_op jit(solution)/shard_map/ppermute | solution.py:450
  816.8 33.6 %collective-permute-start.39 = (bf16[20,16,512]{2,1,0:T(8,128)(2,1)}, bf16[20,16,512]{2,1,0:T(8,128)(2,1)}, u32[]{:S(2)}, u32[]{:S(2)}) collective-permute-start(bf16[20,16,512]{2,1,0:T(8,128)(2,1)} %get-tuple-element.72), channel_id=1, source_target_pairs={{0,16},{8,24},{16,0},{24,8},{1,17},{9,25},{17,1},{25,9},{2,18},{10... | collective-permute-start | bytes 983048 | tf_op jit(solution)/shard_map/ppermute | solution.py:450
  819.1 31.4 %collective-permute-start.40 = (bf16[20,16,512]{2,1,0:T(8,128)(2,1)S(1)}, bf16[20,16,512]{2,1,0:T(8,128)(2,1)}, u32[]{:S(2)}, u32[]{:S(2)}) collective-permute-start(bf16[20,16,512]{2,1,0:T(8,128)(2,1)S(1)} %get-tuple-element.71), channel_id=1, source_target_pairs={{0,24},{8,0},{16,8},{24,16},{1,25},{9,1},{17,9},{25,17},{2,26},{10... | collective-permute-start | bytes 983048 | tf_op jit(solution)/shard_map/ppermute | solution.py:450
  835.9 23.2 %all-to-all-start.11 = ((f32[32,1,256]{2,1,0:T(1,128)}), f32[32,1,256]{2,1,0:T(1,128)}, u32[]{:S(2)}, u32[]{:S(2)}) async-start(f32[32,1,256]{2,1,0:T(1,128)} %broadcast_in_dim.141), calls=%async_computation.14 | async-start | bytes 65536 | tf_op jit(solution)/shard_map/all_to_all | solution.py:744
  859.2 100.2 %all-to-all-start.9 = ((bf16[256,16,512]{2,1,0:T(8,128)(2,1)}), bf16[256,16,512]{2,1,0:T(8,128)(2,1)}, u32[]{:S(2)}, u32[]{:S(2)}) async-start(bf16[256,16,512]{2,1,0:T(8,128)(2,1)} %gather_fusion.31), calls=%async_computation.12 | async-start | bytes 8388608 | tf_op jit(solution)/shard_map/all_to_all | solution.py:757
  (145 other events, 1917.0 us)
Sparse Core Ops, SparseCore 0:
  23.4 103.8 all-gather.10
  180.6 53.6 all-gather.6
  236.8 113.8 all-gather.8
  353.0 57.3 all-gather.12
  551.1 68.5 reduce-scatter.5
  624.0 84.8 reduce-scatter.3
  712.4 79.9 reduce-scatter.7

commit v7 on v6

--- a/solution.py
+++ b/solution.py
@@ -283,24 +283,36 @@
     return jnp.where((key_place >= begin) & (key_place <= query_place), scores, -1e30)
 
 
-def window_start(i, block, window, length):
-    start = jnp.clip(i * block + block - window, 0, length - window)
-    return pl.multiple_of(start, 128)
+def by_window(block, window, work):
+    i, full = pl.program_id(0), window // block
+
+    for j in range(full - 1):
+
+        @pl.when(i == j)
+        def _(j=j):
+            work(0, (j + 1) * block)
+
+    @pl.when(i >= full - 1)
+    def _():
+        work(pl.multiple_of((i + 1) * block - window, 128), window)
 
 
 def attend_kernel(scale, window, q_ref, k_ref, v_ref, b_ref, o_ref, lse_ref):
-    block, length = q_ref.shape[0], k_ref.shape[0]
-    i = pl.program_id(0)
-    start = window_start(i, block, window, length)
-    scores = scores_of(
-        q_ref[...], k_ref[pl.ds(start, window), :], b_ref[...], i * block, start, scale
-    )
-    top = jnp.max(scores, axis=0, keepdims=True)
-    expo = jnp.exp(scores - top)
-    total = jnp.sum(expo, axis=0, keepdims=True)
-    attention = (expo * (1.0 / total)).astype(bf16)
-    o_ref[...] = mm_tn(attention, v_ref[pl.ds(start, window), :]).astype(bf16)
-    lse_ref[...] = top + jnp.log(total)
+    block = q_ref.shape[0]
+
+    def work(start, size):
+        span = pl.ds(start, size)
+        scores = scores_of(
+            q_ref[...], k_ref[span, :], b_ref[...], pl.program_id(0) * block, start, scale
+        )
+        top = jnp.max(scores, axis=0, keepdims=True)
+        expo = jnp.exp(scores - top)
+        total = jnp.sum(expo, axis=0, keepdims=True)
+        attention = (expo * (1.0 / total)).astype(bf16)
+        o_ref[...] = mm_tn(attention, v_ref[span, :]).astype(bf16)
+        lse_ref[...] = top + jnp.log(total)
+
+    by_window(block, window, work)
 
 
 def attend(q, k, v, begins, scale):
@@ -327,25 +339,26 @@
     scale, window, q_ref, d_ref, k_ref, v_ref, b_ref, lse_ref, *refs
 ):
     dq_ref, dk_ref, dv_ref, ka, va = refs[-5:]
-    block, length = q_ref.shape[0], k_ref.shape[0]
-    i = pl.program_id(0)
-    start = window_start(i, block, window, length)
-    span = pl.ds(start, window)
+    block, i = q_ref.shape[0], pl.program_id(0)
 
     @pl.when(i == 0)
     def _():
         ka[...] = jnp.zeros_like(ka)
         va[...] = jnp.zeros_like(va)
 
-    q, d, k = q_ref[...], d_ref[...], k_ref[span, :]
-    scores = scores_of(q, k, b_ref[...], i * block, start, scale)
-    attention = jnp.exp(scores - lse_ref[...])
-    prob_grad = mm_nt(v_ref[span, :], d)
-    center = jnp.sum(attention * prob_grad, axis=0, keepdims=True)
-    score_grad = (attention * (prob_grad - center)).astype(bf16)
-    dq_ref[...] = (mm_tn(score_grad, k) * scale).astype(bf16)
-    ka[span, :] += mm(score_grad, q) * scale
-    va[span, :] += mm(attention.astype(bf16), d)
+    def work(start, size):
+        span = pl.ds(start, size)
+        q, d, k = q_ref[...], d_ref[...], k_ref[span, :]
+        scores = scores_of(q, k, b_ref[...], i * block, start, scale)
+        attention = jnp.exp(scores - lse_ref[...])
+        prob_grad = mm_nt(v_ref[span, :], d)
+        center = jnp.sum(attention * prob_grad, axis=0, keepdims=True)
+        score_grad = (attention * (prob_grad - center)).astype(bf16)
+        dq_ref[...] = (mm_tn(score_grad, k) * scale).astype(bf16)
+        ka[span, :] += mm(score_grad, q) * scale
+        va[span, :] += mm(attention.astype(bf16), d)
+
+    by_window(block, window, work)
 
     @pl.when(i == pl.num_programs(0) - 1)
     def _():

time: 1010 us -> 1010 us (level)
  transfers between devices with their start and end apart: 59 -> 59, of which waited for: 34 -> 34; matrix products, arithmetic and copies ran while one was open for 15% -> 14% of each run, Pallas kernels for 13% -> 13%
where the time goes in v7:
time: 1010 us; the launch traced here: 1000 us
  waiting for transfers between devices  494 us (49%)
  Pallas kernels  171 us (17%)
  local copies, waits for them, and re-layouts  126 us (12%)
  starting transfers between devices  102 us (10%)
  other arithmetic  55.9 us (6%)
  blocking collectives  28.3 us (3%)
  between operations  21.9 us (2%)
    all_gather x1, waiting for transfers between devices, body(): tokens_g = lax.all_gather(inputs, 'hz', axis=0, tiled=True)  102 us
    all_to_all x1, waiting for transfers between devices, body(): got = lax.all_to_all(to_slots, EVERY, 0, 0, tiled=True)  91.8 us
    ppermute x9, waiting for transfers between devices, ring_gather(): blocks.append(lax.ppermute(blocks[-1], 'hz', UP))  73.6 us
    ppermute x8, waiting for transfers between devices, ring_scatter(): lax.ppermute(total, 'hz', UP).astype(f32) + part_of(k)  62.4 us
    ppermute x4, waiting for transfers between devices, ring_scatter(): return lax.ppermute(total, 'hz', UP).astype(f32) + part_of(0)  35.8 us
    ppermute x15, waiting for transfers between devices, exchange_z(): lax.ppermute(part_for(j), 'hz', [(i, (i + j) % Z) for i in range(Z)])  35.5 us
    pallas_call x5, Pallas kernels, nt(): pl.pallas_call(functools.partial(nt_kernel, len(xs)), grid=(steps,), in_s...  31.5 us
    pallas_call x7, Pallas kernels, nn(): pl.pallas_call(nn_kernel, grid=(steps,), in_specs=[pl.BlockSpec(x.shape,...  29.3 us
  transfers between devices with their start and end apart: 59, of which 34 were waited for; matrix products, arithmetic and copies ran while one was open for 14% of the time, Pallas kernels for 13%

profile of v7, /device:TPU:0, one launch (start us, length us, event | category | flops | bytes accessed | tf_op | source)
XLA Modules:
  0.0 999.7 jit_solution(15311541947394766366)
XLA Ops:
  25.5 101.8 %all-gather.11.cloned.1.call-done = bf16[1,512,2048]{2,1,0:T(8,128)(2,1)} async-done(((bf16[1,128,2048]{2,1,0:T(8,128)(2,1)}), bf16[1,512,2048]{2,1,0:T(8,128)(2,1)}) %all-gather.11.cloned.1.call-update) | async-done | bytes 2097168 | tf_op jit(solution)/shard_map/all_gather | solution.py:558
  129.8 18.5 %all-to-all-done = bf16[256,16,512]{2,1,0:T(8,128)(2,1)} async-done(((bf16[256,16,512]{2,1,0:T(8,128)(2,1)}), bf16[256,16,512]{2,1,0:T(8,128)(2,1)}, u32[]{:S(2)}, u32[]{:S(2)}) %all-to-all-start) | async-done | bytes 4194336 | tf_op jit(solution)/shard_map/all_to_all | solution.py:557
  151.1 28.3 %all_to_all.65 = bf16[64,16,512]{2,1,0:T(8,128)(2,1)S(1)} all-to-all(bf16[64,16,512]{2,1,0:T(8,128)(2,1)S(1)} %gather_fusion.1), channel_id=1, replica_groups=mesh['hz'=4,'hp'=4,'seq'=2] {'hz'}, dimensions={0} | all-to-all | bytes 2097152 | tf_op jit(solution)/shard_map/all_to_all | solution.py:567
  206.5 20.4 %collective-permute-done.5 = bf16[32,16,512]{2,1,0:T(8,128)(2,1)S(1)} collective-permute-done((bf16[32,16,512]{2,1,0:T(8,128)(2,1)S(1)}, bf16[32,16,512]{2,1,0:T(8,128)(2,1)S(1)}, u32[]{:S(2)}, u32[]{:S(2)}) %collective-permute-start.5) | collective-permute-done | bytes 524320 | tf_op jit(solution)/shard_map/ppermute | solution.py:463
  250.3 15.0 %all-to-all-start.3 = ((f32[16,3,512]{2,1,0:T(4,128)}), f32[16,3,512]{2,1,0:T(4,128)S(1)}, u32[]{:S(2)}, u32[]{:S(2)}) async-start(f32[16,3,512]{2,1,0:T(4,128)} %broadcast_in_dim.121), calls=%async_computation.3 | async-start | bytes 262144 | tf_op jit(solution)/shard_map/all_to_all | solution.py:496
  337.4 13.3 %all-gather.9.cloned.1.call-done = bf16[8,32,64,512]{3,2,1,0:T(8,128)(2,1)} async-done(((bf16[1,32,64,512]{3,2,1,0:T(8,128)(2,1)}), bf16[8,32,64,512]{3,2,1,0:T(8,128)(2,1)}) %all-gather.9.cloned.1.call-update) | async-done | bytes 16777232 | tf_op jit(solution)/shard_map/all_gather | solution.py:571
  356.5 11.5 %collective-permute-done = bf16[128,2048]{1,0:T(8,128)(2,1)S(1)} collective-permute-done((bf16[128,2048]{1,0:T(8,128)(2,1)S(1)}, bf16[128,2048]{1,0:T(8,128)(2,1)S(1)}, u32[]{:S(2)}, u32[]{:S(2)}) %collective-permute-start) | collective-permute-done | bytes 524320 | tf_op jit(solution)/shard_map/ppermute | solution.py:441
  371.1 12.1 %collective-permute-done.1 = bf16[128,2048]{1,0:T(8,128)(2,1)S(1)} collective-permute-done((bf16[128,2048]{1,0:T(8,128)(2,1)S(1)}, bf16[128,2048]{1,0:T(8,128)(2,1)S(1)}, u32[]{:S(2)}, u32[]{:S(2)}) %collective-permute-start.1) | collective-permute-done | bytes 524320 | tf_op jit(solution)/shard_map/ppermute | solution.py:441
  387.0 10.5 %collective-permute-done.2 = bf16[128,2048]{1,0:T(8,128)(2,1)S(1)} collective-permute-done((bf16[128,2048]{1,0:T(8,128)(2,1)S(1)}, bf16[128,2048]{1,0:T(8,128)(2,1)S(1)}, u32[]{:S(2)}, u32[]{:S(2)}) %collective-permute-start.2) | collective-permute-done | bytes 524320 | tf_op jit(solution)/shard_map/ppermute | solution.py:442
  412.3 9.8 shard_map.167
  442.4 9.7 shard_map.171
  459.7 16.2 %collective-permute-done.15 = bf16[128,2048]{1,0:T(8,128)(2,1)S(1)} collective-permute-done((bf16[128,2048]{1,0:T(8,128)(2,1)S(1)}, bf16[128,2048]{1,0:T(8,128)(2,1)S(1)}, u32[]{:S(2)}, u32[]{:S(2)}) %collective-permute-start.15) | collective-permute-done | bytes 524320 | tf_op jit(solution)/shard_map/ppermute | solution.py:441
  478.2 12.8 %collective-permute-done.16 = bf16[128,2048]{1,0:T(8,128)(2,1)S(1)} collective-permute-done((bf16[128,2048]{1,0:T(8,128)(2,1)S(1)}, bf16[128,2048]{1,0:T(8,128)(2,1)S(1)}, u32[]{:S(2)}, u32[]{:S(2)}) %collective-permute-start.16) | collective-permute-done | bytes 524320 | tf_op jit(solution)/shard_map/ppermute | solution.py:442
  493.6 14.5 %collective-permute-done.17.refs_1_ = bf16[128,2048]{1,0:T(8,128)(2,1)S(1)} collective-permute-done((bf16[128,2048]{1,0:T(8,128)(2,1)S(1)}, bf16[128,2048]{1,0:T(8,128)(2,1)S(1)}, u32[]{:S(2)}, u32[]{:S(2)}) %collective-permute-start.17) | collective-permute-done | bytes 524320 | tf_op jit(solution)/shard_map/ppermute | solution.py:430
  522.1 11.2 %collective-permute-done.20.refs_1_ = bf16[128,2048]{1,0:T(8,128)(2,1)S(1)} collective-permute-done((bf16[128,2048]{1,0:T(8,128)(2,1)}, bf16[128,2048]{1,0:T(8,128)(2,1)S(1)}, u32[]{:S(2)}, u32[]{:S(2)}) %collective-permute-start.20) | collective-permute-done | bytes 524320 | tf_op jit(solution)/shard_map/ppermute | solution.py:430
  584.0 12.4 %collective-permute-done.23 = bf16[128,2048]{1,0:T(8,128)(2,1)S(1)} collective-permute-done((bf16[128,2048]{1,0:T(8,128)(2,1)S(1)}, bf16[128,2048]{1,0:T(8,128)(2,1)S(1)}, u32[]{:S(2)}, u32[]{:S(2)}) %collective-permute-start.23) | collective-permute-done | bytes 524320 | tf_op jit(solution)/shard_map/ppermute | solution.py:441
  596.6 12.4 %collective-permute-done.24 = bf16[128,2048]{1,0:T(8,128)(2,1)S(1)} collective-permute-done((bf16[128,2048]{1,0:T(8,128)(2,1)S(1)}, bf16[128,2048]{1,0:T(8,128)(2,1)S(1)}, u32[]{:S(2)}, u32[]{:S(2)}) %collective-permute-start.24) | collective-permute-done | bytes 524320 | tf_op jit(solution)/shard_map/ppermute | solution.py:442
  610.1 12.6 %collective-permute-done.25 = bf16[128,2048]{1,0:T(8,128)(2,1)S(1)} collective-permute-done((bf16[128,2048]{1,0:T(8,128)(2,1)S(1)}, bf16[128,2048]{1,0:T(8,128)(2,1)S(1)}, u32[]{:S(2)}, u32[]{:S(2)}) %collective-permute-start.25) | collective-permute-done | bytes 524320 | tf_op jit(solution)/shard_map/ppermute | solution.py:430
  622.6 11.0 %collective-permute-done.26 = bf16[128,2048]{1,0:T(8,128)(2,1)S(1)} collective-permute-done((bf16[128,2048]{1,0:T(8,128)(2,1)S(1)}, bf16[128,2048]{1,0:T(8,128)(2,1)S(1)}, u32[]{:S(2)}, u32[]{:S(2)}) %collective-permute-start.26) | collective-permute-done | bytes 524320 | tf_op jit(solution)/shard_map/ppermute | solution.py:430
  655.7 12.0 %all-to-all-done.5 = bf16[4,1,4,128,128]{4,3,2,1,0:T(8,128)(2,1)S(1)} async-done(((bf16[4,1,4,128,128]{4,3,2,1,0:T(8,128)(2,1)}), bf16[4,1,4,128,128]{4,3,2,1,0:T(8,128)(2,1)S(1)}, u32[]{:S(2)}, u32[]{:S(2)}) %all-to-all-start.5) | async-done | bytes 524320 | tf_op jit(solution)/shard_map/all_to_all | solution.py:598
  689.3 11.2 %all-to-all-done.6 = f32[16,2,2048]{2,1,0:T(2,128)S(1)} async-done(((f32[16,2,2048]{2,1,0:T(2,128)}), f32[16,2,2048]{2,1,0:T(2,128)S(1)}, u32[]{:S(2)}, u32[]{:S(2)}) %all-to-all-start.6) | async-done | bytes 262176 | tf_op jit(solution)/shard_map/all_to_all | solution.py:496
  823.1 18.2 %all-to-all-done.8 = bf16[16,4,16,384]{3,2,1,0:T(8,128)(2,1)} async-done(((bf16[16,4,16,384]{3,2,1,0:T(8,128)(2,1)}), bf16[16,4,16,384]{3,2,1,0:T(8,128)(2,1)}, u32[]{:S(2)}, u32[]{:S(2)}) %all-to-all-start.8) | async-done | bytes 786464 | tf_op jit(solution)/shard_map/all_to_all | solution.py:738
  871.7 91.8 %all-to-all-done.9 = bf16[256,16,512]{2,1,0:T(8,128)(2,1)} async-done(((bf16[256,16,512]{2,1,0:T(8,128)(2,1)}), bf16[256,16,512]{2,1,0:T(8,128)(2,1)}, u32[]{:S(2)}, u32[]{:S(2)}) %all-to-all-start.9) | async-done | bytes 4194336 | tf_op jit(solution)/shard_map/all_to_all | solution.py:770
  966.4 26.2 %shard_map.191 = (f32[8,512,512]{2,1,0:T(8,128)}, f32[8,512,512]{2,1,0:T(8,128)}, f32[8,512,512]{2,1,0:T(8,128)}, f32[8,512,512]{2,1,0:T(8,128)}) custom-call(bf16[8,512,512]{2,1,0:T(8,128)(2,1)S(1)} %bitcast.316, f32[8,512,512]{2,1,0:T(8,128)} %ls_ref.1, f32[8,512,512]{2,1,0:T(8,128)} %rs_ref.1, f32[8,512,512]{2,1,0:T(8,128)} %lr_ref.1, ...), custom_call_target="tpu_custom_call" | custom-call | flops 858993472 | bytes 7969177 | tf_op jit(solution)/shard_map/pallas_call | solution.py:400
  (590 shorter events, 464.1 us)
Async XLA Ops:
  13.6 134.8 %all-to-all-start = ((bf16[256,16,512]{2,1,0:T(8,128)(2,1)}), bf16[256,16,512]{2,1,0:T(8,128)(2,1)}, u32[]{:S(2)}, u32[]{:S(2)}) async-start(bf16[256,16,512]{2,1,0:T(8,128)(2,1)} %bitcast.374), calls=%async_computation | async-start | bytes 8388608 | tf_op jit(solution)/shard_map/all_to_all | solution.py:557
  21.0 106.3 %all-gather.11.cloned.1.call-start = ((), (), s32[]{:S(2)}) async-start(), calls=%async_computation.20 | async-start | bytes 2621440 | tf_op jit(solution)/shard_map/all_gather | solution.py:558
  21.7 216.3 %all-gather.7.cloned.1.call-start = ((), (), s32[]{:S(2)}) async-start(), calls=%async_computation.15 | async-start | bytes 9437184 | tf_op jit(solution)/shard_map/all_gather | solution.py:571
  180.5 170.2 %all-gather.9.cloned.1.call-start = ((), (), s32[]{:S(2)}) async-start(), calls=%async_computation.16 | async-start | bytes 18874368 | tf_op jit(solution)/shard_map/all_gather | solution.py:571
  192.5 34.4 %collective-permute-start.5 = (bf16[32,16,512]{2,1,0:T(8,128)(2,1)S(1)}, bf16[32,16,512]{2,1,0:T(8,128)(2,1)S(1)}, u32[]{:S(2)}, u32[]{:S(2)}) collective-permute-start(bf16[32,16,512]{2,1,0:T(8,128)(2,1)S(1)} %gather_fusion.8), channel_id=1, source_target_pairs={{0,16},{8,24},{16,0},{24,8},{1,17},{9,25},{17,1},{25,9},{2,18},{10... | collective-permute-start | bytes 1572872 | tf_op jit(solution)/shard_map/ppermute | solution.py:463
  197.2 29.7 %collective-permute-start.6 = (bf16[32,16,512]{2,1,0:T(8,128)(2,1)S(1)}, bf16[32,16,512]{2,1,0:T(8,128)(2,1)}, u32[]{:S(2)}, u32[]{:S(2)}) collective-permute-start(bf16[32,16,512]{2,1,0:T(8,128)(2,1)S(1)} %gather_fusion.10), channel_id=1, source_target_pairs={{0,24},{8,0},{16,8},{24,16},{1,25},{9,1},{17,9},{25,17},{2,26},{10... | collective-permute-start | bytes 1572872 | tf_op jit(solution)/shard_map/ppermute | solution.py:463
  281.9 38.9 %collective-permute-start.7 = (bf16[16,16,512]{2,1,0:T(8,128)(2,1)S(1)}, bf16[16,16,512]{2,1,0:T(8,128)(2,1)S(1)}, u32[]{:S(2)}, u32[]{:S(2)}) collective-permute-start(bf16[16,16,512]{2,1,0:T(8,128)(2,1)S(1)} %gather_fusion.15), channel_id=1, source_target_pairs={{0,8},{8,16},{16,24},{24,0},{1,9},{9,17},{17,25},{25,1},{2,10},{10... | collective-permute-start | bytes 786440 | tf_op jit(solution)/shard_map/ppermute | solution.py:463
  285.5 35.4 %collective-permute-start.8 = (bf16[16,16,512]{2,1,0:T(8,128)(2,1)S(1)}, bf16[16,16,512]{2,1,0:T(8,128)(2,1)S(1)}, u32[]{:S(2)}, u32[]{:S(2)}) collective-permute-start(bf16[16,16,512]{2,1,0:T(8,128)(2,1)S(1)} %gather_fusion.17), channel_id=1, source_target_pairs={{0,16},{8,24},{16,0},{24,8},{1,17},{9,25},{17,1},{25,9},{2,18},{10... | collective-permute-start | bytes 786440 | tf_op jit(solution)/shard_map/ppermute | solution.py:463
  289.7 31.1 %collective-permute-start.9 = (bf16[16,16,512]{2,1,0:T(8,128)(2,1)S(1)}, bf16[16,16,512]{2,1,0:T(8,128)(2,1)}, u32[]{:S(2)}, u32[]{:S(2)}) collective-permute-start(bf16[16,16,512]{2,1,0:T(8,128)(2,1)S(1)} %gather_fusion.19), channel_id=1, source_target_pairs={{0,24},{8,0},{16,8},{24,16},{1,25},{9,1},{17,9},{25,17},{2,26},{10... | collective-permute-start | bytes 786440 | tf_op jit(solution)/shard_map/ppermute | solution.py:463
  318.0 107.4 %all-gather.13.cloned.1.call-start = ((), (), s32[]{:S(2)}) async-start(), calls=%async_computation.21 | async-start | bytes 9437184 | tf_op jit(solution)/shard_map/all_gather | solution.py:571
  350.7 363.5 %reduce-scatter.6.cloned.1.call-start = ((), (), s32[]{:S(2)}) async-start(), calls=%async_computation.18 | async-start | bytes 9437184 | tf_op jit(solution)/shard_map/reduce_scatter | solution.py:678
  401.2 30.8 %collective-permute-start.14 = (bf16[4,64,2048]{2,1,0:T(8,128)(2,1)}, bf16[4,64,2048]{2,1,0:T(8,128)(2,1)}, u32[]{:S(2)}, u32[]{:S(2)}) collective-permute-start(bf16[4,64,2048]{2,1,0:T(8,128)(2,1)} %shard_map.173), channel_id=1, source_target_pairs={{0,4},{2,6},{4,0},{6,2},{1,5},{3,7},{5,1},{7,3},{8,12},{10,14},{12... | collective-permute-start | bytes 3145736 | tf_op jit(solution)/shard_map/ppermute | solution.py:469
  402.0 32.9 %collective-permute-start.13 = (bf16[4,64,2048]{2,1,0:T(8,128)(2,1)}, bf16[4,64,2048]{2,1,0:T(8,128)(2,1)}, u32[]{:S(2)}, u32[]{:S(2)}) collective-permute-start(bf16[4,64,2048]{2,1,0:T(8,128)(2,1)} %shard_map.172), channel_id=1, source_target_pairs={{0,2},{2,0},{4,6},{6,4},{1,3},{3,1},{5,7},{7,5},{8,10},{10,8},{12,... | collective-permute-start | bytes 3145736 | tf_op jit(solution)/shard_map/ppermute | solution.py:469
  431.8 27.7 %collective-permute-start.10 = (bf16[128,2048]{1,0:T(8,128)(2,1)S(1)}, bf16[128,2048]{1,0:T(8,128)(2,1)S(1)}, u32[]{:S(2)}, u32[]{:S(2)}) collective-permute-start(bf16[128,2048]{1,0:T(8,128)(2,1)S(1)} %slice.521), channel_id=1, source_target_pairs={{0,8},{8,16},{16,24},{24,0},{1,9},{9,17},{17,25},{25,1},{2,10},{10... | collective-permute-start | bytes 1572872 | tf_op jit(solution)/shard_map/ppermute | solution.py:441
  476.1 46.0 %collective-permute-start.22 = (bf16[2,4,64,2048]{3,2,1,0:T(8,128)(2,1)}, bf16[2,4,64,2048]{3,2,1,0:T(8,128)(2,1)}, u32[]{:S(2)}, u32[]{:S(2)}) collective-permute-start(bf16[2,4,64,2048]{3,2,1,0:T(8,128)(2,1)} %pad_maximum_fusion.3), channel_id=1, source_target_pairs={{0,2},{2,0},{4,6},{6,4},{1,3},{3,1},{5,7},{7,5},{8,10},{10,8},{12,... | collective-permute-start | bytes 6291464 | tf_op jit(solution)/shard_map/ppermute | solution.py:469
  477.7 44.4 %collective-permute-start.21 = (bf16[2,4,64,2048]{3,2,1,0:T(8,128)(2,1)S(1)}, bf16[2,4,64,2048]{3,2,1,0:T(8,128)(2,1)}, u32[]{:S(2)}, u32[]{:S(2)}) collective-permute-start(bf16[2,4,64,2048]{3,2,1,0:T(8,128)(2,1)S(1)} %pad_maximum_fusion.2), channel_id=1, source_target_pairs={{0,4},{2,6},{4,0},{6,2},{1,5},{3,7},{5,1},{7,3},{8,12},{10,14},{12... | collective-permute-start | bytes 6291464 | tf_op jit(solution)/shard_map/ppermute | solution.py:469
  551.0 182.1 %reduce-scatter.4.cloned.1.call-start = ((), (), s32[]{:S(2)}) async-start(), calls=%async_computation.17 | async-start | bytes 9437184 | tf_op jit(solution)/shard_map/reduce_scatter | solution.py:678
  562.3 252.9 %reduce-scatter.8.cloned.1.call-start = ((), (), s32[]{:S(2)}) async-start(), calls=%async_computation.19 | async-start | bytes 11796480 | tf_op jit(solution)/shard_map/reduce_scatter | solution.py:678
  734.9 23.4 %collective-permute-start.29 = (bf16[16,16,512]{2,1,0:T(8,128)(2,1)S(1)}, bf16[16,16,512]{2,1,0:T(8,128)(2,1)S(1)}, u32[]{:S(2)}, u32[]{:S(2)}) collective-permute-start(bf16[16,16,512]{2,1,0:T(8,128)(2,1)S(1)} %get-tuple-element.87), channel_id=1, source_target_pairs={{0,16},{8,24},{16,0},{24,8},{1,17},{9,25},{17,1},{25,9},{2,18},{10... | collective-permute-start | bytes 786440 | tf_op jit(solution)/shard_map/ppermute | solution.py:463
  798.1 43.2 %all-to-all-start.8 = ((bf16[16,4,16,384]{3,2,1,0:T(8,128)(2,1)}), bf16[16,4,16,384]{3,2,1,0:T(8,128)(2,1)}, u32[]{:S(2)}, u32[]{:S(2)}) async-start(bf16[16,4,16,384]{3,2,1,0:T(8,128)(2,1)} %bitcast.403), calls=%async_computation.10 | async-start | bytes 1572864 | tf_op jit(solution)/shard_map/all_to_all | solution.py:738
  817.4 35.9 %collective-permute-start.38 = (bf16[20,16,512]{2,1,0:T(8,128)(2,1)}, bf16[20,16,512]{2,1,0:T(8,128)(2,1)}, u32[]{:S(2)}, u32[]{:S(2)}) collective-permute-start(bf16[20,16,512]{2,1,0:T(8,128)(2,1)} %get-tuple-element.73), channel_id=1, source_target_pairs={{0,8},{8,16},{16,24},{24,0},{1,9},{9,17},{17,25},{25,1},{2,10},{10... | collective-permute-start | bytes 983048 | tf_op jit(solution)/shard_map/ppermute | solution.py:463
  819.3 34.1 %collective-permute-start.39 = (bf16[20,16,512]{2,1,0:T(8,128)(2,1)}, bf16[20,16,512]{2,1,0:T(8,128)(2,1)}, u32[]{:S(2)}, u32[]{:S(2)}) collective-permute-start(bf16[20,16,512]{2,1,0:T(8,128)(2,1)} %get-tuple-element.72), channel_id=1, source_target_pairs={{0,16},{8,24},{16,0},{24,8},{1,17},{9,25},{17,1},{25,9},{2,18},{10... | collective-permute-start | bytes 983048 | tf_op jit(solution)/shard_map/ppermute | solution.py:463
  821.6 31.7 %collective-permute-start.40 = (bf16[20,16,512]{2,1,0:T(8,128)(2,1)S(1)}, bf16[20,16,512]{2,1,0:T(8,128)(2,1)}, u32[]{:S(2)}, u32[]{:S(2)}) collective-permute-start(bf16[20,16,512]{2,1,0:T(8,128)(2,1)S(1)} %get-tuple-element.71), channel_id=1, source_target_pairs={{0,24},{8,0},{16,8},{24,16},{1,25},{9,1},{17,9},{25,17},{2,26},{10... | collective-permute-start | bytes 983048 | tf_op jit(solution)/shard_map/ppermute | solution.py:463
  862.0 101.5 %all-to-all-start.9 = ((bf16[256,16,512]{2,1,0:T(8,128)(2,1)}), bf16[256,16,512]{2,1,0:T(8,128)(2,1)}, u32[]{:S(2)}, u32[]{:S(2)}) async-start(bf16[256,16,512]{2,1,0:T(8,128)(2,1)} %gather_fusion.31), calls=%async_computation.12 | async-start | bytes 8388608 | tf_op jit(solution)/shard_map/all_to_all | solution.py:770
  (145 other events, 1918.2 us)
Sparse Core Ops, SparseCore 0:
  23.4 103.8 all-gather.10
  180.6 53.6 all-gather.6
  236.8 113.8 all-gather.8
  353.0 57.3 all-gather.12
  551.1 68.4 reduce-scatter.5
  623.9 83.4 reduce-scatter.3
  710.9 80.0 reduce-scatter.7
